TPU v7x, 32 devices: a whole 2x2x4 slice. The times are simulated.
32 devices in a mesh: img: 4 (over y, core), tile: 8 (over z, x).
Axes of the slice: x: 2, y: 2, z: 4, core: 2. Of those that a mesh axis runs over, the one named last changes fastest.
Arguments:
- coarse: bfloat16 [4, 64, 8, 128], P('img', None, 'tile'), may hold values from -6 to 6
- w_first: bfloat16 [3, 3, 64, 32], replicated, may hold values from -0.25 to 0.25
- b_first: float32 [32], replicated, may hold values from -3 to 3
- w_second: bfloat16 [3, 3, 32, 32], replicated, may hold values from -0.375 to 0.375
- w_skip: bfloat16 [64, 32], replicated, may hold values from -0.75 to 0.75
- fade_alpha: float32 [1], replicated, may hold values from 0.3 to 0.7
- cotangent: bfloat16 [4, 32, 256, 16], P('img', None, 'tile'), may hold values from -6 to 6
Outputs:
- blended: bfloat16 [4, 32, 256, 16], P('img', None, 'tile')
- grad_first: float32 [3, 3, 64, 32], replicated
- grad_bias: float32 [32], replicated
- grad_second: float32 [3, 3, 32, 32], replicated
- grad_skip: float32 [64, 32], replicated
All inputs are finite; a program needn't handle non-finite values.
Results may differ from a plain program's by a relative error of at most 0.0065.
Values may be sent and summed in bfloat16 or wider, within the bound.
No kernel may reach another device: no remote copies, remote signals or barrier semaphores. Data moves between devices by JAX's collectives and lax.ppermute only.
A program may use at most 64 MiB of HBM per device.

v0:
```python
import jax
import jax.numpy as jnp
from jax import lax
from jax.sharding import PartitionSpec as P


def with_halo(cells, sides, width):
    for axis, dim in sides:
        count = lax.axis_size(axis)
        ends = count - 1
        head = lax.slice_in_dim(cells, 0, width, axis=dim)
        tail = lax.slice_in_dim(cells, cells.shape[dim] - width, cells.shape[dim], axis=dim)
        cells = jnp.concatenate(
            [
                lax.ppermute(tail, axis, [(i, (i + 1) % count) for i in range(ends)]),
                cells,
                lax.ppermute(head, axis, [((i + 1) % count, i) for i in range(ends)]),
            ],
            axis=dim,
        )
    return cells


def upsample_axis(values, low_rim, high_rim, along):
    length = values.shape[along]
    left_side = jnp.concatenate(
        [low_rim, lax.slice_in_dim(values, 0, length - 1, axis=along)], along
    )
    right_side = jnp.concatenate([lax.slice_in_dim(values, 1, length, axis=along), high_rim], along)
    even_part = 0.25 * left_side + 0.75 * values
    odd_part = 0.75 * values + 0.25 * right_side
    stacked = jnp.stack([even_part, odd_part], along + 1)
    new_shape = list(values.shape)
    new_shape[along] = 2 * length
    return stacked.reshape(new_shape)


def conv_shift(padded, kernel, out_width, height):
    summed = None
    for shift_w in range(3):
        for shift_h in range(3):
            window_part = padded[:, :, shift_w : shift_w + out_width, shift_h : shift_h + height]
            term = jnp.einsum(
                "bcwh,co->bowh",
                window_part,
                kernel[shift_w, shift_h],
                preferred_element_type=jnp.float32,
            )
            summed = term if summed is None else summed + term
    return summed


def conv_adjoint(padded, kernel, out_width, height):
    summed = None
    for shift_w in range(3):
        for shift_h in range(3):
            window_part = padded[
                :, :, 2 - shift_w : 2 - shift_w + out_width, 2 - shift_h : 2 - shift_h + height
            ]
            term = jnp.einsum(
                "bowh,co->bcwh",
                window_part,
                kernel[shift_w, shift_h],
                preferred_element_type=jnp.float32,
            )
            summed = term if summed is None else summed + term
    return summed


def weight_terms(padded, delta, out_width, height):
    outer_list = []
    for shift_w in range(3):
        inner_list = []
        for shift_h in range(3):
            window_part = padded[:, :, shift_w : shift_w + out_width, shift_h : shift_h + height]
            inner_list.append(
                jnp.einsum("bcwh,bowh->co", window_part, delta, preferred_element_type=jnp.float32)
            )
        outer_list.append(jnp.stack(inner_list))
    return jnp.stack(outer_list)


def pad_rows(values):
    return jnp.pad(values, ((0, 0), (0, 0), (0, 0), (1, 1)))


def local(coarse, w_first, b_first, w_second, w_skip, fade_alpha, cotangent):
    position = lax.axis_index("tile")
    tile_count = lax.axis_size("tile")
    bias_plane = b_first[None, :, None, None]
    bordered = with_halo(coarse, (("tile", 2),), 1)
    own_rows = coarse.astype(jnp.float32)
    low_rim = jnp.where(position == 0, own_rows, bordered[:, :, :1].astype(jnp.float32))
    high_rim = jnp.where(
        position == tile_count - 1, own_rows, bordered[:, :, -1:].astype(jnp.float32)
    )
    row_pass = upsample_axis(own_rows, low_rim, high_rim, 2)
    col_pass = upsample_axis(row_pass, row_pass[:, :, :, :1], row_pass[:, :, :, -1:], 3)
    fine_rows = col_pass.astype(jnp.bfloat16)
    handed = lax.all_to_all(fine_rows, "tile", split_axis=3, concat_axis=2, tiled=True)
    upsampled = jnp.transpose(handed, (0, 1, 3, 2))
    local_width = upsampled.shape[2]
    height = upsampled.shape[3]
    up_pad = pad_rows(with_halo(upsampled, (("tile", 2),), 1))
    pre_first = conv_shift(up_pad, w_first, local_width, height) + bias_plane
    hidden = jax.nn.silu(pre_first).astype(jnp.bfloat16)
    hidden_pad = pad_rows(with_halo(hidden, (("tile", 2),), 1))
    images_here = upsampled.shape[0]
    blend = fade_alpha[0]
    second_out = conv_shift(hidden_pad, w_second, local_width, height)
    skip_out = jnp.einsum("bcwh,co->bowh", upsampled, w_skip, preferred_element_type=jnp.float32)
    blended = (blend * second_out + (1.0 - blend) * skip_out).astype(jnp.bfloat16)
    total_count = images_here * lax.axis_size("img") * local_width * tile_count * height
    loss_scale = float(total_count) ** (-0.5)
    grad_float = cotangent.astype(jnp.float32)
    d_second = (grad_float * (blend * loss_scale)).astype(jnp.bfloat16)
    d_skip = (grad_float * ((1.0 - blend) * loss_scale)).astype(jnp.bfloat16)
    second_pad = pad_rows(with_halo(d_second, (("tile", 2),), 1))
    d_hidden = conv_adjoint(second_pad, w_second, local_width, height)
    sigma = jax.nn.sigmoid(pre_first)
    d_pre = (d_hidden * (sigma * (1.0 + pre_first * (1.0 - sigma)))).astype(jnp.bfloat16)
    grad_first = weight_terms(up_pad, d_pre, local_width, height)
    grad_bias = jnp.sum(d_pre.astype(jnp.float32), axis=(0, 2, 3))
    grad_second = weight_terms(hidden_pad, d_second, local_width, height)
    grad_skip = jnp.einsum("bcwh,bowh->co", upsampled, d_skip, preferred_element_type=jnp.float32)
    grad_first, grad_bias, grad_second, grad_skip = lax.psum(
        (grad_first, grad_bias, grad_second, grad_skip), ("img", "tile")
    )
    return (blended, grad_first, grad_bias, grad_second, grad_skip)


def solution(mesh):
    placed = (P("img", None, "tile", None), P(), P(), P(), P(), P(), P("img", None, "tile", None))
    return jax.shard_map(
        local,
        mesh=mesh,
        in_specs=placed,
        out_specs=(P("img", None, "tile", None), P(), P(), P(), P()),
        check_vma=False,
    )
```

profile of v0, /device:TPU:0, one launch (start us, length us, event | category | flops | bytes accessed | tf_op | source)
XLA Modules:
  0.0 188.7 jit_solution(14178582256204035798)
XLA Ops:
  7.8 1.1 copy.93
  9.0 4.8 %collective-permute-start.6 = (bf16[1,32,1,16]{1,2,3,0:T(2,128)(2,1)S(1)}, bf16[1,32,1,16]{1,2,3,0:T(2,128)(2,1)S(1)}, u32[]{:S(2)}, u32[]{:S(2)}) collective-permute-start(bf16[1,32,1,16]{1,2,3,0:T(2,128)(2,1)S(1)} %get-tuple-element.23), channel_id=1, source_target_pairs={{0,1},{1,2},{2,3},{3,4},{4,5},{5,6},{6,7},{8,9},{9,10},{10,11},{11... | collective-permute-start | bytes 3080 | tf_op jit(solution)/shard_map/ppermute | solution.py:15
  13.8 1.3 collective-permute-start.7
  15.2 1.3 collective-permute-start.1
  16.5 5.2 %collective-permute-start = (bf16[1,64,1,128]{3,1,2,0:T(8,128)(2,1)S(1)}, bf16[1,64,1,128]{3,1,2,0:T(8,128)(2,1)S(1)}, u32[]{:S(2)}, u32[]{:S(2)}) collective-permute-start(bf16[1,64,1,128]{3,1,2,0:T(8,128)(2,1)S(1)} %copy-done.3), channel_id=1, source_target_pairs={{0,1},{1,2},{2,3},{3,4},{4,5},{5,6},{6,7},{8,9},{9,10},{10,11},{11... | collective-permute-start | bytes 49160 | tf_op jit(solution)/shard_map/ppermute | solution.py:15
  21.8 0.8 copy-done.1
  22.5 0.3 fusion.41
  22.8 0.3 convolution_add_fusion.6
  23.2 0.3 convolution_add_fusion.5
  23.5 0.3 convolution_add_fusion.4
  23.8 0.3 convolution_add_fusion.3
  24.1 0.3 convolution_add_fusion.2
  24.4 0.3 convolution_add_fusion.1
  25.4 0.8 reshape.430
  26.2 6.3 %all-to-all-start = ((bf16[8,2,2048]{2,1,0:T(2,128)(2,1)}), bf16[8,2,2048]{2,1,0:T(2,128)(2,1)S(1)}, u32[]{:S(2)}, u32[]{:S(2)}) async-start(bf16[8,2,2048]{2,1,0:T(2,128)(2,1)} %reshape.430), calls=%async_computation | async-start | bytes 131072 | tf_op jit(solution)/shard_map/all_to_all | solution.py:100
  32.5 0.3 fusion.34
  32.8 6.6 %all-to-all-done = bf16[8,2,2048]{2,1,0:T(2,128)(2,1)S(1)} async-done(((bf16[8,2,2048]{2,1,0:T(2,128)(2,1)}), bf16[8,2,2048]{2,1,0:T(2,128)(2,1)S(1)}, u32[]{:S(2)}, u32[]{:S(2)}) %all-to-all-start) | async-done | bytes 65568 | tf_op jit(solution)/shard_map/all_to_all | solution.py:100
  39.6 2.3 %collective-permute-start.2 = (bf16[1,64,1,16]{1,2,3,0:T(2,128)(2,1)S(1)}, bf16[1,64,1,16]{1,2,3,0:T(2,128)(2,1)S(1)}, u32[]{:S(2)}, u32[]{:S(2)}) collective-permute-start(bf16[1,64,1,16]{1,2,3,0:T(2,128)(2,1)S(1)} %get-tuple-element.27), channel_id=1, source_target_pairs={{0,1},{1,2},{2,3},{3,4},{4,5},{5,6},{6,7},{8,9},{9,10},{10,11},{11... | collective-permute-start | bytes 6152 | tf_op jit(solution)/shard_map/ppermute | solution.py:15
  41.9 1.3 collective-permute-start.3
  43.4 4.0 %collective-permute-done.3 = bf16[1,64,1,16]{1,2,3,0:T(2,128)(2,1)S(1)} collective-permute-done((bf16[1,64,1,16]{1,2,3,0:T(2,128)(2,1)S(1)}, bf16[1,64,1,16]{1,2,3,0:T(2,128)(2,1)S(1)}, u32[]{:S(2)}, u32[]{:S(2)}) %collective-permute-start.3) | collective-permute-done | bytes 2080 | tf_op jit(solution)/shard_map/ppermute | solution.py:17
  47.6 0.3 fusion.57
  47.8 0.3 fusion.58
  48.2 0.3 convolution_add_fusion.20
  48.5 0.3 convolution_add_fusion.19
  48.8 0.3 convolution_add_fusion.18
  49.1 0.3 convolution_add_fusion.17
  49.5 0.3 convolution_add_fusion.16
  49.8 0.3 convolution_add_fusion.15
  50.1 0.4 copy-done.4
  50.4 0.3 multiply_convert_fusion
  50.8 0.4 convert_reduce_fusion
  51.4 0.2 convolution_bitcast_fusion.6
  51.6 0.2 convolution_bitcast_fusion.5
  51.9 0.2 convolution_bitcast_fusion.4
  52.1 0.2 convolution_bitcast_fusion.3
  52.3 0.2 convolution_bitcast_fusion.2
  52.5 0.2 convolution_bitcast_fusion
  52.8 0.2 convolution_bitcast_fusion.14
  53.1 4.1 %collective-permute-start.4 = (bf16[1,32,1,16]{2,1,3,0:T(8,128)(2,1)S(1)}, bf16[1,32,1,16]{2,1,3,0:T(8,128)(2,1)S(1)}, u32[]{:S(2)}, u32[]{:S(2)}) collective-permute-start(bf16[1,32,1,16]{2,1,3,0:T(8,128)(2,1)S(1)} %get-tuple-element.25), channel_id=1, source_target_pairs={{0,1},{1,2},{2,3},{3,4},{4,5},{5,6},{6,7},{8,9},{9,10},{10,11},{11... | collective-permute-start | bytes 3080 | tf_op jit(solution)/shard_map/ppermute | solution.py:15
  57.2 1.3 collective-permute-start.5
  58.6 0.2 convolution_bitcast_fusion.7
  59.0 0.7 pad_maximum_fusion
  59.7 4.4 %collective-permute-done.5 = bf16[1,32,1,16]{2,1,3,0:T(8,128)(2,1)S(1)} collective-permute-done((bf16[1,32,1,16]{2,1,3,0:T(8,128)(2,1)S(1)}, bf16[1,32,1,16]{2,1,3,0:T(8,128)(2,1)S(1)}, u32[]{:S(2)}, u32[]{:S(2)}) %collective-permute-start.5) | collective-permute-done | bytes 1056 | tf_op jit(solution)/shard_map/ppermute | solution.py:17
  64.3 0.3 convolution_bitcast_fusion.10
  64.5 0.3 convolution_bitcast_fusion.12
  64.8 0.3 convolution_bitcast_fusion.13
  65.1 0.3 convolution_bitcast_fusion.15
  65.4 0.2 convolution_bitcast_fusion.16
  65.6 0.2 convolution_bitcast_fusion.18
  65.8 0.2 fusion.59
  66.1 0.3 fusion.60
  66.4 0.3 convolution_add_fusion.13
  66.7 0.2 convolution_add_fusion.12
  66.9 0.3 convolution_add_fusion.11
  67.2 0.2 convolution_add_fusion.10
  67.4 0.3 convolution_add_fusion.9
  67.7 0.3 convolution_add_fusion.8
  68.0 0.3 fusion.5
  68.5 0.3 convolution_bitcast_fusion.11
  68.8 0.3 convolution_bitcast_fusion.17
  69.1 42.4 %all-reduce.3 = (f32[32]{0:T(128)}, f32[3,3,32,32]{3,2,1,0:T(8,128)}, f32[64,32]{0,1:T(8,128)}) all-reduce(f32[32]{0:T(128)S(1)} %get-tuple-element.39, f32[3,3,32,32]{3,2,1,0:T(8,128)S(1)} %pad_maximum_fusion.1, f32[64,32]{0,1:T(8,128)S(1)} %convolution_bitcast_fusion.9), channel_id=1, replica_groups=mesh['img'=4,'tile'=8] {'img','tile'}, use_global_device_ids=true, to_apply=%region_2.3 | all-reduce | flops 11296 | bytes 90368 | tf_op jit(solution)/shard_map/psum | solution.py:126
  111.6 0.8 copy.113
  112.4 67.9 %all-reduce.6.cloned.1.call-done = f32[3,3,64,32]{2,3,1,0:T(8,128)} async-done(((f32[3,3,64,32]{2,3,1,0:T(8,128)}), f32[3,3,64,32]{2,3,1,0:T(8,128)}) %all-reduce.6.cloned.1.call-update) | async-done | bytes 73744 | tf_op jit(solution)/shard_map/psum | solution.py:126
  180.3 1.6 copy.146
  (43 shorter events, 2.3 us)
Async XLA Ops:
  7.2 61.1 %copy-start = (bf16[64,32]{0,1:T(8,128)(2,1)S(1)}, bf16[64,32]{0,1:T(8,128)(2,1)}, u32[]{:S(2)}) copy-start(bf16[64,32]{0,1:T(8,128)(2,1)} %param.11) | copy-start | bytes 12292
  9.0 6.2 %copy-start.3 = (bf16[1,64,1,128]{3,1,2,0:T(8,128)(2,1)S(1)}, bf16[1,64,1,128]{3,1,2,0:T(8,128)(2,1)}, u32[]{:S(2)}) copy-start(bf16[1,64,1,128]{3,1,2,0:T(8,128)(2,1)} %param.7) | copy-start | bytes 49156
  9.0 12.7 %collective-permute-start.6 = (bf16[1,32,1,16]{1,2,3,0:T(2,128)(2,1)S(1)}, bf16[1,32,1,16]{1,2,3,0:T(2,128)(2,1)S(1)}, u32[]{:S(2)}, u32[]{:S(2)}) collective-permute-start(bf16[1,32,1,16]{1,2,3,0:T(2,128)(2,1)S(1)} %get-tuple-element.23), channel_id=1, source_target_pairs={{0,1},{1,2},{2,3},{3,4},{4,5},{5,6},{6,7},{8,9},{9,10},{10,11},{11... | collective-permute-start | bytes 3080 | tf_op jit(solution)/shard_map/ppermute | solution.py:15
  13.8 7.8 %collective-permute-start.7 = (bf16[1,32,1,16]{1,2,3,0:T(2,128)(2,1)S(1)}, bf16[1,32,1,16]{1,2,3,0:T(2,128)(2,1)S(1)}, u32[]{:S(2)}, u32[]{:S(2)}) collective-permute-start(bf16[1,32,1,16]{1,2,3,0:T(2,128)(2,1)S(1)} %get-tuple-element.24), channel_id=1, source_target_pairs={{1,0},{2,1},{3,2},{4,3},{5,4},{6,5},{7,6},{9,8},{10,9},{11,10},{12... | collective-permute-start | bytes 3080 | tf_op jit(solution)/shard_map/ppermute | solution.py:17
  15.2 9.6 %collective-permute-start.1 = (bf16[1,64,1,128]{3,1,2,0:T(8,128)(2,1)S(1)}, bf16[1,64,1,128]{3,1,2,0:T(8,128)(2,1)S(1)}, u32[]{:S(2)}, u32[]{:S(2)}) collective-permute-start(bf16[1,64,1,128]{3,1,2,0:T(8,128)(2,1)S(1)} %copy-done.3), channel_id=1, source_target_pairs={{1,0},{2,1},{3,2},{4,3},{5,4},{6,5},{7,6},{9,8},{10,9},{11,10},{12... | collective-permute-start | bytes 49160 | tf_op jit(solution)/shard_map/ppermute | solution.py:17
  16.5 8.3 %collective-permute-start = (bf16[1,64,1,128]{3,1,2,0:T(8,128)(2,1)S(1)}, bf16[1,64,1,128]{3,1,2,0:T(8,128)(2,1)S(1)}, u32[]{:S(2)}, u32[]{:S(2)}) collective-permute-start(bf16[1,64,1,128]{3,1,2,0:T(8,128)(2,1)S(1)} %copy-done.3), channel_id=1, source_target_pairs={{0,1},{1,2},{2,3},{3,4},{4,5},{5,6},{6,7},{8,9},{9,10},{10,11},{11... | collective-permute-start | bytes 49160 | tf_op jit(solution)/shard_map/ppermute | solution.py:15
  21.6 0.9 copy-start.1
  26.2 13.2 %all-to-all-start = ((bf16[8,2,2048]{2,1,0:T(2,128)(2,1)}), bf16[8,2,2048]{2,1,0:T(2,128)(2,1)S(1)}, u32[]{:S(2)}, u32[]{:S(2)}) async-start(bf16[8,2,2048]{2,1,0:T(2,128)(2,1)} %reshape.430), calls=%async_computation | async-start | bytes 131072 | tf_op jit(solution)/shard_map/all_to_all | solution.py:100
  32.5 147.8 %all-reduce.6.cloned.1.call-start = ((), (), s32[]{:S(2)}) async-start(), calls=%async_computation.1 | async-start | bytes 294912 | tf_op jit(solution)/shard_map/psum | solution.py:126
  39.6 3.8 %collective-permute-start.2 = (bf16[1,64,1,16]{1,2,3,0:T(2,128)(2,1)S(1)}, bf16[1,64,1,16]{1,2,3,0:T(2,128)(2,1)S(1)}, u32[]{:S(2)}, u32[]{:S(2)}) collective-permute-start(bf16[1,64,1,16]{1,2,3,0:T(2,128)(2,1)S(1)} %get-tuple-element.27), channel_id=1, source_target_pairs={{0,1},{1,2},{2,3},{3,4},{4,5},{5,6},{6,7},{8,9},{9,10},{10,11},{11... | collective-permute-start | bytes 6152 | tf_op jit(solution)/shard_map/ppermute | solution.py:15
  41.9 5.5 %collective-permute-start.3 = (bf16[1,64,1,16]{1,2,3,0:T(2,128)(2,1)S(1)}, bf16[1,64,1,16]{1,2,3,0:T(2,128)(2,1)S(1)}, u32[]{:S(2)}, u32[]{:S(2)}) collective-permute-start(bf16[1,64,1,16]{1,2,3,0:T(2,128)(2,1)S(1)} %get-tuple-element.28), channel_id=1, source_target_pairs={{1,0},{2,1},{3,2},{4,3},{5,4},{6,5},{7,6},{9,8},{10,9},{11,10},{12... | collective-permute-start | bytes 6152 | tf_op jit(solution)/shard_map/ppermute | solution.py:17
  43.4 4.1 %copy-start.2 = (bf16[3,3,64,32]{2,3,1,0:T(8,128)(2,1)S(1)}, bf16[3,3,64,32]{2,3,1,0:T(8,128)(2,1)}, u32[]{:S(2)}) copy-start(bf16[3,3,64,32]{2,3,1,0:T(8,128)(2,1)} %param.8) | copy-start | bytes 110596
  49.8 0.7 copy-start.4
  53.1 6.6 %collective-permute-start.4 = (bf16[1,32,1,16]{2,1,3,0:T(8,128)(2,1)S(1)}, bf16[1,32,1,16]{2,1,3,0:T(8,128)(2,1)S(1)}, u32[]{:S(2)}, u32[]{:S(2)}) collective-permute-start(bf16[1,32,1,16]{2,1,3,0:T(8,128)(2,1)S(1)} %get-tuple-element.25), channel_id=1, source_target_pairs={{0,1},{1,2},{2,3},{3,4},{4,5},{5,6},{6,7},{8,9},{9,10},{10,11},{11... | collective-permute-start | bytes 3080 | tf_op jit(solution)/shard_map/ppermute | solution.py:15
  57.2 6.9 %collective-permute-start.5 = (bf16[1,32,1,16]{2,1,3,0:T(8,128)(2,1)S(1)}, bf16[1,32,1,16]{2,1,3,0:T(8,128)(2,1)S(1)}, u32[]{:S(2)}, u32[]{:S(2)}) collective-permute-start(bf16[1,32,1,16]{2,1,3,0:T(8,128)(2,1)S(1)} %get-tuple-element.26), channel_id=1, source_target_pairs={{1,0},{2,1},{3,2},{4,3},{5,4},{6,5},{7,6},{9,8},{10,9},{11,10},{12... | collective-permute-start | bytes 3080 | tf_op jit(solution)/shard_map/ppermute | solution.py:17
Sparse Core Ops, SparseCore 0:
  59.8 120.3 all-reduce.5
where the time goes:
time: 191 us; the launch traced here: 189 us
  waiting for transfers between devices  82.9 us (43%)
  blocking collectives  42.4 us (22%)
  starting transfers between devices  27.9 us (15%)
  between operations  15.1 us (8%)
  matrix products  12.8 us (7%)
  local copies, waits for them, and re-layouts  6.21 us (3%)
    psum x1, waiting for transfers between devices, local(): lax.psum((grad_first, grad_bias, grad_second, grad_skip), ('img', 'tile'))  67.9 us
    psum x1, blocking collectives, local(): lax.psum((grad_first, grad_bias, grad_second, grad_skip), ('img', 'tile'))  42.4 us
    ppermute x4, starting transfers between devices, with_halo(): lax.ppermute(tail, axis, [(i, (i + 1) % count) for i in range(ends)])  16.4 us
    ppermute x4, waiting for transfers between devices, with_halo(): lax.ppermute(head, axis, [((i + 1) % count, i) for i in range(ends)])  8.41 us
    all_to_all x1, waiting for transfers between devices, local(): lax.all_to_all(fine_rows, 'tile', split_axis=3, concat_axis=2, tiled=True)  6.57 us
    all_to_all x1, starting transfers between devices, local(): lax.all_to_all(fine_rows, 'tile', split_axis=3, concat_axis=2, tiled=True)  6.3 us
    unnamed x15, local copies, waits for them, and re-layouts  5.57 us
    dot_general x18, matrix products, conv_shift(): jnp.einsum('bcwh,co->bowh', window_part, kernel[shift_w, shift_h], prefer...  5.27 us
  transfers between devices with their start and end apart: 10, of which 4 were waited for; matrix products, arithmetic and copies ran while one was open for 5% of the time, Pallas kernels for 0%

commit v1 on v0

v1 whole, which is shorter than its diff:
```python
import functools
import math

import jax
import jax.numpy as jnp
from jax import lax
from jax.experimental import pallas as pl
from jax.experimental.pallas import tpu as pltpu
from jax.sharding import PartitionSpec as P

F32 = jnp.float32
BF16 = jnp.bfloat16
ROWS = 16
NT = (((1,), (1,)), ((), ()))


def up128(n):
    return -(-n // 128) * 128


def ints(shape, dim):
    return lax.broadcasted_iota(jnp.int32, shape, dim)


def quotient(values, divisor):
    return ((values.astype(F32) + 0.5) * (1.0 / divisor)).astype(jnp.int32)


class Sizes:
    def __init__(self, coarse, cotangent, tiles):
        self.tiles = tiles
        self.cin = coarse.shape[1]
        self.cout = cotangent.shape[1]
        self.coarse_rows = coarse.shape[2] * tiles
        self.coarse_cols = coarse.shape[3]
        self.own_coarse = self.coarse_cols // tiles
        self.width = cotangent.shape[2]
        self.height = cotangent.shape[3]
        self.pitch = self.width + 4
        self.window = self.own_coarse + 4
        self.half = self.window // 2
        self.lanes = up128(self.height * self.pitch)
        self.wide = up128(self.lanes + 2 * self.pitch + 2)


def pack_kernel(z, coarse_ref, out_ref):
    row = coarse_ref[...]
    count = z.tiles * ROWS
    at = ints((count, z.coarse_cols), 0)
    col = ints((count, z.coarse_cols), 1)
    dest = lax.shift_right_logical(at, 4)
    slot = lax.bitwise_and(at, ROWS - 1)
    parts = []
    for half in range(2):
        want = dest * z.own_coarse - 2 + half * z.half + slot
        want = jnp.clip(want, 0, z.coarse_cols - 1)
        pick = jnp.where((want == col) & (slot < z.half), 1.0, 0.0).astype(BF16)
        parts.append(lax.dot_general(pick, row, NT, preferred_element_type=F32))
    packed = jnp.concatenate(parts, axis=1).astype(BF16)
    out_ref[...] = packed.reshape(out_ref.shape)


def prepare_kernel(
    z, scale, cot_ref, wf_ref, ws_ref, alpha_ref, d_hidden_ref, spread_ref, dskip_ref, wf_cat_ref,
    tall_ref, flat_ref,
):
    blend = alpha_ref[0]
    tall_ref[:, : z.width] = cot_ref[...].astype(F32).reshape(z.cout * z.height, z.width)
    flat_ref[...] = jnp.zeros(flat_ref.shape, F32)
    for h in range(z.height):
        piece = tall_ref[pl.ds(h, z.cout, stride=z.height), :]
        start = (h + 1) * z.pitch + 3
        flat_ref[:, start : start + z.width] = piece[:, : z.width]
    flat = flat_ref[...]
    d_second = (flat * (blend * scale)).astype(BF16).astype(F32)
    centre = z.pitch + 1
    dskip_ref[...] = pltpu.roll(flat * ((1.0 - blend) * scale), z.wide - centre, 1)[
        :, : z.lanes
    ].astype(BF16)
    back = []
    for p in range(3):
        for q in range(3):
            start = (2 - q) * z.pitch + 2 - p
            moved = d_second if start == 0 else pltpu.roll(d_second, z.wide - start, 1)
            k = (p * 3 + q) * z.cout
            spread_ref[k : k + z.cout, :] = moved[:, : z.lanes].astype(BF16)
            back.append(ws_ref[p, q])
            c = (p * 3 + q) * z.cin
            wf_cat_ref[:, c : c + z.cin] = wf_ref[p, q]
    d_hidden_ref[...] = jnp.dot(
        jnp.concatenate(back, axis=1), spread_ref[...], preferred_element_type=F32
    )


def main_kernel(
    z, got_ref, d_hidden_ref, spread_ref, dskip_ref, wf_cat_ref, bias_ref,
    grads_ref, up_ref, hidden_ref, interp_ref, taps_ref,
):
    position = lax.axis_index("tile")
    n = ints((ROWS, z.wide), 1) - 1
    slot = ints((ROWS, z.wide), 0)
    h = quotient(n + z.pitch, z.pitch) - 2
    w = n - (h + 1) * z.pitch
    column = position * z.width + w - 2
    inside = (h >= 0) & (h < z.height) & (column >= 0) & (column < z.width * z.tiles)
    w_main = lax.shift_right_logical(w, 1) + 1
    w_other = w_main - 1 + 2 * lax.bitwise_and(w, 1)
    h_main = lax.shift_right_arithmetic(h, 1)
    h_other = jnp.clip(h_main - 1 + 2 * lax.bitwise_and(h, 1), 0, z.coarse_rows - 1)
    col_weights = []
    for half in range(2):
        at = slot + half * z.half
        weight = jnp.where(at == w_main, 0.75, 0.0) + jnp.where(at == w_other, 0.25, 0.0)
        col_weights.append(jnp.where(inside & (slot < z.half), weight, 0.0))
    span = z.coarse_rows * ROWS

    def one_row(r, carry):
        weight = jnp.where(h_main == r, 0.75, 0.0) + jnp.where(h_other == r, 0.25, 0.0)
        for half in range(2):
            at = pl.multiple_of(half * span + r * ROWS, ROWS)
            interp_ref[pl.ds(at, ROWS), :] = (col_weights[half] * weight).astype(BF16)
        return carry

    lax.fori_loop(0, z.coarse_rows, one_row, 0, unroll=z.coarse_rows <= 8)

    turned = got_ref[...].reshape(span, 2 * z.cin).T
    both = jnp.concatenate([turned[: z.cin], turned[z.cin :]], axis=1)
    up = jnp.dot(both, interp_ref[...], preferred_element_type=F32).astype(BF16)
    up32 = up.astype(F32)
    for p in range(3):
        for q in range(3):
            start = q * z.pitch + p
            moved = up32 if start == 0 else pltpu.roll(up32, z.wide - start, 1)
            k = (p * 3 + q) * z.cin
            taps_ref[k : k + z.cin, :] = moved[:, : z.lanes].astype(BF16)
    taps = taps_ref[...]
    centre = taps_ref[4 * z.cin : 5 * z.cin, :]
    up_ref[...] = centre
    pre = jnp.dot(wf_cat_ref[...], taps, preferred_element_type=F32) + bias_ref[...]
    sigma = 1.0 / (1.0 + jnp.exp(-pre))
    m = ints((z.cout, z.lanes), 1)
    mh = quotient(m, z.pitch)
    mw = m - mh * z.pitch
    column = position * z.width + mw - 2
    inside = (mw >= 1) & (mw <= z.width + 2) & (mh < z.height)
    inside = inside & (column >= 0) & (column < z.width * z.tiles)
    hidden = jnp.where(inside, pre * sigma, 0.0).astype(BF16)
    hidden_ref[...] = hidden
    slope = sigma * (1.0 + pre * (1.0 - sigma))
    d_pre = jnp.where(inside, d_hidden_ref[...] * slope, 0.0).astype(BF16)
    first = lax.dot_general(d_pre, taps, NT, preferred_element_type=F32)
    second = lax.dot_general(hidden, spread_ref[...], NT, preferred_element_type=F32)
    skip = lax.dot_general(dskip_ref[...], centre, NT, preferred_element_type=F32)
    ones = jnp.ones((z.cout, z.lanes), BF16)
    biases = lax.dot_general(ones, d_pre, NT, preferred_element_type=F32)
    full = grads_ref.shape[1]
    used = 9 * z.cin + 9 * z.cout + z.cin + z.cout
    pieces = [first, second, skip, biases]
    if full > used:
        pieces.append(jnp.zeros((z.cout, full - used), F32))
    grads_ref[...] = jnp.concatenate(pieces, axis=1).astype(BF16)


def blend_kernel(z, hidden_ref, up_ref, ws_ref, wk_ref, alpha_ref, out_ref, tall_ref):
    blend = alpha_ref[0]
    padded = jnp.concatenate(
        [hidden_ref[...].astype(F32), jnp.zeros((z.cout, z.wide - z.lanes), F32)], axis=1
    )
    padded = pltpu.roll(padded, z.pitch + 1, 1)
    taps = []
    for p in range(3):
        for q in range(3):
            start = q * z.pitch + p
            moved = padded if start == 0 else pltpu.roll(padded, z.wide - start, 1)
            taps.append(moved[:, : z.lanes].astype(BF16))
    taps = jnp.concatenate(taps, axis=0)
    kernel = ws_ref[...].reshape(9 * z.cout, z.cout).T
    second = jnp.dot(kernel, taps, preferred_element_type=F32)
    skip = jnp.dot(wk_ref[...], up_ref[...], preferred_element_type=F32)
    mixed = blend * second + (1.0 - blend) * skip
    for h in range(z.height):
        start = h * z.pitch + 2
        tall_ref[pl.ds(h, z.cout, stride=z.height), : z.width] = mixed[:, start : start + z.width]
    out_ref[...] = tall_ref[:, : z.width].reshape(out_ref.shape).astype(BF16)


def finish_kernel(z, mine_ref, other_ref, first_ref, bias_ref, second_ref, skip_ref):
    total = mine_ref[...].astype(F32) + other_ref[...].astype(F32)
    at = 0
    for p in range(3):
        for q in range(3):
            first_ref[p, q] = total[:, at : at + z.cin]
            at += z.cin
    for p in range(3):
        for q in range(3):
            second_ref[p, q] = total[:, at : at + z.cout]
            at += z.cout
    skip_ref[...] = total[:, at : at + z.cin]
    at += z.cin
    bias_ref[...] = total[0:1, at : at + z.cout]


def call(body, outs, specs, scratch=(), flops=1000000):
    return pl.pallas_call(
        body,
        out_shape=outs,
        in_specs=specs,
        out_specs=jax.tree.map(lambda _: pl.BlockSpec(memory_space=pltpu.VMEM), outs),
        scratch_shapes=scratch,
        compiler_params=pltpu.CompilerParams(vmem_limit_bytes=48 * 1024 * 1024),
        cost_estimate=pl.CostEstimate(flops=flops, bytes_accessed=200000, transcendentals=0),
    )


def butterfly(images, tiles):
    steps = []
    side = 1 if images % 2 == 0 else 0
    k = 1
    while k < images:
        steps.append((k | side if k > 1 else k, 0))
        k *= 2
    k = 1
    while k < tiles:
        steps.append((side, k))
        k *= 2
    return [
        [(i * tiles + t, (i ^ a) * tiles + (t ^ b)) for i in range(images) for t in range(tiles)]
        for a, b in steps
    ]


def local(coarse, w_first, b_first, w_second, w_skip, fade_alpha, cotangent):
    tiles = lax.axis_size("tile")
    images = lax.axis_size("img")
    z = Sizes(coarse, cotangent, tiles)
    vmem = pl.BlockSpec(memory_space=pltpu.VMEM)
    smem = pl.BlockSpec(memory_space=pltpu.SMEM)
    bf, f32 = (lambda *s: jax.ShapeDtypeStruct(s, BF16)), (lambda *s: jax.ShapeDtypeStruct(s, F32))
    total_count = coarse.shape[0] * images * z.width * tiles * z.height
    scale = float(total_count) ** (-0.5)

    packed = call(
        functools.partial(pack_kernel, z), bf(tiles, ROWS, 2 * z.cin), [vmem]
    )(coarse.reshape(z.cin, z.coarse_cols))
    got = lax.all_to_all(packed, "tile", split_axis=0, concat_axis=0, tiled=True)

    cot = jnp.transpose(cotangent[0], (0, 2, 1))
    wf = jnp.transpose(w_first, (0, 1, 3, 2))
    d_hidden, spread, dskip, wf_cat = call(
        functools.partial(prepare_kernel, z, scale),
        (f32(z.cout, z.lanes), bf(9 * z.cout, z.lanes), bf(z.cout, z.lanes), bf(z.cout, 9 * z.cin)),
        [vmem, vmem, vmem, smem],
        [pltpu.VMEM((z.cout * z.height, 128), F32), pltpu.VMEM((z.cout, z.wide), F32)],
    )(cot, wf, w_second, fade_alpha)

    columns = up128(10 * z.cin + 10 * z.cout)
    grads, up, hidden = call(
        functools.partial(main_kernel, z),
        (bf(z.cout, columns), bf(z.cin, z.lanes), bf(z.cout, z.lanes)),
        [vmem] * 6,
        [
            pltpu.VMEM((2 * z.coarse_rows * ROWS, z.wide), BF16),
            pltpu.VMEM((9 * z.cin, z.lanes), BF16),
        ],
    )(got, d_hidden, spread, dskip, wf_cat, b_first.reshape(z.cout, 1))

    blended = call(
        functools.partial(blend_kernel, z),
        bf(z.cout, z.height, z.width),
        [vmem, vmem, vmem, vmem, smem],
        [pltpu.VMEM((z.cout * z.height, 128), F32)],
    )(hidden, up, w_second, jnp.transpose(w_skip), fade_alpha)

    steps = butterfly(images, tiles)
    for pairs in steps[:-1]:
        other = lax.ppermute(grads, ("img", "tile"), pairs)
        grads = (grads.astype(F32) + other.astype(F32)).astype(BF16)
    other = lax.ppermute(grads, ("img", "tile"), steps[-1])
    first, bias, second, skip = call(
        functools.partial(finish_kernel, z),
        (f32(3, 3, z.cout, z.cin), f32(1, z.cout), f32(3, 3, z.cout, z.cout), f32(z.cout, z.cin)),
        [vmem, vmem],
    )(grads, other)
    return (
        jnp.transpose(blended, (0, 2, 1))[None],
        jnp.transpose(first, (0, 1, 3, 2)),
        bias.reshape(z.cout),
        second,
        jnp.transpose(skip),
    )


def solution(mesh):
    placed = (P("img", None, "tile", None), P(), P(), P(), P(), P(), P("img", None, "tile", None))
    return jax.shard_map(
        local,
        mesh=mesh,
        in_specs=placed,
        out_specs=(P("img", None, "tile", None), P(), P(), P(), P()),
        check_vma=False,
    )
```

time: 191 us -> 38.8 us (0.20)
  waiting for transfers between devices: 82.9 us -> 19.4 us
  blocking collectives: 42.4 us -> 0 us
  starting transfers between devices: 27.9 us -> 9.55 us
  between operations: 15.1 us -> 1.36 us
  matrix products: 12.8 us -> 0 us
  Pallas kernels: 0 us -> 4.44 us
  local copies, waits for them, and re-layouts: 6.21 us -> 3.59 us
    psum x1 -> x0, waiting for transfers between devices: 67.9 us -> none  [local(): lax.psum((grad_first, grad_bias, grad_second, grad_skip), ('img', 'tile'))]
    psum x1 -> x0, blocking collectives: 42.4 us -> none  [local(): lax.psum((grad_first, grad_bias, grad_second, grad_skip), ('img', 'tile'))]
    ppermute x8 -> x5, starting transfers between devices: 21.6 us -> 2.29 us  [the longest x4 1.94 us: local(): other = lax.ppermute(grads, ('img', 'tile'), pairs)]
    dot_general x47 -> x0, matrix products: 12.8 us -> none  [the longest x18 5.27 us: conv_shift(): jnp.einsum('bcwh,co->bowh', window_part, kernel[shift_w, shift_h], prefer...]
    ppermute x8 -> x5, waiting for transfers between devices: 8.44 us -> 16.4 us  [the longest x4 11.7 us: local(): other = lax.ppermute(grads, ('img', 'tile'), pairs)]
    pallas_call x0 -> x5, Pallas kernels: none -> 4.44 us  [the longest x1 1.24 us: local(): call(functools.partial(blend_kernel, z), bf(z.cout, z.height, z.width), [...]
    all_to_all x1, waiting for transfers between devices: 6.57 us -> 3 us  [local(): lax.all_to_all(packed, 'tile', split_axis=0, concat_axis=0, tiled=True)]
    unnamed x15 -> x12, local copies, waits for them, and re-layouts: 5.57 us -> 3.51 us
  transfers between devices with their start and end apart: 10 -> 6, of which waited for: 4 -> 6; matrix products, arithmetic and copies ran while one was open for 5% -> 0% of each run, Pallas kernels for 0% -> 5%
where the time goes in v1:
time: 38.8 us; the launch traced here: 38.4 us
  waiting for transfers between devices  19.4 us (50%)
  starting transfers between devices  9.55 us (25%)
  Pallas kernels  4.44 us (11%)
  local copies, waits for them, and re-layouts  3.59 us (9%)
  between operations  1.36 us (4%)
    ppermute x4, waiting for transfers between devices, local(): other = lax.ppermute(grads, ('img', 'tile'), pairs)  11.7 us
    all_to_all x1, starting transfers between devices, local(): lax.all_to_all(packed, 'tile', split_axis=0, concat_axis=0, tiled=True)  7.25 us
    ppermute x1, waiting for transfers between devices, local(): other = lax.ppermute(grads, ('img', 'tile'), steps[-1])  4.64 us
    unnamed x12, local copies, waits for them, and re-layouts  3.51 us
    all_to_all x1, waiting for transfers between devices, local(): lax.all_to_all(packed, 'tile', split_axis=0, concat_axis=0, tiled=True)  3 us
    ppermute x4, starting transfers between devices, local(): other = lax.ppermute(grads, ('img', 'tile'), pairs)  1.94 us
    pallas_call x1, Pallas kernels, local(): call(functools.partial(blend_kernel, z), bf(z.cout, z.height, z.width), [...  1.24 us
    pallas_call x1, Pallas kernels, local(): call(functools.partial(main_kernel, z), (bf(z.cout, columns), bf(z.cin, z...  1.07 us
  transfers between devices with their start and end apart: 6, of which 6 were waited for; matrix products, arithmetic and copies ran while one was open for 0% of the time, Pallas kernels for 5%

profile of v1, /device:TPU:0, one launch (start us, length us, event | category | flops | bytes accessed | tf_op | source)
XLA Modules:
  0.0 38.4 jit_solution(15758984867718583043)
XLA Ops:
  0.6 0.0 copy-start
  0.6 0.0 copy-start.3
  0.7 0.7 %copy-done.3 = bf16[1,64,1,128]{3,1,2,0:T(8,128)(2,1)S(1)} copy-done((bf16[1,64,1,128]{3,1,2,0:T(8,128)(2,1)S(1)}, bf16[1,64,1,128]{3,1,2,0:T(8,128)(2,1)}, u32[]{:S(2)}) %copy-start.3) | copy-done | bytes 16408
  1.4 0.8 %shard_map.110 = bf16[8,16,128]{2,1,0:T(8,128)(2,1)} custom-call(bf16[64,128]{1,0:T(8,128)(2,1)S(1)} %bitcast.15), custom_call_target="tpu_custom_call" | custom-call | flops 1000000 | bytes 200000 | tf_op jit(solution)/shard_map/pallas_call | solution.py:242
  2.2 7.3 %all-to-all-start = ((bf16[8,16,128]{2,1,0:T(8,128)(2,1)}), bf16[8,16,128]{2,1,0:T(8,128)(2,1)S(1)}, u32[]{:S(2)}, u32[]{:S(2)}) async-start(bf16[8,16,128]{2,1,0:T(8,128)(2,1)} %shard_map.110), calls=%async_computation | async-start | bytes 65536 | tf_op jit(solution)/shard_map/all_to_all | solution.py:245
  10.1 0.0 copy-start.5
  10.1 0.6 %copy-done.5 = f32[32]{0:T(128)S(1)} copy-done((f32[32]{0:T(128)S(1)}, f32[32]{0:T(128)}, u32[]{:S(2)}) %copy-start.5) | copy-done | bytes 152
  10.8 0.1 copy.12.bias_ref
  10.9 0.0 copy-done
  10.9 0.0 copy-start.1
  10.9 0.9 %copy-done.1 = bf16[1,32,32,16]{2,3,1,0:T(8,128)(2,1)S(1)} copy-done((bf16[1,32,32,16]{2,3,1,0:T(8,128)(2,1)S(1)}, bf16[1,32,32,16]{2,3,1,0:T(8,128)(2,1)}, u32[]{:S(2)}) %copy-start.1) | copy-done | bytes 32792
  11.8 0.0 copy-start.2
  11.8 0.9 %copy-done.2 = bf16[3,3,64,32]{2,3,1,0:T(8,128)(2,1)S(1)} copy-done((bf16[3,3,64,32]{2,3,1,0:T(8,128)(2,1)S(1)}, bf16[3,3,64,32]{2,3,1,0:T(8,128)(2,1)}, u32[]{:S(2)}) %copy-start.2) | copy-done | bytes 36888
  12.7 0.5 %shard_map.111 = (f32[32,640]{1,0:T(8,128)S(1)}, bf16[288,640]{1,0:T(8,128)(2,1)S(1)}, bf16[32,640]{1,0:T(8,128)(2,1)S(1)}, bf16[32,576]{1,0:T(8,128)(2,1)S(1)}) custom-call(bf16[32,16,32]{2,1,0:T(8,128)(2,1)S(1)} %bitcast.13, bf16[3,3,32,64]{3,2,1,0:T(8,128)(2,1)S(1)} %bitcast.14, bf16[3,3,32,32]{3,2,1,0:T(8,128)(2,1)S(1)} %copy-done, f32[1]{0:T(128)S(6)} %copy.13.alpha_ref), custom_call_target="tpu_custom_call" | custom-call | flops 1000000 | bytes 200000 | tf_op jit(solution)/shard_map/pallas_call | solution.py:249
  13.2 3.0 %all-to-all-done.got_ref = bf16[8,16,128]{2,1,0:T(8,128)(2,1)S(1)} async-done(((bf16[8,16,128]{2,1,0:T(8,128)(2,1)}), bf16[8,16,128]{2,1,0:T(8,128)(2,1)S(1)}, u32[]{:S(2)}, u32[]{:S(2)}) %all-to-all-start) | async-done | bytes 32800 | tf_op jit(solution)/shard_map/all_to_all | solution.py:245
  16.2 1.1 %shard_map.112 = (bf16[32,1024]{1,0:T(8,128)(2,1)S(1)}, bf16[64,640]{1,0:T(8,128)(2,1)S(1)}, bf16[32,640]{1,0:T(8,128)(2,1)S(1)}) custom-call(bf16[8,16,128]{2,1,0:T(8,128)(2,1)S(1)} %all-to-all-done.got_ref, f32[32,640]{1,0:T(8,128)S(1)} %get-tuple-element.16.d_hidden_ref, bf16[288,640]{1,0:T(8,128)(2,1)S(1)} %get-tuple-element.17.spread_ref, ...), custom_call_target="tpu_custom_call" | custom-call | flops 1000000 | bytes 200000 | tf_op jit(solution)/shard_map/pallas_call | solution.py:257
  17.2 0.1 collective-permute-start
  17.3 1.2 %collective-permute-done = bf16[32,1024]{1,0:T(8,128)(2,1)S(1)} collective-permute-done((bf16[32,1024]{1,0:T(8,128)(2,1)S(1)}, bf16[32,1024]{1,0:T(8,128)(2,1)S(1)}, u32[]{:S(2)}, u32[]{:S(2)}) %collective-permute-start) | collective-permute-done | bytes 65568 | tf_op jit(solution)/shard_map/ppermute | solution.py:276
  18.6 1.3 %collective-permute-start.1 = (bf16[32,1024]{1,0:T(8,128)(2,1)S(1)}, bf16[32,1024]{1,0:T(8,128)(2,1)S(1)}, u32[]{:S(2)}, u32[]{:S(2)}) collective-permute-start(bf16[32,1024]{1,0:T(8,128)(2,1)S(1)} %add_convert_fusion.3), channel_id=1, source_target_pairs={{0,24},{1,25},{2,26},{3,27},{4,28},{5,29},{6,30},{7,31},{8,16},{9,... | collective-permute-start | bytes 196616 | tf_op jit(solution)/shard_map/ppermute | solution.py:276
  19.9 2.8 %collective-permute-done.1 = bf16[32,1024]{1,0:T(8,128)(2,1)S(1)} collective-permute-done((bf16[32,1024]{1,0:T(8,128)(2,1)S(1)}, bf16[32,1024]{1,0:T(8,128)(2,1)S(1)}, u32[]{:S(2)}, u32[]{:S(2)}) %collective-permute-start.1) | collective-permute-done | bytes 65568 | tf_op jit(solution)/shard_map/ppermute | solution.py:276
  22.7 0.3 collective-permute-start.2
  23.0 3.8 %collective-permute-done.2 = bf16[32,1024]{1,0:T(8,128)(2,1)S(1)} collective-permute-done((bf16[32,1024]{1,0:T(8,128)(2,1)S(1)}, bf16[32,1024]{1,0:T(8,128)(2,1)S(1)}, u32[]{:S(2)}, u32[]{:S(2)}) %collective-permute-start.2) | collective-permute-done | bytes 65568 | tf_op jit(solution)/shard_map/ppermute | solution.py:276
  26.9 0.2 collective-permute-start.3
  27.1 3.9 %collective-permute-done.3 = bf16[32,1024]{1,0:T(8,128)(2,1)S(1)} collective-permute-done((bf16[32,1024]{1,0:T(8,128)(2,1)S(1)}, bf16[32,1024]{1,0:T(8,128)(2,1)S(1)}, u32[]{:S(2)}, u32[]{:S(2)}) %collective-permute-start.3) | collective-permute-done | bytes 65568 | tf_op jit(solution)/shard_map/ppermute | solution.py:276
  31.0 0.0 copy-start.4
  31.0 0.4 collective-permute-start.4
  31.4 0.3 copy-done.4
  31.7 1.2 %shard_map.113 = bf16[32,16,32]{2,1,0:T(8,128)(2,1)} custom-call(bf16[32,640]{1,0:T(8,128)(2,1)S(1)} %get-tuple-element.20.hidden_ref, bf16[64,640]{1,0:T(8,128)(2,1)S(1)} %get-tuple-element.21.up_ref, bf16[3,3,32,32]{3,2,1,0:T(8,128)(2,1)S(1)} %copy-done, bf16[32,64]{1,0:T(8,128)(2,1)S(1)} %bitcast.16, f32[1]{0:T(128)S(6)} %copy.13.alpha_ref), custom_call_target="tpu_custom_call" | custom-call | flops 1000000 | bytes 200000 | tf_op jit(solution)/shard_map/pallas_call | solution.py:267
  32.9 4.6 %collective-permute-done.4.other_ref = bf16[32,1024]{1,0:T(8,128)(2,1)S(1)} collective-permute-done((bf16[32,1024]{1,0:T(8,128)(2,1)S(1)}, bf16[32,1024]{1,0:T(8,128)(2,1)S(1)}, u32[]{:S(2)}, u32[]{:S(2)}) %collective-permute-start.4) | collective-permute-done | bytes 65568 | tf_op jit(solution)/shard_map/ppermute | solution.py:278
  37.6 0.8 %shard_map.114 = (f32[3,3,32,64]{3,2,1,0:T(8,128)}, f32[1,32]{1,0:T(1,128)}, f32[3,3,32,32]{3,2,1,0:T(8,128)}, f32[32,64]{1,0:T(8,128)}) custom-call(bf16[32,1024]{1,0:T(8,128)(2,1)S(1)} %add_convert_fusion.mine_ref, bf16[32,1024]{1,0:T(8,128)(2,1)S(1)} %collective-permute-done.4.other_ref), custom_call_target="tpu_custom_call" | custom-call | flops 1000000 | bytes 200000 | tf_op jit(solution)/shard_map/pallas_call | solution.py:279
  (4 shorter events, 0.1 us)
Async XLA Ops:
  0.6 10.2 %copy-start = (bf16[3,3,32,32]{3,2,1,0:T(8,128)(2,1)S(1)}, bf16[3,3,32,32]{3,2,1,0:T(8,128)(2,1)}, u32[]{:S(2)}) copy-start(bf16[3,3,32,32]{3,2,1,0:T(8,128)(2,1)} %ws_ref.3) | copy-start | bytes 55300
  0.6 0.8 %copy-start.3 = (bf16[1,64,1,128]{3,1,2,0:T(8,128)(2,1)S(1)}, bf16[1,64,1,128]{3,1,2,0:T(8,128)(2,1)}, u32[]{:S(2)}) copy-start(bf16[1,64,1,128]{3,1,2,0:T(8,128)(2,1)} %param.7) | copy-start | bytes 49156
  2.2 13.9 %all-to-all-start = ((bf16[8,16,128]{2,1,0:T(8,128)(2,1)}), bf16[8,16,128]{2,1,0:T(8,128)(2,1)S(1)}, u32[]{:S(2)}, u32[]{:S(2)}) async-start(bf16[8,16,128]{2,1,0:T(8,128)(2,1)} %shard_map.110), calls=%async_computation | async-start | bytes 65536 | tf_op jit(solution)/shard_map/all_to_all | solution.py:245
  10.1 0.7 %copy-start.5 = (f32[32]{0:T(128)S(1)}, f32[32]{0:T(128)}, u32[]{:S(2)}) copy-start(f32[32]{0:T(128)} %param.9) | copy-start | bytes 388
  10.9 0.9 %copy-start.1 = (bf16[1,32,32,16]{2,3,1,0:T(8,128)(2,1)S(1)}, bf16[1,32,32,16]{2,3,1,0:T(8,128)(2,1)}, u32[]{:S(2)}) copy-start(bf16[1,32,32,16]{2,3,1,0:T(8,128)(2,1)} %param.13) | copy-start | bytes 98308
  11.8 0.9 %copy-start.2 = (bf16[3,3,64,32]{2,3,1,0:T(8,128)(2,1)S(1)}, bf16[3,3,64,32]{2,3,1,0:T(8,128)(2,1)}, u32[]{:S(2)}) copy-start(bf16[3,3,64,32]{2,3,1,0:T(8,128)(2,1)} %param.8) | copy-start | bytes 110596
  17.2 1.3 %collective-permute-start = (bf16[32,1024]{1,0:T(8,128)(2,1)S(1)}, bf16[32,1024]{1,0:T(8,128)(2,1)S(1)}, u32[]{:S(2)}, u32[]{:S(2)}) collective-permute-start(bf16[32,1024]{1,0:T(8,128)(2,1)S(1)} %get-tuple-element.22), channel_id=1, source_target_pairs={{0,8},{1,9},{2,10},{3,11},{4,12},{5,13},{6,14},{7,15},{8,0},{9,1},... | collective-permute-start | bytes 196616 | tf_op jit(solution)/shard_map/ppermute | solution.py:276
  18.6 4.1 %collective-permute-start.1 = (bf16[32,1024]{1,0:T(8,128)(2,1)S(1)}, bf16[32,1024]{1,0:T(8,128)(2,1)S(1)}, u32[]{:S(2)}, u32[]{:S(2)}) collective-permute-start(bf16[32,1024]{1,0:T(8,128)(2,1)S(1)} %add_convert_fusion.3), channel_id=1, source_target_pairs={{0,24},{1,25},{2,26},{3,27},{4,28},{5,29},{6,30},{7,31},{8,16},{9,... | collective-permute-start | bytes 196616 | tf_op jit(solution)/shard_map/ppermute | solution.py:276
  22.7 4.1 %collective-permute-start.2 = (bf16[32,1024]{1,0:T(8,128)(2,1)S(1)}, bf16[32,1024]{1,0:T(8,128)(2,1)S(1)}, u32[]{:S(2)}, u32[]{:S(2)}) collective-permute-start(bf16[32,1024]{1,0:T(8,128)(2,1)S(1)} %add_convert_fusion.2), channel_id=1, source_target_pairs={{0,9},{1,8},{2,11},{3,10},{4,13},{5,12},{6,15},{7,14},{8,1},{9,0},... | collective-permute-start | bytes 196616 | tf_op jit(solution)/shard_map/ppermute | solution.py:276
  26.9 4.1 %collective-permute-start.3 = (bf16[32,1024]{1,0:T(8,128)(2,1)S(1)}, bf16[32,1024]{1,0:T(8,128)(2,1)S(1)}, u32[]{:S(2)}, u32[]{:S(2)}) collective-permute-start(bf16[32,1024]{1,0:T(8,128)(2,1)S(1)} %add_convert_fusion.1), channel_id=1, source_target_pairs={{0,10},{1,11},{2,8},{3,9},{4,14},{5,15},{6,12},{7,13},{8,2},{9,3},... | collective-permute-start | bytes 196616 | tf_op jit(solution)/shard_map/ppermute | solution.py:276
  31.0 0.7 %copy-start.4 = (bf16[64,32]{0,1:T(8,128)(2,1)S(1)}, bf16[64,32]{0,1:T(8,128)(2,1)}, u32[]{:S(2)}) copy-start(bf16[64,32]{0,1:T(8,128)(2,1)} %param.11) | copy-start | bytes 12292
  31.0 6.6 %collective-permute-start.4 = (bf16[32,1024]{1,0:T(8,128)(2,1)S(1)}, bf16[32,1024]{1,0:T(8,128)(2,1)S(1)}, u32[]{:S(2)}, u32[]{:S(2)}) collective-permute-start(bf16[32,1024]{1,0:T(8,128)(2,1)S(1)} %add_convert_fusion.mine_ref), channel_id=1, source_target_pairs={{0,12},{1,13},{2,14},{3,15},{4,8},{5,9},{6,10},{7,11},{8,4},{9,5},... | collective-permute-start | bytes 196616 | tf_op jit(solution)/shard_map/ppermute | solution.py:278

commit v2 on v1

--- a/solution.py
+++ b/solution.py
@@ -1,5 +1,4 @@
 import functools
-import math
 
 import jax
 import jax.numpy as jnp
@@ -27,7 +26,8 @@
 
 
 class Sizes:
-    def __init__(self, coarse, cotangent, tiles):
+    def __init__(self, coarse, cotangent, images, tiles):
+        self.images = images
         self.tiles = tiles
         self.cin = coarse.shape[1]
         self.cout = cotangent.shape[1]
@@ -60,43 +60,7 @@
     out_ref[...] = packed.reshape(out_ref.shape)
 
 
-def prepare_kernel(
-    z, scale, cot_ref, wf_ref, ws_ref, alpha_ref, d_hidden_ref, spread_ref, dskip_ref, wf_cat_ref,
-    tall_ref, flat_ref,
-):
-    blend = alpha_ref[0]
-    tall_ref[:, : z.width] = cot_ref[...].astype(F32).reshape(z.cout * z.height, z.width)
-    flat_ref[...] = jnp.zeros(flat_ref.shape, F32)
-    for h in range(z.height):
-        piece = tall_ref[pl.ds(h, z.cout, stride=z.height), :]
-        start = (h + 1) * z.pitch + 3
-        flat_ref[:, start : start + z.width] = piece[:, : z.width]
-    flat = flat_ref[...]
-    d_second = (flat * (blend * scale)).astype(BF16).astype(F32)
-    centre = z.pitch + 1
-    dskip_ref[...] = pltpu.roll(flat * ((1.0 - blend) * scale), z.wide - centre, 1)[
-        :, : z.lanes
-    ].astype(BF16)
-    back = []
-    for p in range(3):
-        for q in range(3):
-            start = (2 - q) * z.pitch + 2 - p
-            moved = d_second if start == 0 else pltpu.roll(d_second, z.wide - start, 1)
-            k = (p * 3 + q) * z.cout
-            spread_ref[k : k + z.cout, :] = moved[:, : z.lanes].astype(BF16)
-            back.append(ws_ref[p, q])
-            c = (p * 3 + q) * z.cin
-            wf_cat_ref[:, c : c + z.cin] = wf_ref[p, q]
-    d_hidden_ref[...] = jnp.dot(
-        jnp.concatenate(back, axis=1), spread_ref[...], preferred_element_type=F32
-    )
-
-
-def main_kernel(
-    z, got_ref, d_hidden_ref, spread_ref, dskip_ref, wf_cat_ref, bias_ref,
-    grads_ref, up_ref, hidden_ref, interp_ref, taps_ref,
-):
-    position = lax.axis_index("tile")
+def interpolation(z, position, interp_ref):
     n = ints((ROWS, z.wide), 1) - 1
     slot = ints((ROWS, z.wide), 0)
     h = quotient(n + z.pitch, z.pitch) - 2
@@ -123,7 +87,56 @@
 
     lax.fori_loop(0, z.coarse_rows, one_row, 0, unroll=z.coarse_rows <= 8)
 
-    turned = got_ref[...].reshape(span, 2 * z.cin).T
+
+def prepare_kernel(
+    z, scale, cot_ref, ws_ref, row_ref, d_hidden_ref, spread_ref, dskip_ref, interp_ref, bias_ref,
+    tall_ref, flat_ref,
+):
+    blend = row_ref[:, z.cout :]
+    interpolation(z, lax.axis_index("tile"), interp_ref)
+    diagonal = ints((z.cout, z.cout), 0) == ints((z.cout, z.cout), 1)
+    bias_ref[...] = jnp.sum(jnp.where(diagonal, row_ref[:, : z.cout], 0.0), axis=1, keepdims=True)
+    flat_ref[...] = jnp.zeros(flat_ref.shape, F32)
+    tall_ref[:, : z.width] = cot_ref[...].astype(F32).reshape(z.cout * z.height, z.width)
+    for h in range(z.height):
+        piece = tall_ref[pl.ds(h, z.cout, stride=z.height), :]
+        start = (h + 1) * z.pitch + 3
+        flat_ref[:, start : start + z.width] = piece[:, : z.width]
+    flat = flat_ref[...]
+    d_second = (flat * (blend * scale)).astype(BF16).astype(F32)
+    dskip_ref[...] = pltpu.roll(flat * ((1.0 - blend) * scale), z.wide - (z.pitch + 1), 1)[
+        :, : z.lanes
+    ].astype(BF16)
+    back = []
+    for p in range(3):
+        for q in range(3):
+            start = (2 - q) * z.pitch + 2 - p
+            moved = d_second if start == 0 else pltpu.roll(d_second, z.wide - start, 1)
+            k = (p * 3 + q) * z.cout
+            spread_ref[k : k + z.cout, :] = moved[:, : z.lanes].astype(BF16)
+            back.append(ws_ref[p, q])
+    d_hidden_ref[...] = jnp.dot(
+        jnp.concatenate(back, axis=1), spread_ref[...], preferred_element_type=F32
+    )
+
+
+def holds_top(z):
+    image, tile = lax.axis_index("img"), lax.axis_index("tile")
+    bits = jnp.int32(0)
+    for index, count in ((image, z.images), (tile, z.tiles)):
+        k = 1
+        while k < count:
+            bits = bits ^ (lax.div(index, jnp.int32(k)) & 1)
+            k *= 2
+    return bits == 0
+
+
+def main_kernel(
+    z, got_ref, d_hidden_ref, spread_ref, dskip_ref, wf_ref, bias_ref, interp_ref,
+    keep_ref, give_ref, up_ref, hidden_ref, taps_ref,
+):
+    position = lax.axis_index("tile")
+    turned = got_ref[...].reshape(z.coarse_rows * ROWS, 2 * z.cin).T
     both = jnp.concatenate([turned[: z.cin], turned[z.cin :]], axis=1)
     up = jnp.dot(both, interp_ref[...], preferred_element_type=F32).astype(BF16)
     up32 = up.astype(F32)
@@ -136,7 +149,8 @@
     taps = taps_ref[...]
     centre = taps_ref[4 * z.cin : 5 * z.cin, :]
     up_ref[...] = centre
-    pre = jnp.dot(wf_cat_ref[...], taps, preferred_element_type=F32) + bias_ref[...]
+    kernel = jnp.concatenate([wf_ref[p, q] for p in range(3) for q in range(3)], axis=1)
+    pre = jnp.dot(kernel, taps, preferred_element_type=F32) + bias_ref[...]
     sigma = 1.0 / (1.0 + jnp.exp(-pre))
     m = ints((z.cout, z.lanes), 1)
     mh = quotient(m, z.pitch)
@@ -153,16 +167,20 @@
     skip = lax.dot_general(dskip_ref[...], centre, NT, preferred_element_type=F32)
     ones = jnp.ones((z.cout, z.lanes), BF16)
     biases = lax.dot_general(ones, d_pre, NT, preferred_element_type=F32)
-    full = grads_ref.shape[1]
-    used = 9 * z.cin + 9 * z.cout + z.cin + z.cout
+    full = keep_ref.shape[1]
+    used = 10 * z.cin + 10 * z.cout
     pieces = [first, second, skip, biases]
     if full > used:
         pieces.append(jnp.zeros((z.cout, full - used), F32))
-    grads_ref[...] = jnp.concatenate(pieces, axis=1).astype(BF16)
-
-
-def blend_kernel(z, hidden_ref, up_ref, ws_ref, wk_ref, alpha_ref, out_ref, tall_ref):
-    blend = alpha_ref[0]
+    grads = jnp.concatenate(pieces, axis=1)
+    half = z.cout // 2
+    top = holds_top(z)
+    keep_ref[...] = jnp.where(top, grads[:half], grads[half:])
+    give_ref[...] = jnp.where(top, grads[half:], grads[:half])
+
+
+def blend_kernel(z, hidden_ref, up_ref, ws_ref, wk_ref, row_ref, out_ref, tall_ref):
+    blend = row_ref[:, z.cout :]
     padded = jnp.concatenate(
         [hidden_ref[...].astype(F32), jnp.zeros((z.cout, z.wide - z.lanes), F32)], axis=1
     )
@@ -185,7 +203,11 @@
 
 
 def finish_kernel(z, mine_ref, other_ref, first_ref, bias_ref, second_ref, skip_ref):
-    total = mine_ref[...].astype(F32) + other_ref[...].astype(F32)
+    top = holds_top(z)
+    mine, other = mine_ref[...], other_ref[...]
+    total = jnp.concatenate(
+        [jnp.where(top, mine, other), jnp.where(top, other, mine)], axis=0
+    )
     at = 0
     for p in range(3):
         for q in range(3):
@@ -212,75 +234,92 @@
     )
 
 
-def butterfly(images, tiles):
-    steps = []
-    side = 1 if images % 2 == 0 else 0
-    k = 1
+def swap(values, images, tiles, across):
+    a, b = across
+    pairs = [
+        (i * tiles + t, (i ^ a) * tiles + (t ^ b)) for i in range(images) for t in range(tiles)
+    ]
+    return lax.ppermute(values, ("img", "tile"), pairs)
+
+
+def total_over_chips(mine, images, tiles):
+    bits = []
+    k = 2
     while k < images:
-        steps.append((k | side if k > 1 else k, 0))
+        bits.append((k, 0))
         k *= 2
     k = 1
     while k < tiles:
-        steps.append((side, k))
+        bits.append((0, k))
         k *= 2
-    return [
-        [(i * tiles + t, (i ^ a) * tiles + (t ^ b)) for i in range(images) for t in range(tiles)]
-        for a, b in steps
-    ]
+    for at in range(0, len(bits), 2):
+        group = bits[at : at + 2]
+        sent = mine.astype(BF16)
+        partners = [(a ^ 1, b) for a, b in group]
+        if len(group) == 2:
+            partners.append((group[0][0] ^ group[1][0], group[0][1] ^ group[1][1]))
+        got = [swap(sent, images, tiles, across).astype(F32) for across in partners]
+        mine = sent.astype(F32) + got[0]
+        if len(got) == 3:
+            mine = mine + (got[1] + got[2])
+    return mine
 
 
 def local(coarse, w_first, b_first, w_second, w_skip, fade_alpha, cotangent):
     tiles = lax.axis_size("tile")
     images = lax.axis_size("img")
-    z = Sizes(coarse, cotangent, tiles)
+    z = Sizes(coarse, cotangent, images, tiles)
     vmem = pl.BlockSpec(memory_space=pltpu.VMEM)
-    smem = pl.BlockSpec(memory_space=pltpu.SMEM)
     bf, f32 = (lambda *s: jax.ShapeDtypeStruct(s, BF16)), (lambda *s: jax.ShapeDtypeStruct(s, F32))
     total_count = coarse.shape[0] * images * z.width * tiles * z.height
     scale = float(total_count) ** (-0.5)
 
+    cot = jnp.transpose(cotangent[0], (0, 2, 1))
+    wf = jnp.transpose(w_first, (0, 1, 3, 2))
+    row = jnp.concatenate([b_first, fade_alpha]).reshape(1, z.cout + 1)
     packed = call(
         functools.partial(pack_kernel, z), bf(tiles, ROWS, 2 * z.cin), [vmem]
     )(coarse.reshape(z.cin, z.coarse_cols))
     got = lax.all_to_all(packed, "tile", split_axis=0, concat_axis=0, tiled=True)
 
-    cot = jnp.transpose(cotangent[0], (0, 2, 1))
-    wf = jnp.transpose(w_first, (0, 1, 3, 2))
-    d_hidden, spread, dskip, wf_cat = call(
+    d_hidden, spread, dskip, interp, bias = call(
         functools.partial(prepare_kernel, z, scale),
-        (f32(z.cout, z.lanes), bf(9 * z.cout, z.lanes), bf(z.cout, z.lanes), bf(z.cout, 9 * z.cin)),
-        [vmem, vmem, vmem, smem],
+        (
+            f32(z.cout, z.lanes),
+            bf(9 * z.cout, z.lanes),
+            bf(z.cout, z.lanes),
+            bf(2 * z.coarse_rows * ROWS, z.wide),
+            f32(z.cout, 1),
+        ),
+        [vmem] * 3,
         [pltpu.VMEM((z.cout * z.height, 128), F32), pltpu.VMEM((z.cout, z.wide), F32)],
-    )(cot, wf, w_second, fade_alpha)
+    )(cot, w_second, row)
 
     columns = up128(10 * z.cin + 10 * z.cout)
-    grads, up, hidden = call(
+    half = z.cout // 2
+    keep, give, up, hidden = call(
         functools.partial(main_kernel, z),
-        (bf(z.cout, columns), bf(z.cin, z.lanes), bf(z.cout, z.lanes)),
-        [vmem] * 6,
-        [
-            pltpu.VMEM((2 * z.coarse_rows * ROWS, z.wide), BF16),
-            pltpu.VMEM((9 * z.cin, z.lanes), BF16),
-        ],
-    )(got, d_hidden, spread, dskip, wf_cat, b_first.reshape(z.cout, 1))
+        (f32(half, columns), f32(half, columns), bf(z.cin, z.lanes), bf(z.cout, z.lanes)),
+        [vmem] * 7,
+        [pltpu.VMEM((9 * z.cin, z.lanes), BF16)],
+    )(got, d_hidden, spread, dskip, wf, bias, interp)
 
     blended = call(
         functools.partial(blend_kernel, z),
         bf(z.cout, z.height, z.width),
-        [vmem, vmem, vmem, vmem, smem],
+        [vmem] * 5,
         [pltpu.VMEM((z.cout * z.height, 128), F32)],
-    )(hidden, up, w_second, jnp.transpose(w_skip), fade_alpha)
-
-    steps = butterfly(images, tiles)
-    for pairs in steps[:-1]:
-        other = lax.ppermute(grads, ("img", "tile"), pairs)
-        grads = (grads.astype(F32) + other.astype(F32)).astype(BF16)
-    other = lax.ppermute(grads, ("img", "tile"), steps[-1])
+    )(hidden, up, w_second, jnp.transpose(w_skip), row)
+
+    mine = keep + swap(give, images, tiles, (1, 0))
+    mine = total_over_chips(mine, images, tiles)
+    mine, blended = lax.optimization_barrier((mine, blended))
+    other = swap(mine, images, tiles, (1, 0))
     first, bias, second, skip = call(
         functools.partial(finish_kernel, z),
         (f32(3, 3, z.cout, z.cin), f32(1, z.cout), f32(3, 3, z.cout, z.cout), f32(z.cout, z.cin)),
-        [vmem, vmem],
-    )(grads, other)
+        [vmem] * 2,
+    )(mine, other)
     return (
         jnp.transpose(blended, (0, 2, 1))[None],
         jnp.transpose(first, (0, 1, 3, 2)),

time: 38.8 us -> 33.4 us (0.86)
  waiting for transfers between devices: 19.4 us -> 10.4 us
  starting transfers between devices: 9.55 us -> 15 us
  local copies, waits for them, and re-layouts: 3.59 us -> 1.66 us
    ppermute x5 -> x8, waiting for transfers between devices: 16.4 us -> 6.01 us  [swap(): return lax.ppermute(values, ('img', 'tile'), pairs)]
    ppermute x5 -> x8, starting transfers between devices: 2.29 us -> 7.73 us  [swap(): return lax.ppermute(values, ('img', 'tile'), pairs)]
    unnamed x12, local copies, waits for them, and re-layouts: 3.51 us -> 1.66 us
    all_to_all x1, waiting for transfers between devices: 3 us -> 4.36 us  [local(): lax.all_to_all(packed, 'tile', split_axis=0, concat_axis=0, tiled=True)]
  transfers between devices with their start and end apart: 6 -> 9, of which waited for: 6 -> 7; matrix products, arithmetic and copies ran while one was open for 0% -> 0% of each run, Pallas kernels for 5% -> 6%
where the time goes in v2:
time: 33.4 us; the launch traced here: 33.1 us
  starting transfers between devices  15 us (45%)
  waiting for transfers between devices  10.4 us (31%)
  Pallas kernels  4.59 us (14%)
  local copies, waits for them, and re-layouts  1.66 us (5%)
  between operations  1.37 us (4%)
    ppermute x8, starting transfers between devices, swap(): return lax.ppermute(values, ('img', 'tile'), pairs)  7.73 us
    all_to_all x1, starting transfers between devices, local(): lax.all_to_all(packed, 'tile', split_axis=0, concat_axis=0, tiled=True)  7.25 us
    ppermute x8, waiting for transfers between devices, swap(): return lax.ppermute(values, ('img', 'tile'), pairs)  6.01 us
    all_to_all x1, waiting for transfers between devices, local(): lax.all_to_all(packed, 'tile', split_axis=0, concat_axis=0, tiled=True)  4.36 us
    unnamed x12, local copies, waits for them, and re-layouts  1.66 us
    pallas_call x1, Pallas kernels, local(): call(functools.partial(blend_kernel, z), bf(z.cout, z.height, z.width), [...  1.24 us
    pallas_call x1, Pallas kernels, local(): call(functools.partial(main_kernel, z), (f32(half, columns), f32(half, co...  1.05 us
    pallas_call x1, Pallas kernels, local(): call(functools.partial(pack_kernel, z), bf(tiles, ROWS, 2 * z.cin), [vmem])  0.83 us
  transfers between devices with their start and end apart: 9, of which 7 were waited for; matrix products, arithmetic and copies ran while one was open for 0% of the time, Pallas kernels for 6%

profile of v2, /device:TPU:0, one launch (start us, length us, event | category | flops | bytes accessed | tf_op | source)
XLA Modules:
  0.0 33.1 jit_solution(8086634723507712547)
XLA Ops:
  0.6 0.0 copy-start
  0.6 0.0 copy-start.3
  0.7 0.7 %copy-done.3 = bf16[1,64,1,128]{3,1,2,0:T(8,128)(2,1)S(1)} copy-done((bf16[1,64,1,128]{3,1,2,0:T(8,128)(2,1)S(1)}, bf16[1,64,1,128]{3,1,2,0:T(8,128)(2,1)}, u32[]{:S(2)}) %copy-start.3) | copy-done | bytes 16408
  1.4 0.8 %shard_map.110 = bf16[8,16,128]{2,1,0:T(8,128)(2,1)} custom-call(bf16[64,128]{1,0:T(8,128)(2,1)S(1)} %bitcast.16), custom_call_target="tpu_custom_call" | custom-call | flops 1000000 | bytes 200000 | tf_op jit(solution)/shard_map/pallas_call | solution.py:280
  2.2 7.3 %all-to-all-start = ((bf16[8,16,128]{2,1,0:T(8,128)(2,1)}), bf16[8,16,128]{2,1,0:T(8,128)(2,1)S(1)}, u32[]{:S(2)}, u32[]{:S(2)}) async-start(bf16[8,16,128]{2,1,0:T(8,128)(2,1)} %shard_map.110), calls=%async_computation | async-start | bytes 65536 | tf_op jit(solution)/shard_map/all_to_all | solution.py:283
  9.5 0.0 copy-start.5
  10.1 0.0 copy-done.5
  10.2 0.1 maximum_bitcast_fusion.row_ref
  10.2 0.0 copy-done
  10.2 0.0 copy-start.1
  10.2 0.9 %copy-done.1 = bf16[1,32,32,16]{2,3,1,0:T(8,128)(2,1)S(1)} copy-done((bf16[1,32,32,16]{2,3,1,0:T(8,128)(2,1)S(1)}, bf16[1,32,32,16]{2,3,1,0:T(8,128)(2,1)}, u32[]{:S(2)}) %copy-start.1) | copy-done | bytes 32792
  11.1 0.0 copy-start.2
  11.1 0.6 %shard_map.111 = (f32[32,640]{1,0:T(8,128)S(1)}, bf16[288,640]{1,0:T(8,128)(2,1)S(1)}, bf16[32,640]{1,0:T(8,128)(2,1)S(1)}, bf16[256,768]{1,0:T(8,128)(2,1)S(1)}, f32[32,1]{1,0:T(8,128)S(1)}) custom-call(bf16[32,16,32]{2,1,0:T(8,128)(2,1)S(1)} %bitcast.14, bf16[3,3,32,32]{3,2,1,0:T(8,128)(2,1)S(1)} %copy-done, f32[1,33]{1,0:T(1,128)S(1)} %maximum_bitcast_fusion.row_ref), custom_call_target="tpu_custom_call" | custom-call | flops 1000000 | bytes 200000 | tf_op jit(solution)/shard_map/pallas_call | solution.py:285
  11.8 4.4 %all-to-all-done.got_ref = bf16[8,16,128]{2,1,0:T(8,128)(2,1)S(1)} async-done(((bf16[8,16,128]{2,1,0:T(8,128)(2,1)}), bf16[8,16,128]{2,1,0:T(8,128)(2,1)S(1)}, u32[]{:S(2)}, u32[]{:S(2)}) %all-to-all-start) | async-done | bytes 32800 | tf_op jit(solution)/shard_map/all_to_all | solution.py:283
  16.2 0.0 copy-done.2
  16.2 1.0 %shard_map.112 = (f32[16,1024]{1,0:T(8,128)S(1)}, f32[16,1024]{1,0:T(8,128)S(1)}, bf16[64,640]{1,0:T(8,128)(2,1)S(1)}, bf16[32,640]{1,0:T(8,128)(2,1)S(1)}) custom-call(bf16[8,16,128]{2,1,0:T(8,128)(2,1)S(1)} %all-to-all-done.got_ref, f32[32,640]{1,0:T(8,128)S(1)} %get-tuple-element.20.d_hidden_ref, bf16[288,640]{1,0:T(8,128)(2,1)S(1)} %get-tuple-element.21.spread_ref, ...), custom_call_target="tpu_custom_call" | custom-call | flops 1000000 | bytes 200000 | tf_op jit(solution)/shard_map/pallas_call | solution.py:300
  17.2 0.1 collective-permute-start
  17.3 1.2 %collective-permute-done = f32[16,1024]{1,0:T(8,128)S(1)} collective-permute-done((f32[16,1024]{1,0:T(8,128)S(1)}, f32[16,1024]{1,0:T(8,128)S(1)}, u32[]{:S(2)}, u32[]{:S(2)}) %collective-permute-start) | collective-permute-done | bytes 65568 | tf_op jit(solution)/shard_map/ppermute | solution.py:242
  18.6 1.5 %collective-permute-start.3 = (bf16[16,1024]{1,0:T(8,128)(2,1)S(1)}, bf16[16,1024]{1,0:T(8,128)(2,1)S(1)}, u32[]{:S(2)}, u32[]{:S(2)}) collective-permute-start(bf16[16,1024]{1,0:T(8,128)(2,1)S(1)} %add_convert_fusion.1), channel_id=1, source_target_pairs={{0,17},{1,16},{2,19},{3,18},{4,21},{5,20},{6,23},{7,22},{8,25},{9,... | collective-permute-start | bytes 98312 | tf_op jit(solution)/shard_map/ppermute | solution.py:242
  20.1 1.0 %collective-permute-start.2 = (bf16[16,1024]{1,0:T(8,128)(2,1)S(1)}, bf16[16,1024]{1,0:T(8,128)(2,1)S(1)}, u32[]{:S(2)}, u32[]{:S(2)}) collective-permute-start(bf16[16,1024]{1,0:T(8,128)(2,1)S(1)} %add_convert_fusion.1), channel_id=1, source_target_pairs={{0,9},{1,8},{2,11},{3,10},{4,13},{5,12},{6,15},{7,14},{8,1},{9,0},... | collective-permute-start | bytes 98312 | tf_op jit(solution)/shard_map/ppermute | solution.py:242
  21.1 0.7 %collective-permute-start.1 = (bf16[16,1024]{1,0:T(8,128)(2,1)S(1)}, bf16[16,1024]{1,0:T(8,128)(2,1)S(1)}, u32[]{:S(2)}, u32[]{:S(2)}) collective-permute-start(bf16[16,1024]{1,0:T(8,128)(2,1)S(1)} %add_convert_fusion.1), channel_id=1, source_target_pairs={{0,24},{1,25},{2,26},{3,27},{4,28},{5,29},{6,30},{7,31},{8,16},{9,... | collective-permute-start | bytes 98312 | tf_op jit(solution)/shard_map/ppermute | solution.py:242
  21.8 1.9 %collective-permute-done.3 = bf16[16,1024]{1,0:T(8,128)(2,1)S(1)} collective-permute-done((bf16[16,1024]{1,0:T(8,128)(2,1)S(1)}, bf16[16,1024]{1,0:T(8,128)(2,1)S(1)}, u32[]{:S(2)}, u32[]{:S(2)}) %collective-permute-start.3) | collective-permute-done | bytes 32800 | tf_op jit(solution)/shard_map/ppermute | solution.py:242
  23.7 0.0 collective-permute-done.2
  23.7 0.7 %collective-permute-done.1 = bf16[16,1024]{1,0:T(8,128)(2,1)S(1)} collective-permute-done((bf16[16,1024]{1,0:T(8,128)(2,1)S(1)}, bf16[16,1024]{1,0:T(8,128)(2,1)S(1)}, u32[]{:S(2)}, u32[]{:S(2)}) %collective-permute-start.1) | collective-permute-done | bytes 32800 | tf_op jit(solution)/shard_map/ppermute | solution.py:242
  24.4 0.0 copy-start.4
  24.5 0.6 %collective-permute-start.6 = (bf16[16,1024]{1,0:T(8,128)(2,1)S(1)}, bf16[16,1024]{1,0:T(8,128)(2,1)S(1)}, u32[]{:S(2)}, u32[]{:S(2)}) collective-permute-start(bf16[16,1024]{1,0:T(8,128)(2,1)S(1)} %add_convert_fusion), channel_id=1, source_target_pairs={{0,6},{1,7},{2,4},{3,5},{4,2},{5,3},{6,0},{7,1},{8,14},{9,15},{10,... | collective-permute-start | bytes 98312 | tf_op jit(solution)/shard_map/ppermute | solution.py:242
  25.1 1.2 %collective-permute-start.5 = (bf16[16,1024]{1,0:T(8,128)(2,1)S(1)}, bf16[16,1024]{1,0:T(8,128)(2,1)S(1)}, u32[]{:S(2)}, u32[]{:S(2)}) collective-permute-start(bf16[16,1024]{1,0:T(8,128)(2,1)S(1)} %add_convert_fusion), channel_id=1, source_target_pairs={{0,12},{1,13},{2,14},{3,15},{4,8},{5,9},{6,10},{7,11},{8,4},{9,5},... | collective-permute-start | bytes 98312 | tf_op jit(solution)/shard_map/ppermute | solution.py:242
  26.3 2.3 %collective-permute-start.4 = (bf16[16,1024]{1,0:T(8,128)(2,1)S(1)}, bf16[16,1024]{1,0:T(8,128)(2,1)S(1)}, u32[]{:S(2)}, u32[]{:S(2)}) collective-permute-start(bf16[16,1024]{1,0:T(8,128)(2,1)S(1)} %add_convert_fusion), channel_id=1, source_target_pairs={{0,10},{1,11},{2,8},{3,9},{4,14},{5,15},{6,12},{7,13},{8,2},{9,3},... | collective-permute-start | bytes 98312 | tf_op jit(solution)/shard_map/ppermute | solution.py:242
  28.6 0.0 copy-done.4
  28.6 1.2 %shard_map.113 = bf16[32,16,32]{2,1,0:T(8,128)(2,1)} custom-call(bf16[32,640]{1,0:T(8,128)(2,1)S(1)} %get-tuple-element.27.hidden_ref, bf16[64,640]{1,0:T(8,128)(2,1)S(1)} %get-tuple-element.28.up_ref, bf16[3,3,32,32]{3,2,1,0:T(8,128)(2,1)S(1)} %copy-done, bf16[32,64]{1,0:T(8,128)(2,1)S(1)} %bitcast.17, f32[1,33]{1,0:T(1,128)S(1)} %maximum_bitcast_fusion.row_ref), custom_call_target="tpu_custom_call" | custom-call | flops 1000000 | bytes 200000 | tf_op jit(solution)/shard_map/pallas_call | solution.py:307
  29.9 0.8 %collective-permute-done.6 = bf16[16,1024]{1,0:T(8,128)(2,1)S(1)} collective-permute-done((bf16[16,1024]{1,0:T(8,128)(2,1)S(1)}, bf16[16,1024]{1,0:T(8,128)(2,1)S(1)}, u32[]{:S(2)}, u32[]{:S(2)}) %collective-permute-start.6) | collective-permute-done | bytes 32800 | tf_op jit(solution)/shard_map/ppermute | solution.py:242
  30.7 0.0 collective-permute-done.5
  30.7 0.2 collective-permute-done.4
  31.0 0.2 collective-permute-start.7
  31.2 1.1 %collective-permute-done.7.other_ref = f32[16,1024]{1,0:T(8,128)S(1)} collective-permute-done((f32[16,1024]{1,0:T(8,128)S(1)}, f32[16,1024]{1,0:T(8,128)S(1)}, u32[]{:S(2)}, u32[]{:S(2)}) %collective-permute-start.7) | collective-permute-done | bytes 65568 | tf_op jit(solution)/shard_map/ppermute | solution.py:242
  32.3 0.8 %shard_map.114 = (f32[3,3,32,64]{3,2,1,0:T(8,128)}, f32[1,32]{1,0:T(1,128)}, f32[3,3,32,32]{3,2,1,0:T(8,128)}, f32[32,64]{1,0:T(8,128)}) custom-call(f32[16,1024]{1,0:T(8,128)S(1)} %add_add_fusion.mine_ref, f32[16,1024]{1,0:T(8,128)S(1)} %collective-permute-done.7.other_ref), custom_call_target="tpu_custom_call" | custom-call | flops 1000000 | bytes 200000 | tf_op jit(solution)/shard_map/pallas_call | solution.py:318
  (3 shorter events, 0.0 us)
Async XLA Ops:
  0.6 9.6 %copy-start = (bf16[3,3,32,32]{3,2,1,0:T(8,128)(2,1)S(1)}, bf16[3,3,32,32]{3,2,1,0:T(8,128)(2,1)}, u32[]{:S(2)}) copy-start(bf16[3,3,32,32]{3,2,1,0:T(8,128)(2,1)} %ws_ref.3) | copy-start | bytes 55300
  0.6 0.8 %copy-start.3 = (bf16[1,64,1,128]{3,1,2,0:T(8,128)(2,1)S(1)}, bf16[1,64,1,128]{3,1,2,0:T(8,128)(2,1)}, u32[]{:S(2)}) copy-start(bf16[1,64,1,128]{3,1,2,0:T(8,128)(2,1)} %param.7) | copy-start | bytes 49156
  2.2 13.9 %all-to-all-start = ((bf16[8,16,128]{2,1,0:T(8,128)(2,1)}), bf16[8,16,128]{2,1,0:T(8,128)(2,1)S(1)}, u32[]{:S(2)}, u32[]{:S(2)}) async-start(bf16[8,16,128]{2,1,0:T(8,128)(2,1)} %shard_map.110), calls=%async_computation | async-start | bytes 65536 | tf_op jit(solution)/shard_map/all_to_all | solution.py:283
  9.5 0.7 %copy-start.5 = (f32[32]{0:T(128)S(1)}, f32[32]{0:T(128)}, u32[]{:S(2)}) copy-start(f32[32]{0:T(128)} %param.9) | copy-start | bytes 388
  10.2 0.9 %copy-start.1 = (bf16[1,32,32,16]{2,3,1,0:T(8,128)(2,1)S(1)}, bf16[1,32,32,16]{2,3,1,0:T(8,128)(2,1)}, u32[]{:S(2)}) copy-start(bf16[1,32,32,16]{2,3,1,0:T(8,128)(2,1)} %param.13) | copy-start | bytes 98308
  11.1 5.0 %copy-start.2 = (bf16[3,3,64,32]{2,3,1,0:T(8,128)(2,1)S(1)}, bf16[3,3,64,32]{2,3,1,0:T(8,128)(2,1)}, u32[]{:S(2)}) copy-start(bf16[3,3,64,32]{2,3,1,0:T(8,128)(2,1)} %param.8) | copy-start | bytes 110596
  17.2 1.3 %collective-permute-start = (f32[16,1024]{1,0:T(8,128)S(1)}, f32[16,1024]{1,0:T(8,128)S(1)}, u32[]{:S(2)}, u32[]{:S(2)}) collective-permute-start(f32[16,1024]{1,0:T(8,128)S(1)} %get-tuple-element.26), channel_id=1, source_target_pairs={{0,8},{1,9},{2,10},{3,11},{4,12},{5,13},{6,14},{7,15},{8,0},{9,1},... | collective-permute-start | bytes 196616 | tf_op jit(solution)/shard_map/ppermute | solution.py:242
  18.6 5.1 %collective-permute-start.3 = (bf16[16,1024]{1,0:T(8,128)(2,1)S(1)}, bf16[16,1024]{1,0:T(8,128)(2,1)S(1)}, u32[]{:S(2)}, u32[]{:S(2)}) collective-permute-start(bf16[16,1024]{1,0:T(8,128)(2,1)S(1)} %add_convert_fusion.1), channel_id=1, source_target_pairs={{0,17},{1,16},{2,19},{3,18},{4,21},{5,20},{6,23},{7,22},{8,25},{9,... | collective-permute-start | bytes 98312 | tf_op jit(solution)/shard_map/ppermute | solution.py:242
  20.1 3.6 %collective-permute-start.2 = (bf16[16,1024]{1,0:T(8,128)(2,1)S(1)}, bf16[16,1024]{1,0:T(8,128)(2,1)S(1)}, u32[]{:S(2)}, u32[]{:S(2)}) collective-permute-start(bf16[16,1024]{1,0:T(8,128)(2,1)S(1)} %add_convert_fusion.1), channel_id=1, source_target_pairs={{0,9},{1,8},{2,11},{3,10},{4,13},{5,12},{6,15},{7,14},{8,1},{9,0},... | collective-permute-start | bytes 98312 | tf_op jit(solution)/shard_map/ppermute | solution.py:242
  21.1 3.3 %collective-permute-start.1 = (bf16[16,1024]{1,0:T(8,128)(2,1)S(1)}, bf16[16,1024]{1,0:T(8,128)(2,1)S(1)}, u32[]{:S(2)}, u32[]{:S(2)}) collective-permute-start(bf16[16,1024]{1,0:T(8,128)(2,1)S(1)} %add_convert_fusion.1), channel_id=1, source_target_pairs={{0,24},{1,25},{2,26},{3,27},{4,28},{5,29},{6,30},{7,31},{8,16},{9,... | collective-permute-start | bytes 98312 | tf_op jit(solution)/shard_map/ppermute | solution.py:242
  24.4 4.2 %copy-start.4 = (bf16[64,32]{0,1:T(8,128)(2,1)S(1)}, bf16[64,32]{0,1:T(8,128)(2,1)}, u32[]{:S(2)}) copy-start(bf16[64,32]{0,1:T(8,128)(2,1)} %param.11) | copy-start | bytes 12292
  24.5 6.2 %collective-permute-start.6 = (bf16[16,1024]{1,0:T(8,128)(2,1)S(1)}, bf16[16,1024]{1,0:T(8,128)(2,1)S(1)}, u32[]{:S(2)}, u32[]{:S(2)}) collective-permute-start(bf16[16,1024]{1,0:T(8,128)(2,1)S(1)} %add_convert_fusion), channel_id=1, source_target_pairs={{0,6},{1,7},{2,4},{3,5},{4,2},{5,3},{6,0},{7,1},{8,14},{9,15},{10,... | collective-permute-start | bytes 98312 | tf_op jit(solution)/shard_map/ppermute | solution.py:242
  25.1 5.6 %collective-permute-start.5 = (bf16[16,1024]{1,0:T(8,128)(2,1)S(1)}, bf16[16,1024]{1,0:T(8,128)(2,1)S(1)}, u32[]{:S(2)}, u32[]{:S(2)}) collective-permute-start(bf16[16,1024]{1,0:T(8,128)(2,1)S(1)} %add_convert_fusion), channel_id=1, source_target_pairs={{0,12},{1,13},{2,14},{3,15},{4,8},{5,9},{6,10},{7,11},{8,4},{9,5},... | collective-permute-start | bytes 98312 | tf_op jit(solution)/shard_map/ppermute | solution.py:242
  26.3 4.6 %collective-permute-start.4 = (bf16[16,1024]{1,0:T(8,128)(2,1)S(1)}, bf16[16,1024]{1,0:T(8,128)(2,1)S(1)}, u32[]{:S(2)}, u32[]{:S(2)}) collective-permute-start(bf16[16,1024]{1,0:T(8,128)(2,1)S(1)} %add_convert_fusion), channel_id=1, source_target_pairs={{0,10},{1,11},{2,8},{3,9},{4,14},{5,15},{6,12},{7,13},{8,2},{9,3},... | collective-permute-start | bytes 98312 | tf_op jit(solution)/shard_map/ppermute | solution.py:242
  31.0 1.3 %collective-permute-start.7 = (f32[16,1024]{1,0:T(8,128)S(1)}, f32[16,1024]{1,0:T(8,128)S(1)}, u32[]{:S(2)}, u32[]{:S(2)}) collective-permute-start(f32[16,1024]{1,0:T(8,128)S(1)} %add_add_fusion.mine_ref), channel_id=1, source_target_pairs={{0,8},{1,9},{2,10},{3,11},{4,12},{5,13},{6,14},{7,15},{8,0},{9,1},... | collective-permute-start | bytes 196616 | tf_op jit(solution)/shard_map/ppermute | solution.py:242

commit v3 on v2

--- a/solution.py
+++ b/solution.py
@@ -40,19 +40,23 @@
         self.window = self.own_coarse + 4
         self.half = self.window // 2
         self.lanes = up128(self.height * self.pitch)
+        self.pair = tiles // 2
+        self.both = 2 * self.lanes
         self.wide = up128(self.lanes + 2 * self.pitch + 2)
 
 
 def pack_kernel(z, coarse_ref, out_ref):
     row = coarse_ref[...]
-    count = z.tiles * ROWS
+    count = z.tiles * 2 * ROWS
     at = ints((count, z.coarse_cols), 0)
     col = ints((count, z.coarse_cols), 1)
-    dest = lax.shift_right_logical(at, 4)
+    dest = lax.shift_right_logical(at, 5)
+    strip = lax.bitwise_and(lax.shift_right_logical(at, 4), 1)
+    tile = lax.bitwise_and(dest, z.pair - 1) + strip * z.pair
     slot = lax.bitwise_and(at, ROWS - 1)
     parts = []
     for half in range(2):
-        want = dest * z.own_coarse - 2 + half * z.half + slot
+        want = tile * z.own_coarse - 2 + half * z.half + slot
         want = jnp.clip(want, 0, z.coarse_cols - 1)
         pick = jnp.where((want == col) & (slot < z.half), 1.0, 0.0).astype(BF16)
         parts.append(lax.dot_general(pick, row, NT, preferred_element_type=F32))
@@ -60,13 +64,18 @@
     out_ref[...] = packed.reshape(out_ref.shape)
 
 
-def interpolation(z, position, interp_ref):
+def strips(z):
+    position = lax.axis_index("tile")
+    low = lax.bitwise_and(position, z.pair - 1)
+    return (low, low + z.pair), position < z.pair
+
+
+def interpolation(z, interp_ref):
     n = ints((ROWS, z.wide), 1) - 1
     slot = ints((ROWS, z.wide), 0)
     h = quotient(n + z.pitch, z.pitch) - 2
     w = n - (h + 1) * z.pitch
-    column = position * z.width + w - 2
-    inside = (h >= 0) & (h < z.height) & (column >= 0) & (column < z.width * z.tiles)
+    inside = (h >= 0) & (h < z.height)
     w_main = lax.shift_right_logical(w, 1) + 1
     w_other = w_main - 1 + 2 * lax.bitwise_and(w, 1)
     h_main = lax.shift_right_arithmetic(h, 1)
@@ -89,35 +98,37 @@
 
 
 def prepare_kernel(
-    z, scale, cot_ref, ws_ref, row_ref, d_hidden_ref, spread_ref, dskip_ref, interp_ref, bias_ref,
-    tall_ref, flat_ref,
+    z, scale, cot_ref, other_ref, ws_ref, row_ref,
+    d_hidden_ref, spread_ref, dskip_ref, interp_ref, bias_ref, tall_ref, flat_ref,
 ):
     blend = row_ref[:, z.cout :]
-    interpolation(z, lax.axis_index("tile"), interp_ref)
+    interpolation(z, interp_ref)
     diagonal = ints((z.cout, z.cout), 0) == ints((z.cout, z.cout), 1)
     bias_ref[...] = jnp.sum(jnp.where(diagonal, row_ref[:, : z.cout], 0.0), axis=1, keepdims=True)
+    lower = strips(z)[1]
+    own, other = cot_ref[...].astype(F32), other_ref[...].astype(F32)
+    count = z.cout * z.height
+    tall_ref[:count, : z.width] = jnp.where(lower, own, other).reshape(count, z.width)
+    tall_ref[count:, : z.width] = jnp.where(lower, other, own).reshape(count, z.width)
+    back = jnp.concatenate([ws_ref[p, q] for p in range(3) for q in range(3)], axis=1)
     flat_ref[...] = jnp.zeros(flat_ref.shape, F32)
-    tall_ref[:, : z.width] = cot_ref[...].astype(F32).reshape(z.cout * z.height, z.width)
-    for h in range(z.height):
-        piece = tall_ref[pl.ds(h, z.cout, stride=z.height), :]
-        start = (h + 1) * z.pitch + 3
-        flat_ref[:, start : start + z.width] = piece[:, : z.width]
-    flat = flat_ref[...]
-    d_second = (flat * (blend * scale)).astype(BF16).astype(F32)
-    dskip_ref[...] = pltpu.roll(flat * ((1.0 - blend) * scale), z.wide - (z.pitch + 1), 1)[
-        :, : z.lanes
-    ].astype(BF16)
-    back = []
-    for p in range(3):
-        for q in range(3):
-            start = (2 - q) * z.pitch + 2 - p
-            moved = d_second if start == 0 else pltpu.roll(d_second, z.wide - start, 1)
-            k = (p * 3 + q) * z.cout
-            spread_ref[k : k + z.cout, :] = moved[:, : z.lanes].astype(BF16)
-            back.append(ws_ref[p, q])
-    d_hidden_ref[...] = jnp.dot(
-        jnp.concatenate(back, axis=1), spread_ref[...], preferred_element_type=F32
-    )
+    for s in range(2):
+        lanes = slice(s * z.lanes, (s + 1) * z.lanes)
+        for h in range(z.height):
+            piece = tall_ref[pl.ds(s * count + h, z.cout, stride=z.height), :]
+            start = (h + 1) * z.pitch + 3
+            flat_ref[:, start : start + z.width] = piece[:, : z.width]
+        flat = flat_ref[...]
+        d_second = (flat * (blend * scale)).astype(BF16).astype(F32)
+        d_skip = pltpu.roll(flat * ((1.0 - blend) * scale), z.wide - (z.pitch + 1), 1)
+        dskip_ref[:, lanes] = d_skip[:, : z.lanes].astype(BF16)
+        for p in range(3):
+            for q in range(3):
+                start = (2 - q) * z.pitch + 2 - p
+                moved = d_second if start == 0 else pltpu.roll(d_second, z.wide - start, 1)
+                k = (p * 3 + q) * z.cout
+                spread_ref[k : k + z.cout, lanes] = moved[:, : z.lanes].astype(BF16)
+    d_hidden_ref[...] = jnp.dot(back, spread_ref[...], preferred_element_type=F32)
 
 
 def holds_top(z):
@@ -135,37 +146,47 @@
     z, got_ref, d_hidden_ref, spread_ref, dskip_ref, wf_ref, bias_ref, interp_ref,
     keep_ref, give_ref, up_ref, hidden_ref, taps_ref,
 ):
-    position = lax.axis_index("tile")
-    turned = got_ref[...].reshape(z.coarse_rows * ROWS, 2 * z.cin).T
-    both = jnp.concatenate([turned[: z.cin], turned[z.cin :]], axis=1)
-    up = jnp.dot(both, interp_ref[...], preferred_element_type=F32).astype(BF16)
-    up32 = up.astype(F32)
-    for p in range(3):
-        for q in range(3):
-            start = q * z.pitch + p
-            moved = up32 if start == 0 else pltpu.roll(up32, z.wide - start, 1)
-            k = (p * 3 + q) * z.cin
-            taps_ref[k : k + z.cin, :] = moved[:, : z.lanes].astype(BF16)
+    tiles, lower = strips(z)
+    n = ints((1, z.wide), 1) - 1
+    w = n - (quotient(n + z.pitch, z.pitch) - 1) * z.pitch - 2
+    m = ints((1, z.lanes), 1)
+    mh = quotient(m, z.pitch)
+    mw = m - mh * z.pitch - 2
+    wanted = []
+    for s in range(2):
+        turned = got_ref[:, s * ROWS : (s + 1) * ROWS, :]
+        turned = turned.reshape(z.coarse_rows * ROWS, 2 * z.cin).T
+        windows = jnp.concatenate([turned[: z.cin], turned[z.cin :]], axis=1)
+        up = jnp.dot(windows, interp_ref[...], preferred_element_type=F32)
+        column = tiles[s] * z.width + w
+        inside = jnp.where((column >= 0) & (column < z.width * z.tiles), 1.0, 0.0)
+        up = (up * inside).astype(BF16).astype(F32)
+        for p in range(3):
+            for q in range(3):
+                start = q * z.pitch + p
+                moved = up if start == 0 else pltpu.roll(up, z.wide - start, 1)
+                k = (p * 3 + q) * z.cin
+                lanes = slice(s * z.lanes, (s + 1) * z.lanes)
+                taps_ref[k : k + z.cin, lanes] = moved[:, : z.lanes].astype(BF16)
+        column = tiles[s] * z.width + mw
+        inside = (mw >= -1) & (mw <= z.width) & (mh < z.height)
+        inside = inside & (column >= 0) & (column < z.width * z.tiles)
+        wanted.append(jnp.where(inside, 1.0, 0.0))
+    inside = jnp.concatenate(wanted, axis=1)
     taps = taps_ref[...]
     centre = taps_ref[4 * z.cin : 5 * z.cin, :]
-    up_ref[...] = centre
+    up_ref[...] = jnp.where(lower, centre[:, : z.lanes], centre[:, z.lanes :])
     kernel = jnp.concatenate([wf_ref[p, q] for p in range(3) for q in range(3)], axis=1)
     pre = jnp.dot(kernel, taps, preferred_element_type=F32) + bias_ref[...]
     sigma = 1.0 / (1.0 + jnp.exp(-pre))
-    m = ints((z.cout, z.lanes), 1)
-    mh = quotient(m, z.pitch)
-    mw = m - mh * z.pitch
-    column = position * z.width + mw - 2
-    inside = (mw >= 1) & (mw <= z.width + 2) & (mh < z.height)
-    inside = inside & (column >= 0) & (column < z.width * z.tiles)
-    hidden = jnp.where(inside, pre * sigma, 0.0).astype(BF16)
-    hidden_ref[...] = hidden
+    hidden = (pre * sigma * inside).astype(BF16)
+    hidden_ref[...] = jnp.where(lower, hidden[:, : z.lanes], hidden[:, z.lanes :])
     slope = sigma * (1.0 + pre * (1.0 - sigma))
-    d_pre = jnp.where(inside, d_hidden_ref[...] * slope, 0.0).astype(BF16)
+    d_pre = (d_hidden_ref[...] * slope * inside).astype(BF16)
     first = lax.dot_general(d_pre, taps, NT, preferred_element_type=F32)
     second = lax.dot_general(hidden, spread_ref[...], NT, preferred_element_type=F32)
     skip = lax.dot_general(dskip_ref[...], centre, NT, preferred_element_type=F32)
-    ones = jnp.ones((z.cout, z.lanes), BF16)
+    ones = jnp.ones((z.cout, z.both), BF16)
     biases = lax.dot_general(ones, d_pre, NT, preferred_element_type=F32)
     full = keep_ref.shape[1]
     used = 10 * z.cin + 10 * z.cout
@@ -249,7 +270,7 @@
         bits.append((k, 0))
         k *= 2
     k = 1
-    while k < tiles:
+    while k < tiles // 2:
         bits.append((0, k))
         k *= 2
     for at in range(0, len(bits), 2):
@@ -277,23 +298,24 @@
     cot = jnp.transpose(cotangent[0], (0, 2, 1))
     wf = jnp.transpose(w_first, (0, 1, 3, 2))
     row = jnp.concatenate([b_first, fade_alpha]).reshape(1, z.cout + 1)
+    other_cot = swap(cot, images, tiles, (0, z.pair))
     packed = call(
-        functools.partial(pack_kernel, z), bf(tiles, ROWS, 2 * z.cin), [vmem]
+        functools.partial(pack_kernel, z), bf(tiles, 2 * ROWS, 2 * z.cin), [vmem]
     )(coarse.reshape(z.cin, z.coarse_cols))
     got = lax.all_to_all(packed, "tile", split_axis=0, concat_axis=0, tiled=True)
 
     d_hidden, spread, dskip, interp, bias = call(
         functools.partial(prepare_kernel, z, scale),
         (
-            f32(z.cout, z.lanes),
-            bf(9 * z.cout, z.lanes),
-            bf(z.cout, z.lanes),
+            f32(z.cout, z.both),
+            bf(9 * z.cout, z.both),
+            bf(z.cout, z.both),
             bf(2 * z.coarse_rows * ROWS, z.wide),
             f32(z.cout, 1),
         ),
-        [vmem] * 3,
-        [pltpu.VMEM((z.cout * z.height, 128), F32), pltpu.VMEM((z.cout, z.wide), F32)],
-    )(cot, w_second, row)
+        [vmem] * 4,
+        [pltpu.VMEM((2 * z.cout * z.height, 128), F32), pltpu.VMEM((z.cout, z.wide), F32)],
+    )(cot, other_cot, w_second, row)
 
     columns = up128(10 * z.cin + 10 * z.cout)
     half = z.cout // 2
@@ -301,7 +323,7 @@
         functools.partial(main_kernel, z),
         (f32(half, columns), f32(half, columns), bf(z.cin, z.lanes), bf(z.cout, z.lanes)),
         [vmem] * 7,
-        [pltpu.VMEM((9 * z.cin, z.lanes), BF16)],
+        [pltpu.VMEM((9 * z.cin, z.both), BF16)],
     )(got, d_hidden, spread, dskip, wf, bias, interp)
 
     blended = call(

time: 33.4 us -> 36 us (1.078)
  waiting for transfers between devices: 10.4 us -> 13 us
  Pallas kernels: 4.59 us -> 5.54 us
  starting transfers between devices: 15 us -> 14.2 us
    ppermute x8 -> x7, waiting for transfers between devices: 6.01 us -> 13 us  [swap(): return lax.ppermute(values, ('img', 'tile'), pairs)]
    all_to_all x1, waiting for transfers between devices: 4.36 us -> 0.01 us  [local(): lax.all_to_all(packed, 'tile', split_axis=0, concat_axis=0, tiled=True)]
    ppermute x8 -> x7, starting transfers between devices: 7.73 us -> 6.81 us  [swap(): return lax.ppermute(values, ('img', 'tile'), pairs)]
    pallas_call x1, Pallas kernels: 1.05 us -> 1.63 us  [local(): call(functools.partial(main_kernel, z), (f32(half, columns), f32(half, co...]
    pallas_call x2, Pallas kernels: 1.48 us -> 1.86 us  [the longest x1 0.96 us: local(): call(functools.partial(prepare_kernel, z, scale), (f32(z.cout, z.both), b...]
  transfers between devices with their start and end apart: 9 -> 8, of which waited for: 7 -> 6; matrix products, arithmetic and copies ran while one was open for 0% -> 0% of each run, Pallas kernels for 6% -> 6%
where the time goes in v3:
time: 36 us; the launch traced here: 35.6 us
  starting transfers between devices  14.2 us (39%)
  waiting for transfers between devices  13 us (36%)
  Pallas kernels  5.54 us (15%)
  between operations  1.37 us (4%)
  local copies, waits for them, and re-layouts  1.36 us (4%)
    ppermute x7, waiting for transfers between devices, swap(): return lax.ppermute(values, ('img', 'tile'), pairs)  13 us
    all_to_all x1, starting transfers between devices, local(): lax.all_to_all(packed, 'tile', split_axis=0, concat_axis=0, tiled=True)  7.38 us
    ppermute x7, starting transfers between devices, swap(): return lax.ppermute(values, ('img', 'tile'), pairs)  6.81 us
    pallas_call x1, Pallas kernels, local(): call(functools.partial(main_kernel, z), (f32(half, columns), f32(half, co...  1.63 us
    unnamed x12, local copies, waits for them, and re-layouts  1.36 us
    pallas_call x1, Pallas kernels, local(): call(functools.partial(blend_kernel, z), bf(z.cout, z.height, z.width), [...  1.24 us
    pallas_call x1, Pallas kernels, local(): call(functools.partial(prepare_kernel, z, scale), (f32(z.cout, z.both), b...  0.96 us
    pallas_call x1, Pallas kernels, local(): call(functools.partial(pack_kernel, z), bf(tiles, 2 * ROWS, 2 * z.cin), [...  0.9 us
  transfers between devices with their start and end apart: 8, of which 6 were waited for; matrix products, arithmetic and copies ran while one was open for 0% of the time, Pallas kernels for 6%

profile of v3, /device:TPU:0, one launch (start us, length us, event | category | flops | bytes accessed | tf_op | source)
XLA Modules:
  0.0 35.6 jit_solution(15895744409966723681)
XLA Ops:
  0.6 0.0 copy-start.1
  0.6 0.0 copy-start.3
  0.7 0.7 %copy-done.3 = bf16[1,64,1,128]{3,1,2,0:T(8,128)(2,1)S(1)} copy-done((bf16[1,64,1,128]{3,1,2,0:T(8,128)(2,1)S(1)}, bf16[1,64,1,128]{3,1,2,0:T(8,128)(2,1)}, u32[]{:S(2)}) %copy-start.3) | copy-done | bytes 16408
  1.4 0.9 %shard_map.110 = bf16[8,32,128]{2,1,0:T(8,128)(2,1)} custom-call(bf16[64,128]{1,0:T(8,128)(2,1)S(1)} %bitcast.17), custom_call_target="tpu_custom_call" | custom-call | flops 1000000 | bytes 200000 | tf_op jit(solution)/shard_map/pallas_call | solution.py:302
  2.3 0.0 copy-start
  2.3 7.4 %all-to-all-start = ((bf16[8,32,128]{2,1,0:T(8,128)(2,1)}), bf16[8,32,128]{2,1,0:T(8,128)(2,1)S(1)}, u32[]{:S(2)}, u32[]{:S(2)}) async-start(bf16[8,32,128]{2,1,0:T(8,128)(2,1)} %shard_map.110), calls=%async_computation | async-start | bytes 131072 | tf_op jit(solution)/shard_map/all_to_all | solution.py:305
  9.7 0.0 copy-done.1
  9.7 0.0 copy-start.5
  9.7 3.0 %collective-permute-start = (bf16[32,16,32]{2,1,0:T(8,128)(2,1)S(1)}, bf16[32,16,32]{2,1,0:T(8,128)(2,1)S(1)}, u32[]{:S(2)}, u32[]{:S(2)}) collective-permute-start(bf16[32,16,32]{2,1,0:T(8,128)(2,1)S(1)} %bitcast.14), channel_id=1, source_target_pairs={{0,4},{1,5},{2,6},{3,7},{4,0},{5,1},{6,2},{7,3},{8,12},{9,13},{10,... | collective-permute-start | bytes 98312 | tf_op jit(solution)/shard_map/ppermute | solution.py:263
  13.3 0.0 copy-done.5
  13.3 0.1 maximum_bitcast_fusion.row_ref
  13.4 0.0 copy-start.2
  13.4 6.5 %collective-permute-done.other_ref = bf16[32,16,32]{2,1,0:T(8,128)(2,1)S(1)} collective-permute-done((bf16[32,16,32]{2,1,0:T(8,128)(2,1)S(1)}, bf16[32,16,32]{2,1,0:T(8,128)(2,1)S(1)}, u32[]{:S(2)}, u32[]{:S(2)}) %collective-permute-start) | collective-permute-done | bytes 32800 | tf_op jit(solution)/shard_map/ppermute | solution.py:263
  20.0 0.0 copy-done
  20.0 1.0 %shard_map.111 = (f32[32,1280]{1,0:T(8,128)S(1)}, bf16[288,1280]{1,0:T(8,128)(2,1)S(1)}, bf16[32,1280]{1,0:T(8,128)(2,1)S(1)}, bf16[256,768]{1,0:T(8,128)(2,1)S(1)}, f32[32,1]{1,0:T(8,128)S(1)}) custom-call(bf16[32,16,32]{2,1,0:T(8,128)(2,1)S(1)} %bitcast.15, bf16[32,16,32]{2,1,0:T(8,128)(2,1)S(1)} %collective-permute-done.other_ref, ...), custom_call_target="tpu_custom_call" | custom-call | flops 1000000 | bytes 200000 | tf_op jit(solution)/shard_map/pallas_call | solution.py:307
  20.9 0.0 all-to-all-done.got_ref
  20.9 0.0 copy-done.2
  20.9 1.6 %shard_map.112 = (f32[16,1024]{1,0:T(8,128)S(1)}, f32[16,1024]{1,0:T(8,128)S(1)}, bf16[64,640]{1,0:T(8,128)(2,1)S(1)}, bf16[32,640]{1,0:T(8,128)(2,1)S(1)}) custom-call(bf16[8,32,128]{2,1,0:T(8,128)(2,1)S(1)} %all-to-all-done.got_ref, f32[32,1280]{1,0:T(8,128)S(1)} %get-tuple-element.20.d_hidden_ref, bf16[288,1280]{1,0:T(8,128)(2,1)S(1)} %get-tuple-element.21.spread_ref, ...), custom_call_target="tpu_custom_call" | custom-call | flops 1000000 | bytes 200000 | tf_op jit(solution)/shard_map/pallas_call | solution.py:322
  22.6 0.1 collective-permute-start.1
  22.7 1.2 %collective-permute-done.1 = f32[16,1024]{1,0:T(8,128)S(1)} collective-permute-done((f32[16,1024]{1,0:T(8,128)S(1)}, f32[16,1024]{1,0:T(8,128)S(1)}, u32[]{:S(2)}, u32[]{:S(2)}) %collective-permute-start.1) | collective-permute-done | bytes 65568 | tf_op jit(solution)/shard_map/ppermute | solution.py:263
  23.9 2.5 %collective-permute-start.4 = (bf16[16,1024]{1,0:T(8,128)(2,1)S(1)}, bf16[16,1024]{1,0:T(8,128)(2,1)S(1)}, u32[]{:S(2)}, u32[]{:S(2)}) collective-permute-start(bf16[16,1024]{1,0:T(8,128)(2,1)S(1)} %add_convert_fusion.1), channel_id=1, source_target_pairs={{0,17},{1,16},{2,19},{3,18},{4,21},{5,20},{6,23},{7,22},{8,25},{9,... | collective-permute-start | bytes 98312 | tf_op jit(solution)/shard_map/ppermute | solution.py:263
  26.4 0.0 collective-permute-start.3
  26.4 0.7 %collective-permute-start.2 = (bf16[16,1024]{1,0:T(8,128)(2,1)S(1)}, bf16[16,1024]{1,0:T(8,128)(2,1)S(1)}, u32[]{:S(2)}, u32[]{:S(2)}) collective-permute-start(bf16[16,1024]{1,0:T(8,128)(2,1)S(1)} %add_convert_fusion.1), channel_id=1, source_target_pairs={{0,24},{1,25},{2,26},{3,27},{4,28},{5,29},{6,30},{7,31},{8,16},{9,... | collective-permute-start | bytes 98312 | tf_op jit(solution)/shard_map/ppermute | solution.py:263
  27.2 1.6 %collective-permute-done.4 = bf16[16,1024]{1,0:T(8,128)(2,1)S(1)} collective-permute-done((bf16[16,1024]{1,0:T(8,128)(2,1)S(1)}, bf16[16,1024]{1,0:T(8,128)(2,1)S(1)}, u32[]{:S(2)}, u32[]{:S(2)}) %collective-permute-start.4) | collective-permute-done | bytes 32800 | tf_op jit(solution)/shard_map/ppermute | solution.py:263
  28.8 1.2 %collective-permute-done.3 = bf16[16,1024]{1,0:T(8,128)(2,1)S(1)} collective-permute-done((bf16[16,1024]{1,0:T(8,128)(2,1)S(1)}, bf16[16,1024]{1,0:T(8,128)(2,1)S(1)}, u32[]{:S(2)}, u32[]{:S(2)}) %collective-permute-start.3) | collective-permute-done | bytes 32800 | tf_op jit(solution)/shard_map/ppermute | solution.py:263
  30.0 0.0 collective-permute-done.2
  30.0 0.0 copy-start.4
  30.1 0.1 collective-permute-start.5
  30.1 0.6 %copy-done.4 = bf16[64,32]{0,1:T(8,128)(2,1)S(1)} copy-done((bf16[64,32]{0,1:T(8,128)(2,1)S(1)}, bf16[64,32]{0,1:T(8,128)(2,1)}, u32[]{:S(2)}) %copy-start.4) | copy-done | bytes 4120
  30.7 1.2 %shard_map.113 = bf16[32,16,32]{2,1,0:T(8,128)(2,1)} custom-call(bf16[32,640]{1,0:T(8,128)(2,1)S(1)} %get-tuple-element.27.hidden_ref, bf16[64,640]{1,0:T(8,128)(2,1)S(1)} %get-tuple-element.28.up_ref, bf16[3,3,32,32]{3,2,1,0:T(8,128)(2,1)S(1)} %copy-done, bf16[32,64]{1,0:T(8,128)(2,1)S(1)} %bitcast.18, f32[1,33]{1,0:T(1,128)S(1)} %maximum_bitcast_fusion.row_ref), custom_call_target="tpu_custom_call" | custom-call | flops 1000000 | bytes 200000 | tf_op jit(solution)/shard_map/pallas_call | solution.py:329
  32.0 1.5 %collective-permute-done.5 = bf16[16,1024]{1,0:T(8,128)(2,1)S(1)} collective-permute-done((bf16[16,1024]{1,0:T(8,128)(2,1)S(1)}, bf16[16,1024]{1,0:T(8,128)(2,1)S(1)}, u32[]{:S(2)}, u32[]{:S(2)}) %collective-permute-start.5) | collective-permute-done | bytes 32800 | tf_op jit(solution)/shard_map/ppermute | solution.py:263
  33.5 0.4 %collective-permute-start.6 = (f32[16,1024]{1,0:T(8,128)S(1)}, f32[16,1024]{1,0:T(8,128)S(1)}, u32[]{:S(2)}, u32[]{:S(2)}) collective-permute-start(f32[16,1024]{1,0:T(8,128)S(1)} %convert_add_fusion.mine_ref), channel_id=1, source_target_pairs={{0,8},{1,9},{2,10},{3,11},{4,12},{5,13},{6,14},{7,15},{8,0},{9,1},... | collective-permute-start | bytes 196616 | tf_op jit(solution)/shard_map/ppermute | solution.py:263
  33.9 0.9 %collective-permute-done.6.other_ref = f32[16,1024]{1,0:T(8,128)S(1)} collective-permute-done((f32[16,1024]{1,0:T(8,128)S(1)}, f32[16,1024]{1,0:T(8,128)S(1)}, u32[]{:S(2)}, u32[]{:S(2)}) %collective-permute-start.6) | collective-permute-done | bytes 65568 | tf_op jit(solution)/shard_map/ppermute | solution.py:263
  34.8 0.8 %shard_map.114 = (f32[3,3,32,64]{3,2,1,0:T(8,128)}, f32[1,32]{1,0:T(1,128)}, f32[3,3,32,32]{3,2,1,0:T(8,128)}, f32[32,64]{1,0:T(8,128)}) custom-call(f32[16,1024]{1,0:T(8,128)S(1)} %convert_add_fusion.mine_ref, f32[16,1024]{1,0:T(8,128)S(1)} %collective-permute-done.6.other_ref), custom_call_target="tpu_custom_call" | custom-call | flops 1000000 | bytes 200000 | tf_op jit(solution)/shard_map/pallas_call | solution.py:340
  (3 shorter events, 0.0 us)
Async XLA Ops:
  0.6 9.1 %copy-start.1 = (bf16[1,32,32,16]{2,3,1,0:T(8,128)(2,1)S(1)}, bf16[1,32,32,16]{2,3,1,0:T(8,128)(2,1)}, u32[]{:S(2)}) copy-start(bf16[1,32,32,16]{2,3,1,0:T(8,128)(2,1)} %param.13) | copy-start | bytes 98308
  0.6 0.8 %copy-start.3 = (bf16[1,64,1,128]{3,1,2,0:T(8,128)(2,1)S(1)}, bf16[1,64,1,128]{3,1,2,0:T(8,128)(2,1)}, u32[]{:S(2)}) copy-start(bf16[1,64,1,128]{3,1,2,0:T(8,128)(2,1)} %param.7) | copy-start | bytes 49156
  2.3 17.7 %copy-start = (bf16[3,3,32,32]{3,2,1,0:T(8,128)(2,1)S(1)}, bf16[3,3,32,32]{3,2,1,0:T(8,128)(2,1)}, u32[]{:S(2)}) copy-start(bf16[3,3,32,32]{3,2,1,0:T(8,128)(2,1)} %ws_ref.3) | copy-start | bytes 55300
  2.3 18.6 %all-to-all-start = ((bf16[8,32,128]{2,1,0:T(8,128)(2,1)}), bf16[8,32,128]{2,1,0:T(8,128)(2,1)S(1)}, u32[]{:S(2)}, u32[]{:S(2)}) async-start(bf16[8,32,128]{2,1,0:T(8,128)(2,1)} %shard_map.110), calls=%async_computation | async-start | bytes 131072 | tf_op jit(solution)/shard_map/all_to_all | solution.py:305
  9.7 3.6 %copy-start.5 = (f32[32]{0:T(128)S(1)}, f32[32]{0:T(128)}, u32[]{:S(2)}) copy-start(f32[32]{0:T(128)} %param.9) | copy-start | bytes 388
  9.7 10.3 %collective-permute-start = (bf16[32,16,32]{2,1,0:T(8,128)(2,1)S(1)}, bf16[32,16,32]{2,1,0:T(8,128)(2,1)S(1)}, u32[]{:S(2)}, u32[]{:S(2)}) collective-permute-start(bf16[32,16,32]{2,1,0:T(8,128)(2,1)S(1)} %bitcast.14), channel_id=1, source_target_pairs={{0,4},{1,5},{2,6},{3,7},{4,0},{5,1},{6,2},{7,3},{8,12},{9,13},{10,... | collective-permute-start | bytes 98312 | tf_op jit(solution)/shard_map/ppermute | solution.py:263
  13.4 7.5 %copy-start.2 = (bf16[3,3,64,32]{2,3,1,0:T(8,128)(2,1)S(1)}, bf16[3,3,64,32]{2,3,1,0:T(8,128)(2,1)}, u32[]{:S(2)}) copy-start(bf16[3,3,64,32]{2,3,1,0:T(8,128)(2,1)} %param.8) | copy-start | bytes 110596
  22.6 1.3 %collective-permute-start.1 = (f32[16,1024]{1,0:T(8,128)S(1)}, f32[16,1024]{1,0:T(8,128)S(1)}, u32[]{:S(2)}, u32[]{:S(2)}) collective-permute-start(f32[16,1024]{1,0:T(8,128)S(1)} %get-tuple-element.26), channel_id=1, source_target_pairs={{0,8},{1,9},{2,10},{3,11},{4,12},{5,13},{6,14},{7,15},{8,0},{9,1},... | collective-permute-start | bytes 196616 | tf_op jit(solution)/shard_map/ppermute | solution.py:263
  23.9 4.9 %collective-permute-start.4 = (bf16[16,1024]{1,0:T(8,128)(2,1)S(1)}, bf16[16,1024]{1,0:T(8,128)(2,1)S(1)}, u32[]{:S(2)}, u32[]{:S(2)}) collective-permute-start(bf16[16,1024]{1,0:T(8,128)(2,1)S(1)} %add_convert_fusion.1), channel_id=1, source_target_pairs={{0,17},{1,16},{2,19},{3,18},{4,21},{5,20},{6,23},{7,22},{8,25},{9,... | collective-permute-start | bytes 98312 | tf_op jit(solution)/shard_map/ppermute | solution.py:263
  26.4 3.6 %collective-permute-start.3 = (bf16[16,1024]{1,0:T(8,128)(2,1)S(1)}, bf16[16,1024]{1,0:T(8,128)(2,1)S(1)}, u32[]{:S(2)}, u32[]{:S(2)}) collective-permute-start(bf16[16,1024]{1,0:T(8,128)(2,1)S(1)} %add_convert_fusion.1), channel_id=1, source_target_pairs={{0,9},{1,8},{2,11},{3,10},{4,13},{5,12},{6,15},{7,14},{8,1},{9,0},... | collective-permute-start | bytes 98312 | tf_op jit(solution)/shard_map/ppermute | solution.py:263
  26.4 3.6 %collective-permute-start.2 = (bf16[16,1024]{1,0:T(8,128)(2,1)S(1)}, bf16[16,1024]{1,0:T(8,128)(2,1)S(1)}, u32[]{:S(2)}, u32[]{:S(2)}) collective-permute-start(bf16[16,1024]{1,0:T(8,128)(2,1)S(1)} %add_convert_fusion.1), channel_id=1, source_target_pairs={{0,24},{1,25},{2,26},{3,27},{4,28},{5,29},{6,30},{7,31},{8,16},{9,... | collective-permute-start | bytes 98312 | tf_op jit(solution)/shard_map/ppermute | solution.py:263
  30.0 0.7 %copy-start.4 = (bf16[64,32]{0,1:T(8,128)(2,1)S(1)}, bf16[64,32]{0,1:T(8,128)(2,1)}, u32[]{:S(2)}) copy-start(bf16[64,32]{0,1:T(8,128)(2,1)} %param.11) | copy-start | bytes 12292
  30.1 3.4 %collective-permute-start.5 = (bf16[16,1024]{1,0:T(8,128)(2,1)S(1)}, bf16[16,1024]{1,0:T(8,128)(2,1)S(1)}, u32[]{:S(2)}, u32[]{:S(2)}) collective-permute-start(bf16[16,1024]{1,0:T(8,128)(2,1)S(1)} %add_convert_fusion), channel_id=1, source_target_pairs={{0,10},{1,11},{2,8},{3,9},{4,14},{5,15},{6,12},{7,13},{8,2},{9,3},... | collective-permute-start | bytes 98312 | tf_op jit(solution)/shard_map/ppermute | solution.py:263
  33.5 1.3 %collective-permute-start.6 = (f32[16,1024]{1,0:T(8,128)S(1)}, f32[16,1024]{1,0:T(8,128)S(1)}, u32[]{:S(2)}, u32[]{:S(2)}) collective-permute-start(f32[16,1024]{1,0:T(8,128)S(1)} %convert_add_fusion.mine_ref), channel_id=1, source_target_pairs={{0,8},{1,9},{2,10},{3,11},{4,12},{5,13},{6,14},{7,15},{8,0},{9,1},... | collective-permute-start | bytes 196616 | tf_op jit(solution)/shard_map/ppermute | solution.py:263

commit v4 on v3

--- a/solution.py
+++ b/solution.py
@@ -41,7 +41,6 @@
         self.half = self.window // 2
         self.lanes = up128(self.height * self.pitch)
         self.pair = tiles // 2
-        self.both = 2 * self.lanes
         self.wide = up128(self.lanes + 2 * self.pitch + 2)
 
 
@@ -52,7 +51,7 @@
     col = ints((count, z.coarse_cols), 1)
     dest = lax.shift_right_logical(at, 5)
     strip = lax.bitwise_and(lax.shift_right_logical(at, 4), 1)
-    tile = lax.bitwise_and(dest, z.pair - 1) + strip * z.pair
+    tile = dest ^ (strip * z.pair)
     slot = lax.bitwise_and(at, ROWS - 1)
     parts = []
     for half in range(2):
@@ -62,12 +61,6 @@
         parts.append(lax.dot_general(pick, row, NT, preferred_element_type=F32))
     packed = jnp.concatenate(parts, axis=1).astype(BF16)
     out_ref[...] = packed.reshape(out_ref.shape)
-
-
-def strips(z):
-    position = lax.axis_index("tile")
-    low = lax.bitwise_and(position, z.pair - 1)
-    return (low, low + z.pair), position < z.pair
 
 
 def interpolation(z, interp_ref):
@@ -97,38 +90,45 @@
     lax.fori_loop(0, z.coarse_rows, one_row, 0, unroll=z.coarse_rows <= 8)
 
 
+def flatten_kernel(z, cot_ref, flat_ref, tall_ref, wide_ref):
+    tall_ref[:, : z.width] = cot_ref[...].astype(F32).reshape(z.cout * z.height, z.width)
+    wide_ref[...] = jnp.zeros(wide_ref.shape, F32)
+    for h in range(z.height):
+        piece = tall_ref[pl.ds(h, z.cout, stride=z.height), :]
+        start = h * z.pitch + 2
+        wide_ref[:, start : start + z.width] = piece[:, : z.width]
+    flat_ref[...] = wide_ref[...].astype(BF16)
+
+
+def backward(z, scale, flat_ref, ws_ref, row_ref, spread_ref):
+    blend = row_ref[:, z.cout :]
+    flat = flat_ref[...].astype(F32)
+    d_skip = (flat * ((1.0 - blend) * scale)).astype(BF16)
+    d_second = (flat * (blend * scale)).astype(BF16).astype(F32)
+    d_second = jnp.concatenate([d_second, jnp.zeros((z.cout, z.wide - z.lanes), F32)], axis=1)
+    back = []
+    for p in range(3):
+        for q in range(3):
+            shift = (q - 1) * z.pitch + p - 1
+            moved = d_second if shift == 0 else pltpu.roll(d_second, shift % z.wide, 1)
+            k = (p * 3 + q) * z.cout
+            spread_ref[k : k + z.cout, :] = moved[:, : z.lanes].astype(BF16)
+            back.append(ws_ref[p, q])
+    d_hidden = jnp.dot(
+        jnp.concatenate(back, axis=1), spread_ref[...], preferred_element_type=F32
+    )
+    return d_skip, d_hidden
+
+
 def prepare_kernel(
-    z, scale, cot_ref, other_ref, ws_ref, row_ref,
-    d_hidden_ref, spread_ref, dskip_ref, interp_ref, bias_ref, tall_ref, flat_ref,
+    z, scale, flat_ref, ws_ref, row_ref, d_hidden_ref, spread_ref, dskip_ref, interp_ref, bias_ref
 ):
-    blend = row_ref[:, z.cout :]
     interpolation(z, interp_ref)
     diagonal = ints((z.cout, z.cout), 0) == ints((z.cout, z.cout), 1)
     bias_ref[...] = jnp.sum(jnp.where(diagonal, row_ref[:, : z.cout], 0.0), axis=1, keepdims=True)
-    lower = strips(z)[1]
-    own, other = cot_ref[...].astype(F32), other_ref[...].astype(F32)
-    count = z.cout * z.height
-    tall_ref[:count, : z.width] = jnp.where(lower, own, other).reshape(count, z.width)
-    tall_ref[count:, : z.width] = jnp.where(lower, other, own).reshape(count, z.width)
-    back = jnp.concatenate([ws_ref[p, q] for p in range(3) for q in range(3)], axis=1)
-    flat_ref[...] = jnp.zeros(flat_ref.shape, F32)
-    for s in range(2):
-        lanes = slice(s * z.lanes, (s + 1) * z.lanes)
-        for h in range(z.height):
-            piece = tall_ref[pl.ds(s * count + h, z.cout, stride=z.height), :]
-            start = (h + 1) * z.pitch + 3
-            flat_ref[:, start : start + z.width] = piece[:, : z.width]
-        flat = flat_ref[...]
-        d_second = (flat * (blend * scale)).astype(BF16).astype(F32)
-        d_skip = pltpu.roll(flat * ((1.0 - blend) * scale), z.wide - (z.pitch + 1), 1)
-        dskip_ref[:, lanes] = d_skip[:, : z.lanes].astype(BF16)
-        for p in range(3):
-            for q in range(3):
-                start = (2 - q) * z.pitch + 2 - p
-                moved = d_second if start == 0 else pltpu.roll(d_second, z.wide - start, 1)
-                k = (p * 3 + q) * z.cout
-                spread_ref[k : k + z.cout, lanes] = moved[:, : z.lanes].astype(BF16)
-    d_hidden_ref[...] = jnp.dot(back, spread_ref[...], preferred_element_type=F32)
+    d_skip, d_hidden = backward(z, scale, flat_ref, ws_ref, row_ref, spread_ref)
+    dskip_ref[...] = d_skip
+    d_hidden_ref[...] = d_hidden
 
 
 def holds_top(z):
@@ -142,23 +142,34 @@
     return bits == 0
 
 
-def main_kernel(
+def gradients(z, d_hidden, d_skip, spread, slope, hidden, taps, centre):
+    d_pre = (d_hidden * slope).astype(BF16)
+    first = lax.dot_general(d_pre, taps, NT, preferred_element_type=F32)
+    second = lax.dot_general(hidden, spread, NT, preferred_element_type=F32)
+    skip = lax.dot_general(d_skip, centre, NT, preferred_element_type=F32)
+    ones = jnp.ones((z.cout, z.lanes), BF16)
+    biases = lax.dot_general(ones, d_pre, NT, preferred_element_type=F32)
+    return jnp.concatenate([first, second, skip, biases], axis=1)
+
+
+def forward_kernel(
     z, got_ref, d_hidden_ref, spread_ref, dskip_ref, wf_ref, bias_ref, interp_ref,
-    keep_ref, give_ref, up_ref, hidden_ref, taps_ref,
+    sums_ref, up_ref, hidden_ref, other_taps_ref, other_hidden_ref, other_slope_ref, taps_ref,
 ):
-    tiles, lower = strips(z)
+    position = lax.axis_index("tile")
     n = ints((1, z.wide), 1) - 1
     w = n - (quotient(n + z.pitch, z.pitch) - 1) * z.pitch - 2
     m = ints((1, z.lanes), 1)
     mh = quotient(m, z.pitch)
     mw = m - mh * z.pitch - 2
-    wanted = []
-    for s in range(2):
+    kernel = jnp.concatenate([wf_ref[p, q] for p in range(3) for q in range(3)], axis=1)
+    for s, here_ref in enumerate((taps_ref, other_taps_ref)):
+        tile = position ^ (s * z.pair)
         turned = got_ref[:, s * ROWS : (s + 1) * ROWS, :]
         turned = turned.reshape(z.coarse_rows * ROWS, 2 * z.cin).T
         windows = jnp.concatenate([turned[: z.cin], turned[z.cin :]], axis=1)
         up = jnp.dot(windows, interp_ref[...], preferred_element_type=F32)
-        column = tiles[s] * z.width + w
+        column = tile * z.width + w
         inside = jnp.where((column >= 0) & (column < z.width * z.tiles), 1.0, 0.0)
         up = (up * inside).astype(BF16).astype(F32)
         for p in range(3):
@@ -166,34 +177,40 @@
                 start = q * z.pitch + p
                 moved = up if start == 0 else pltpu.roll(up, z.wide - start, 1)
                 k = (p * 3 + q) * z.cin
-                lanes = slice(s * z.lanes, (s + 1) * z.lanes)
-                taps_ref[k : k + z.cin, lanes] = moved[:, : z.lanes].astype(BF16)
-        column = tiles[s] * z.width + mw
+                here_ref[k : k + z.cin, :] = moved[:, : z.lanes].astype(BF16)
+        column = tile * z.width + mw
         inside = (mw >= -1) & (mw <= z.width) & (mh < z.height)
         inside = inside & (column >= 0) & (column < z.width * z.tiles)
-        wanted.append(jnp.where(inside, 1.0, 0.0))
-    inside = jnp.concatenate(wanted, axis=1)
-    taps = taps_ref[...]
+        inside = jnp.where(inside, 1.0, 0.0)
+        taps = here_ref[...]
+        pre = jnp.dot(kernel, taps, preferred_element_type=F32) + bias_ref[...]
+        sigma = 1.0 / (1.0 + jnp.exp(-pre))
+        hidden = (pre * sigma * inside).astype(BF16)
+        slope = sigma * (1.0 + pre * (1.0 - sigma)) * inside
+        if s == 0:
+            centre = here_ref[4 * z.cin : 5 * z.cin, :]
+            up_ref[...] = centre
+            hidden_ref[...] = hidden
+            sums_ref[...] = gradients(
+                z, d_hidden_ref[...], dskip_ref[...], spread_ref[...], slope, hidden, taps, centre
+            )
+        else:
+            other_hidden_ref[...] = hidden
+            other_slope_ref[...] = slope
+
+
+def other_kernel(
+    z, scale, sums_ref, taps_ref, hidden_ref, slope_ref, flat_ref, ws_ref, row_ref,
+    keep_ref, give_ref, spread_ref,
+):
+    d_skip, d_hidden = backward(z, scale, flat_ref, ws_ref, row_ref, spread_ref)
     centre = taps_ref[4 * z.cin : 5 * z.cin, :]
-    up_ref[...] = jnp.where(lower, centre[:, : z.lanes], centre[:, z.lanes :])
-    kernel = jnp.concatenate([wf_ref[p, q] for p in range(3) for q in range(3)], axis=1)
-    pre = jnp.dot(kernel, taps, preferred_element_type=F32) + bias_ref[...]
-    sigma = 1.0 / (1.0 + jnp.exp(-pre))
-    hidden = (pre * sigma * inside).astype(BF16)
-    hidden_ref[...] = jnp.where(lower, hidden[:, : z.lanes], hidden[:, z.lanes :])
-    slope = sigma * (1.0 + pre * (1.0 - sigma))
-    d_pre = (d_hidden_ref[...] * slope * inside).astype(BF16)
-    first = lax.dot_general(d_pre, taps, NT, preferred_element_type=F32)
-    second = lax.dot_general(hidden, spread_ref[...], NT, preferred_element_type=F32)
-    skip = lax.dot_general(dskip_ref[...], centre, NT, preferred_element_type=F32)
-    ones = jnp.ones((z.cout, z.both), BF16)
-    biases = lax.dot_general(ones, d_pre, NT, preferred_element_type=F32)
-    full = keep_ref.shape[1]
-    used = 10 * z.cin + 10 * z.cout
-    pieces = [first, second, skip, biases]
+    grads = sums_ref[...] + gradients(
+        z, d_hidden, d_skip, spread_ref[...], slope_ref[...], hidden_ref[...], taps_ref[...], centre
+    )
+    full, used = keep_ref.shape[1], grads.shape[1]
     if full > used:
-        pieces.append(jnp.zeros((z.cout, full - used), F32))
-    grads = jnp.concatenate(pieces, axis=1)
+        grads = jnp.concatenate([grads, jnp.zeros((z.cout, full - used), F32)], axis=1)
     half = z.cout // 2
     top = holds_top(z)
     keep_ref[...] = jnp.where(top, grads[:half], grads[half:])
@@ -295,36 +312,53 @@
     total_count = coarse.shape[0] * images * z.width * tiles * z.height
     scale = float(total_count) ** (-0.5)
 
-    cot = jnp.transpose(cotangent[0], (0, 2, 1))
-    wf = jnp.transpose(w_first, (0, 1, 3, 2))
-    row = jnp.concatenate([b_first, fade_alpha]).reshape(1, z.cout + 1)
-    other_cot = swap(cot, images, tiles, (0, z.pair))
     packed = call(
         functools.partial(pack_kernel, z), bf(tiles, 2 * ROWS, 2 * z.cin), [vmem]
     )(coarse.reshape(z.cin, z.coarse_cols))
     got = lax.all_to_all(packed, "tile", split_axis=0, concat_axis=0, tiled=True)
 
+    flat = call(
+        functools.partial(flatten_kernel, z),
+        bf(z.cout, z.lanes),
+        [vmem],
+        [pltpu.VMEM((z.cout * z.height, 128), F32), pltpu.VMEM((z.cout, z.lanes), F32)],
+    )(jnp.transpose(cotangent[0], (0, 2, 1)))
+    other_flat = swap(flat, images, tiles, (0, z.pair))
+    row = jnp.concatenate([b_first, fade_alpha]).reshape(1, z.cout + 1)
     d_hidden, spread, dskip, interp, bias = call(
         functools.partial(prepare_kernel, z, scale),
         (
-            f32(z.cout, z.both),
-            bf(9 * z.cout, z.both),
-            bf(z.cout, z.both),
+            f32(z.cout, z.lanes),
+            bf(9 * z.cout, z.lanes),
+            bf(z.cout, z.lanes),
             bf(2 * z.coarse_rows * ROWS, z.wide),
             f32(z.cout, 1),
         ),
-        [vmem] * 4,
-        [pltpu.VMEM((2 * z.cout * z.height, 128), F32), pltpu.VMEM((z.cout, z.wide), F32)],
-    )(cot, other_cot, w_second, row)
-
-    columns = up128(10 * z.cin + 10 * z.cout)
-    half = z.cout // 2
-    keep, give, up, hidden = call(
-        functools.partial(main_kernel, z),
-        (f32(half, columns), f32(half, columns), bf(z.cin, z.lanes), bf(z.cout, z.lanes)),
+        [vmem] * 3,
+    )(flat, w_second, row)
+
+    used = 10 * z.cin + 10 * z.cout
+    sums, up, hidden, *other = call(
+        functools.partial(forward_kernel, z),
+        (
+            f32(z.cout, used),
+            bf(z.cin, z.lanes),
+            bf(z.cout, z.lanes),
+            bf(9 * z.cin, z.lanes),
+            bf(z.cout, z.lanes),
+            f32(z.cout, z.lanes),
+        ),
         [vmem] * 7,
-        [pltpu.VMEM((9 * z.cin, z.both), BF16)],
-    )(got, d_hidden, spread, dskip, wf, bias, interp)
+        [pltpu.VMEM((9 * z.cin, z.lanes), BF16)],
+    )(got, d_hidden, spread, dskip, jnp.transpose(w_first, (0, 1, 3, 2)), bias, interp)
+
+    half = f32(z.cout // 2, up128(used))
+    keep, give = call(
+        functools.partial(other_kernel, z, scale),
+        (half, half),
+        [vmem] * 7,
+        [pltpu.VMEM((9 * z.cout, z.lanes), BF16)],
+    )(sums, *other, other_flat, w_second, row)
 
     blended = call(
         functools.partial(blend_kernel, z),

time: 36 us -> 32.2 us (0.89)
  waiting for transfers between devices: 13 us -> 8.75 us
  starting transfers between devices: 14.2 us -> 14.8 us
  local copies, waits for them, and re-layouts: 1.36 us -> 0.93 us
    ppermute x7, waiting for transfers between devices: 13 us -> 6.23 us  [swap(): return lax.ppermute(values, ('img', 'tile'), pairs)]
    all_to_all x1, waiting for transfers between devices: 0.01 us -> 2.51 us  [local(): lax.all_to_all(packed, 'tile', split_axis=0, concat_axis=0, tiled=True)]
    ppermute x7, starting transfers between devices: 6.81 us -> 7.53 us  [swap(): return lax.ppermute(values, ('img', 'tile'), pairs)]
    unnamed x12, local copies, waits for them, and re-layouts: 1.36 us -> 0.93 us
    pallas_call x2 -> x4, Pallas kernels: 2.59 us -> 2.91 us  [the longest x1 1.47 us: local(): call(functools.partial(forward_kernel, z), (f32(z.cout, used), bf(z.cin,...]
  transfers between devices with their start and end apart: 8 -> 8, of which waited for: 6 -> 6; matrix products, arithmetic and copies ran while one was open for 0% -> 0% of each run, Pallas kernels for 6% -> 11%
where the time goes in v4:
time: 32.2 us; the launch traced here: 31.8 us
  starting transfers between devices  14.8 us (46%)
  waiting for transfers between devices  8.75 us (27%)
  Pallas kernels  5.86 us (18%)
  between operations  1.39 us (4%)
  local copies, waits for them, and re-layouts  0.93 us (3%)
    ppermute x7, starting transfers between devices, swap(): return lax.ppermute(values, ('img', 'tile'), pairs)  7.53 us
    all_to_all x1, starting transfers between devices, local(): lax.all_to_all(packed, 'tile', split_axis=0, concat_axis=0, tiled=True)  7.25 us
    ppermute x7, waiting for transfers between devices, swap(): return lax.ppermute(values, ('img', 'tile'), pairs)  6.23 us
    all_to_all x1, waiting for transfers between devices, local(): lax.all_to_all(packed, 'tile', split_axis=0, concat_axis=0, tiled=True)  2.51 us
    pallas_call x1, Pallas kernels, local(): call(functools.partial(forward_kernel, z), (f32(z.cout, used), bf(z.cin,...  1.47 us
    pallas_call x1, Pallas kernels, local(): call(functools.partial(blend_kernel, z), bf(z.cout, z.height, z.width), [...  1.24 us
    unnamed x12, local copies, waits for them, and re-layouts  0.93 us
    pallas_call x1, Pallas kernels, local(): call(functools.partial(pack_kernel, z), bf(tiles, 2 * ROWS, 2 * z.cin), [...  0.9 us
  transfers between devices with their start and end apart: 8, of which 6 were waited for; matrix products, arithmetic and copies ran while one was open for 0% of the time, Pallas kernels for 11%

profile of v4, /device:TPU:0, one launch (start us, length us, event | category | flops | bytes accessed | tf_op | source)
XLA Modules:
  0.0 31.8 jit_solution(7093351174954637523)
XLA Ops:
  0.6 0.0 copy-start.1
  0.6 0.0 copy-start.3
  0.7 0.7 %copy-done.3 = bf16[1,64,1,128]{3,1,2,0:T(8,128)(2,1)S(1)} copy-done((bf16[1,64,1,128]{3,1,2,0:T(8,128)(2,1)S(1)}, bf16[1,64,1,128]{3,1,2,0:T(8,128)(2,1)}, u32[]{:S(2)}) %copy-start.3) | copy-done | bytes 16408
  1.4 0.9 %shard_map.110 = bf16[8,32,128]{2,1,0:T(8,128)(2,1)} custom-call(bf16[64,128]{1,0:T(8,128)(2,1)S(1)} %bitcast.16), custom_call_target="tpu_custom_call" | custom-call | flops 1000000 | bytes 200000 | tf_op jit(solution)/shard_map/pallas_call | solution.py:315
  2.3 7.3 %all-to-all-start = ((bf16[8,32,128]{2,1,0:T(8,128)(2,1)}), bf16[8,32,128]{2,1,0:T(8,128)(2,1)S(1)}, u32[]{:S(2)}, u32[]{:S(2)}) async-start(bf16[8,32,128]{2,1,0:T(8,128)(2,1)} %shard_map.110), calls=%async_computation | async-start | bytes 131072 | tf_op jit(solution)/shard_map/all_to_all | solution.py:318
  9.5 0.0 copy-done.1
  9.5 0.0 copy-start.5
  9.6 0.0 copy-start
  9.6 0.2 shard_map.111.flat_ref
  9.8 0.0 copy-start.2
  9.8 3.0 %collective-permute-start = (bf16[32,640]{1,0:T(8,128)(2,1)S(1)}, bf16[32,640]{1,0:T(8,128)(2,1)S(1)}, u32[]{:S(2)}, u32[]{:S(2)}) collective-permute-start(bf16[32,640]{1,0:T(8,128)(2,1)S(1)} %shard_map.111.flat_ref), channel_id=1, source_target_pairs={{0,4},{1,5},{2,6},{3,7},{4,0},{5,1},{6,2},{7,3},{8,12},{9,13},{10,... | collective-permute-start | bytes 122888 | tf_op jit(solution)/shard_map/ppermute | solution.py:280
  13.4 0.0 copy-done.5
  13.4 0.1 maximum_bitcast_fusion.row_ref
  13.5 0.0 copy-done
  13.5 0.5 %shard_map.112 = (f32[32,640]{1,0:T(8,128)S(1)}, bf16[288,640]{1,0:T(8,128)(2,1)S(1)}, bf16[32,640]{1,0:T(8,128)(2,1)S(1)}, bf16[256,768]{1,0:T(8,128)(2,1)S(1)}, f32[32,1]{1,0:T(8,128)S(1)}) custom-call(bf16[32,640]{1,0:T(8,128)(2,1)S(1)} %shard_map.111.flat_ref, bf16[3,3,32,32]{3,2,1,0:T(8,128)(2,1)S(1)} %copy-done, f32[1,33]{1,0:T(1,128)S(1)} %maximum_bitcast_fusion.row_ref), custom_call_target="tpu_custom_call" | custom-call | flops 1000000 | bytes 200000 | tf_op jit(solution)/shard_map/pallas_call | solution.py:328
  13.9 2.5 %all-to-all-done.got_ref = bf16[8,32,128]{2,1,0:T(8,128)(2,1)S(1)} async-done(((bf16[8,32,128]{2,1,0:T(8,128)(2,1)}), bf16[8,32,128]{2,1,0:T(8,128)(2,1)S(1)}, u32[]{:S(2)}, u32[]{:S(2)}) %all-to-all-start) | async-done | bytes 65568 | tf_op jit(solution)/shard_map/all_to_all | solution.py:318
  16.4 0.0 copy-done.2
  16.5 1.5 %shard_map.113 = (f32[32,960]{1,0:T(8,128)S(1)}, bf16[64,640]{1,0:T(8,128)(2,1)S(1)}, bf16[32,640]{1,0:T(8,128)(2,1)S(1)}, bf16[576,640]{1,0:T(8,128)(2,1)S(1)},...) custom-call(bf16[8,32,128]{2,1,0:T(8,128)(2,1)S(1)} %all-to-all-done.got_ref, ...), custom_call_target="tpu_custom_call" | custom-call | flops 1000000 | bytes 200000 | tf_op jit(solution)/shard_map/pallas_call | solution.py:341
  17.9 0.0 collective-permute-done.flat_ref
  17.9 0.8 %shard_map.114 = (f32[16,1024]{1,0:T(8,128)S(1)}, f32[16,1024]{1,0:T(8,128)S(1)}) custom-call(f32[32,960]{1,0:T(8,128)S(1)} %get-tuple-element.29.sums_ref, bf16[576,640]{1,0:T(8,128)(2,1)S(1)} %get-tuple-element.30.taps_ref, bf16[32,640]{1,0:T(8,128)(2,1)S(1)} %get-tuple-element.31.hidden_ref, f32[32,640]{1,0:T(8,128)S(1)} %get-tuple-element.32.slope_ref, ...), custom_call_target="tpu_custom_call" | custom-call | flops 1000000 | bytes 200000 | tf_op jit(solution)/shard_map/pallas_call | solution.py:356
  18.8 0.1 collective-permute-start.1
  18.8 1.2 %collective-permute-done.1 = f32[16,1024]{1,0:T(8,128)S(1)} collective-permute-done((f32[16,1024]{1,0:T(8,128)S(1)}, f32[16,1024]{1,0:T(8,128)S(1)}, u32[]{:S(2)}, u32[]{:S(2)}) %collective-permute-start.1) | collective-permute-done | bytes 65568 | tf_op jit(solution)/shard_map/ppermute | solution.py:280
  20.1 1.4 %collective-permute-start.4 = (bf16[16,1024]{1,0:T(8,128)(2,1)S(1)}, bf16[16,1024]{1,0:T(8,128)(2,1)S(1)}, u32[]{:S(2)}, u32[]{:S(2)}) collective-permute-start(bf16[16,1024]{1,0:T(8,128)(2,1)S(1)} %add_convert_fusion.1), channel_id=1, source_target_pairs={{0,17},{1,16},{2,19},{3,18},{4,21},{5,20},{6,23},{7,22},{8,25},{9,... | collective-permute-start | bytes 98312 | tf_op jit(solution)/shard_map/ppermute | solution.py:280
  21.5 1.1 %collective-permute-start.3 = (bf16[16,1024]{1,0:T(8,128)(2,1)S(1)}, bf16[16,1024]{1,0:T(8,128)(2,1)S(1)}, u32[]{:S(2)}, u32[]{:S(2)}) collective-permute-start(bf16[16,1024]{1,0:T(8,128)(2,1)S(1)} %add_convert_fusion.1), channel_id=1, source_target_pairs={{0,9},{1,8},{2,11},{3,10},{4,13},{5,12},{6,15},{7,14},{8,1},{9,0},... | collective-permute-start | bytes 98312 | tf_op jit(solution)/shard_map/ppermute | solution.py:280
  22.6 0.7 %collective-permute-start.2 = (bf16[16,1024]{1,0:T(8,128)(2,1)S(1)}, bf16[16,1024]{1,0:T(8,128)(2,1)S(1)}, u32[]{:S(2)}, u32[]{:S(2)}) collective-permute-start(bf16[16,1024]{1,0:T(8,128)(2,1)S(1)} %add_convert_fusion.1), channel_id=1, source_target_pairs={{0,24},{1,25},{2,26},{3,27},{4,28},{5,29},{6,30},{7,31},{8,16},{9,... | collective-permute-start | bytes 98312 | tf_op jit(solution)/shard_map/ppermute | solution.py:280
  23.4 1.8 %collective-permute-done.4 = bf16[16,1024]{1,0:T(8,128)(2,1)S(1)} collective-permute-done((bf16[16,1024]{1,0:T(8,128)(2,1)S(1)}, bf16[16,1024]{1,0:T(8,128)(2,1)S(1)}, u32[]{:S(2)}, u32[]{:S(2)}) %collective-permute-start.4) | collective-permute-done | bytes 32800 | tf_op jit(solution)/shard_map/ppermute | solution.py:280
  25.1 0.0 collective-permute-done.3
  25.1 0.8 %collective-permute-done.2 = bf16[16,1024]{1,0:T(8,128)(2,1)S(1)} collective-permute-done((bf16[16,1024]{1,0:T(8,128)(2,1)S(1)}, bf16[16,1024]{1,0:T(8,128)(2,1)S(1)}, u32[]{:S(2)}, u32[]{:S(2)}) %collective-permute-start.2) | collective-permute-done | bytes 32800 | tf_op jit(solution)/shard_map/ppermute | solution.py:280
  26.0 0.0 copy-start.4
  26.0 0.5 %collective-permute-start.5 = (bf16[16,1024]{1,0:T(8,128)(2,1)S(1)}, bf16[16,1024]{1,0:T(8,128)(2,1)S(1)}, u32[]{:S(2)}, u32[]{:S(2)}) collective-permute-start(bf16[16,1024]{1,0:T(8,128)(2,1)S(1)} %add_convert_fusion), channel_id=1, source_target_pairs={{0,10},{1,11},{2,8},{3,9},{4,14},{5,15},{6,12},{7,13},{8,2},{9,3},... | collective-permute-start | bytes 98312 | tf_op jit(solution)/shard_map/ppermute | solution.py:280
  26.5 0.2 copy-done.4
  26.7 1.2 %shard_map.115 = bf16[32,16,32]{2,1,0:T(8,128)(2,1)} custom-call(bf16[32,640]{1,0:T(8,128)(2,1)S(1)} %get-tuple-element.35.hidden_ref, bf16[64,640]{1,0:T(8,128)(2,1)S(1)} %get-tuple-element.36.up_ref, bf16[3,3,32,32]{3,2,1,0:T(8,128)(2,1)S(1)} %copy-done, bf16[32,64]{1,0:T(8,128)(2,1)S(1)} %bitcast.17, f32[1,33]{1,0:T(1,128)S(1)} %maximum_bitcast_fusion.row_ref), custom_call_target="tpu_custom_call" | custom-call | flops 1000000 | bytes 200000 | tf_op jit(solution)/shard_map/pallas_call | solution.py:363
  27.9 1.5 %collective-permute-done.5 = bf16[16,1024]{1,0:T(8,128)(2,1)S(1)} collective-permute-done((bf16[16,1024]{1,0:T(8,128)(2,1)S(1)}, bf16[16,1024]{1,0:T(8,128)(2,1)S(1)}, u32[]{:S(2)}, u32[]{:S(2)}) %collective-permute-start.5) | collective-permute-done | bytes 32800 | tf_op jit(solution)/shard_map/ppermute | solution.py:280
  29.4 0.7 %collective-permute-start.6 = (f32[16,1024]{1,0:T(8,128)S(1)}, f32[16,1024]{1,0:T(8,128)S(1)}, u32[]{:S(2)}, u32[]{:S(2)}) collective-permute-start(f32[16,1024]{1,0:T(8,128)S(1)} %convert_add_fusion.mine_ref), channel_id=1, source_target_pairs={{0,8},{1,9},{2,10},{3,11},{4,12},{5,13},{6,14},{7,15},{8,0},{9,1},... | collective-permute-start | bytes 196616 | tf_op jit(solution)/shard_map/ppermute | solution.py:280
  30.1 0.9 %collective-permute-done.6.other_ref = f32[16,1024]{1,0:T(8,128)S(1)} collective-permute-done((f32[16,1024]{1,0:T(8,128)S(1)}, f32[16,1024]{1,0:T(8,128)S(1)}, u32[]{:S(2)}, u32[]{:S(2)}) %collective-permute-start.6) | collective-permute-done | bytes 65568 | tf_op jit(solution)/shard_map/ppermute | solution.py:280
  31.0 0.8 %shard_map.116 = (f32[3,3,32,64]{3,2,1,0:T(8,128)}, f32[1,32]{1,0:T(1,128)}, f32[3,3,32,32]{3,2,1,0:T(8,128)}, f32[32,64]{1,0:T(8,128)}) custom-call(f32[16,1024]{1,0:T(8,128)S(1)} %convert_add_fusion.mine_ref, f32[16,1024]{1,0:T(8,128)S(1)} %collective-permute-done.6.other_ref), custom_call_target="tpu_custom_call" | custom-call | flops 1000000 | bytes 200000 | tf_op jit(solution)/shard_map/pallas_call | solution.py:374
  (3 shorter events, 0.0 us)
Async XLA Ops:
  0.6 8.9 %copy-start.1 = (bf16[1,32,32,16]{2,3,1,0:T(8,128)(2,1)S(1)}, bf16[1,32,32,16]{2,3,1,0:T(8,128)(2,1)}, u32[]{:S(2)}) copy-start(bf16[1,32,32,16]{2,3,1,0:T(8,128)(2,1)} %param.13) | copy-start | bytes 98308
  0.6 0.8 %copy-start.3 = (bf16[1,64,1,128]{3,1,2,0:T(8,128)(2,1)S(1)}, bf16[1,64,1,128]{3,1,2,0:T(8,128)(2,1)}, u32[]{:S(2)}) copy-start(bf16[1,64,1,128]{3,1,2,0:T(8,128)(2,1)} %param.7) | copy-start | bytes 49156
  2.3 14.2 %all-to-all-start = ((bf16[8,32,128]{2,1,0:T(8,128)(2,1)}), bf16[8,32,128]{2,1,0:T(8,128)(2,1)S(1)}, u32[]{:S(2)}, u32[]{:S(2)}) async-start(bf16[8,32,128]{2,1,0:T(8,128)(2,1)} %shard_map.110), calls=%async_computation | async-start | bytes 131072 | tf_op jit(solution)/shard_map/all_to_all | solution.py:318
  9.5 3.8 %copy-start.5 = (f32[32]{0:T(128)S(1)}, f32[32]{0:T(128)}, u32[]{:S(2)}) copy-start(f32[32]{0:T(128)} %param.9) | copy-start | bytes 388
  9.6 3.9 %copy-start = (bf16[3,3,32,32]{3,2,1,0:T(8,128)(2,1)S(1)}, bf16[3,3,32,32]{3,2,1,0:T(8,128)(2,1)}, u32[]{:S(2)}) copy-start(bf16[3,3,32,32]{3,2,1,0:T(8,128)(2,1)} %ws_ref.5) | copy-start | bytes 55300
  9.8 6.7 %copy-start.2 = (bf16[3,3,64,32]{2,3,1,0:T(8,128)(2,1)S(1)}, bf16[3,3,64,32]{2,3,1,0:T(8,128)(2,1)}, u32[]{:S(2)}) copy-start(bf16[3,3,64,32]{2,3,1,0:T(8,128)(2,1)} %param.8) | copy-start | bytes 110596
  9.8 8.2 %collective-permute-start = (bf16[32,640]{1,0:T(8,128)(2,1)S(1)}, bf16[32,640]{1,0:T(8,128)(2,1)S(1)}, u32[]{:S(2)}, u32[]{:S(2)}) collective-permute-start(bf16[32,640]{1,0:T(8,128)(2,1)S(1)} %shard_map.111.flat_ref), channel_id=1, source_target_pairs={{0,4},{1,5},{2,6},{3,7},{4,0},{5,1},{6,2},{7,3},{8,12},{9,13},{10,... | collective-permute-start | bytes 122888 | tf_op jit(solution)/shard_map/ppermute | solution.py:280
  18.8 1.3 %collective-permute-start.1 = (f32[16,1024]{1,0:T(8,128)S(1)}, f32[16,1024]{1,0:T(8,128)S(1)}, u32[]{:S(2)}, u32[]{:S(2)}) collective-permute-start(f32[16,1024]{1,0:T(8,128)S(1)} %get-tuple-element.34), channel_id=1, source_target_pairs={{0,8},{1,9},{2,10},{3,11},{4,12},{5,13},{6,14},{7,15},{8,0},{9,1},... | collective-permute-start | bytes 196616 | tf_op jit(solution)/shard_map/ppermute | solution.py:280
  20.1 5.1 %collective-permute-start.4 = (bf16[16,1024]{1,0:T(8,128)(2,1)S(1)}, bf16[16,1024]{1,0:T(8,128)(2,1)S(1)}, u32[]{:S(2)}, u32[]{:S(2)}) collective-permute-start(bf16[16,1024]{1,0:T(8,128)(2,1)S(1)} %add_convert_fusion.1), channel_id=1, source_target_pairs={{0,17},{1,16},{2,19},{3,18},{4,21},{5,20},{6,23},{7,22},{8,25},{9,... | collective-permute-start | bytes 98312 | tf_op jit(solution)/shard_map/ppermute | solution.py:280
  21.5 3.6 %collective-permute-start.3 = (bf16[16,1024]{1,0:T(8,128)(2,1)S(1)}, bf16[16,1024]{1,0:T(8,128)(2,1)S(1)}, u32[]{:S(2)}, u32[]{:S(2)}) collective-permute-start(bf16[16,1024]{1,0:T(8,128)(2,1)S(1)} %add_convert_fusion.1), channel_id=1, source_target_pairs={{0,9},{1,8},{2,11},{3,10},{4,13},{5,12},{6,15},{7,14},{8,1},{9,0},... | collective-permute-start | bytes 98312 | tf_op jit(solution)/shard_map/ppermute | solution.py:280
  22.6 3.3 %collective-permute-start.2 = (bf16[16,1024]{1,0:T(8,128)(2,1)S(1)}, bf16[16,1024]{1,0:T(8,128)(2,1)S(1)}, u32[]{:S(2)}, u32[]{:S(2)}) collective-permute-start(bf16[16,1024]{1,0:T(8,128)(2,1)S(1)} %add_convert_fusion.1), channel_id=1, source_target_pairs={{0,24},{1,25},{2,26},{3,27},{4,28},{5,29},{6,30},{7,31},{8,16},{9,... | collective-permute-start | bytes 98312 | tf_op jit(solution)/shard_map/ppermute | solution.py:280
  26.0 0.7 %copy-start.4 = (bf16[64,32]{0,1:T(8,128)(2,1)S(1)}, bf16[64,32]{0,1:T(8,128)(2,1)}, u32[]{:S(2)}) copy-start(bf16[64,32]{0,1:T(8,128)(2,1)} %param.11) | copy-start | bytes 12292
  26.0 3.4 %collective-permute-start.5 = (bf16[16,1024]{1,0:T(8,128)(2,1)S(1)}, bf16[16,1024]{1,0:T(8,128)(2,1)S(1)}, u32[]{:S(2)}, u32[]{:S(2)}) collective-permute-start(bf16[16,1024]{1,0:T(8,128)(2,1)S(1)} %add_convert_fusion), channel_id=1, source_target_pairs={{0,10},{1,11},{2,8},{3,9},{4,14},{5,15},{6,12},{7,13},{8,2},{9,3},... | collective-permute-start | bytes 98312 | tf_op jit(solution)/shard_map/ppermute | solution.py:280
  29.4 1.6 %collective-permute-start.6 = (f32[16,1024]{1,0:T(8,128)S(1)}, f32[16,1024]{1,0:T(8,128)S(1)}, u32[]{:S(2)}, u32[]{:S(2)}) collective-permute-start(f32[16,1024]{1,0:T(8,128)S(1)} %convert_add_fusion.mine_ref), channel_id=1, source_target_pairs={{0,8},{1,9},{2,10},{3,11},{4,12},{5,13},{6,14},{7,15},{8,0},{9,1},... | collective-permute-start | bytes 196616 | tf_op jit(solution)/shard_map/ppermute | solution.py:280

commit v5 on v4

--- a/solution.py
+++ b/solution.py
@@ -290,8 +290,10 @@
     while k < tiles // 2:
         bits.append((0, k))
         k *= 2
-    for at in range(0, len(bits), 2):
-        group = bits[at : at + 2]
+    odd = len(bits) % 2
+    groups = [bits[:odd]] if odd else []
+    groups += [(bits[at + 1], bits[at]) for at in range(odd, len(bits), 2)]
+    for group in groups:
         sent = mine.astype(BF16)
         partners = [(a ^ 1, b) for a, b in group]
         if len(group) == 2:

time: 32.2 us -> 31.1 us (0.966)
  waiting for transfers between devices: 8.75 us -> 7.56 us
    ppermute x7, waiting for transfers between devices: 6.23 us -> 5.04 us  [swap(): return lax.ppermute(values, ('img', 'tile'), pairs)]
  transfers between devices with their start and end apart: 8 -> 8, of which waited for: 6 -> 5; matrix products, arithmetic and copies ran while one was open for 0% -> 0% of each run, Pallas kernels for 11% -> 11%
where the time goes in v5:
time: 31.1 us; the launch traced here: 30.8 us
  starting transfers between devices  15.1 us (49%)
  waiting for transfers between devices  7.56 us (24%)
  Pallas kernels  5.86 us (19%)
  between operations  1.39 us (4%)
  local copies, waits for them, and re-layouts  0.77 us (2%)
    ppermute x7, starting transfers between devices, swap(): return lax.ppermute(values, ('img', 'tile'), pairs)  7.84 us
    all_to_all x1, starting transfers between devices, local(): lax.all_to_all(packed, 'tile', split_axis=0, concat_axis=0, tiled=True)  7.25 us
    ppermute x7, waiting for transfers between devices, swap(): return lax.ppermute(values, ('img', 'tile'), pairs)  5.04 us
    all_to_all x1, waiting for transfers between devices, local(): lax.all_to_all(packed, 'tile', split_axis=0, concat_axis=0, tiled=True)  2.51 us
    pallas_call x1, Pallas kernels, local(): call(functools.partial(forward_kernel, z), (f32(z.cout, used), bf(z.cin,...  1.47 us
    pallas_call x1, Pallas kernels, local(): call(functools.partial(blend_kernel, z), bf(z.cout, z.height, z.width), [...  1.24 us
    pallas_call x1, Pallas kernels, local(): call(functools.partial(pack_kernel, z), bf(tiles, 2 * ROWS, 2 * z.cin), [...  0.9 us
    pallas_call x1, Pallas kernels, local(): call(functools.partial(finish_kernel, z), (f32(3, 3, z.cout, z.cin), f32(...  0.81 us
  transfers between devices with their start and end apart: 8, of which 5 were waited for; matrix products, arithmetic and copies ran while one was open for 0% of the time, Pallas kernels for 11%

profile of v5, /device:TPU:0, one launch (start us, length us, event | category | flops | bytes accessed | tf_op | source)
XLA Modules:
  0.0 30.8 jit_solution(1951853762440697390)
XLA Ops:
  0.6 0.0 copy-start.1
  0.6 0.0 copy-start.3
  0.7 0.7 %copy-done.3 = bf16[1,64,1,128]{3,1,2,0:T(8,128)(2,1)S(1)} copy-done((bf16[1,64,1,128]{3,1,2,0:T(8,128)(2,1)S(1)}, bf16[1,64,1,128]{3,1,2,0:T(8,128)(2,1)}, u32[]{:S(2)}) %copy-start.3) | copy-done | bytes 16408
  1.4 0.9 %shard_map.110 = bf16[8,32,128]{2,1,0:T(8,128)(2,1)} custom-call(bf16[64,128]{1,0:T(8,128)(2,1)S(1)} %bitcast.16), custom_call_target="tpu_custom_call" | custom-call | flops 1000000 | bytes 200000 | tf_op jit(solution)/shard_map/pallas_call | solution.py:317
  2.3 7.3 %all-to-all-start = ((bf16[8,32,128]{2,1,0:T(8,128)(2,1)}), bf16[8,32,128]{2,1,0:T(8,128)(2,1)S(1)}, u32[]{:S(2)}, u32[]{:S(2)}) async-start(bf16[8,32,128]{2,1,0:T(8,128)(2,1)} %shard_map.110), calls=%async_computation | async-start | bytes 131072 | tf_op jit(solution)/shard_map/all_to_all | solution.py:320
  9.5 0.0 copy-done.1
  9.5 0.0 copy-start.5
  9.6 0.0 copy-start
  9.6 0.2 shard_map.111.flat_ref
  9.8 0.0 copy-start.2
  9.8 3.0 %collective-permute-start = (bf16[32,640]{1,0:T(8,128)(2,1)S(1)}, bf16[32,640]{1,0:T(8,128)(2,1)S(1)}, u32[]{:S(2)}, u32[]{:S(2)}) collective-permute-start(bf16[32,640]{1,0:T(8,128)(2,1)S(1)} %shard_map.111.flat_ref), channel_id=1, source_target_pairs={{0,4},{1,5},{2,6},{3,7},{4,0},{5,1},{6,2},{7,3},{8,12},{9,13},{10,... | collective-permute-start | bytes 122888 | tf_op jit(solution)/shard_map/ppermute | solution.py:280
  13.4 0.0 copy-done.5
  13.4 0.1 maximum_bitcast_fusion.row_ref
  13.5 0.0 copy-done
  13.5 0.5 %shard_map.112 = (f32[32,640]{1,0:T(8,128)S(1)}, bf16[288,640]{1,0:T(8,128)(2,1)S(1)}, bf16[32,640]{1,0:T(8,128)(2,1)S(1)}, bf16[256,768]{1,0:T(8,128)(2,1)S(1)}, f32[32,1]{1,0:T(8,128)S(1)}) custom-call(bf16[32,640]{1,0:T(8,128)(2,1)S(1)} %shard_map.111.flat_ref, bf16[3,3,32,32]{3,2,1,0:T(8,128)(2,1)S(1)} %copy-done, f32[1,33]{1,0:T(1,128)S(1)} %maximum_bitcast_fusion.row_ref), custom_call_target="tpu_custom_call" | custom-call | flops 1000000 | bytes 200000 | tf_op jit(solution)/shard_map/pallas_call | solution.py:330
  13.9 2.5 %all-to-all-done.got_ref = bf16[8,32,128]{2,1,0:T(8,128)(2,1)S(1)} async-done(((bf16[8,32,128]{2,1,0:T(8,128)(2,1)}), bf16[8,32,128]{2,1,0:T(8,128)(2,1)S(1)}, u32[]{:S(2)}, u32[]{:S(2)}) %all-to-all-start) | async-done | bytes 65568 | tf_op jit(solution)/shard_map/all_to_all | solution.py:320
  16.4 0.0 copy-done.2
  16.5 1.5 %shard_map.113 = (f32[32,960]{1,0:T(8,128)S(1)}, bf16[64,640]{1,0:T(8,128)(2,1)S(1)}, bf16[32,640]{1,0:T(8,128)(2,1)S(1)}, bf16[576,640]{1,0:T(8,128)(2,1)S(1)},...) custom-call(bf16[8,32,128]{2,1,0:T(8,128)(2,1)S(1)} %all-to-all-done.got_ref, ...), custom_call_target="tpu_custom_call" | custom-call | flops 1000000 | bytes 200000 | tf_op jit(solution)/shard_map/pallas_call | solution.py:343
  17.9 0.0 collective-permute-done.flat_ref
  17.9 0.8 %shard_map.114 = (f32[16,1024]{1,0:T(8,128)S(1)}, f32[16,1024]{1,0:T(8,128)S(1)}) custom-call(f32[32,960]{1,0:T(8,128)S(1)} %get-tuple-element.29.sums_ref, bf16[576,640]{1,0:T(8,128)(2,1)S(1)} %get-tuple-element.30.taps_ref, bf16[32,640]{1,0:T(8,128)(2,1)S(1)} %get-tuple-element.31.hidden_ref, f32[32,640]{1,0:T(8,128)S(1)} %get-tuple-element.32.slope_ref, ...), custom_call_target="tpu_custom_call" | custom-call | flops 1000000 | bytes 200000 | tf_op jit(solution)/shard_map/pallas_call | solution.py:358
  18.8 0.1 collective-permute-start.1
  18.8 1.2 %collective-permute-done.1 = f32[16,1024]{1,0:T(8,128)S(1)} collective-permute-done((f32[16,1024]{1,0:T(8,128)S(1)}, f32[16,1024]{1,0:T(8,128)S(1)}, u32[]{:S(2)}, u32[]{:S(2)}) %collective-permute-start.1) | collective-permute-done | bytes 65568 | tf_op jit(solution)/shard_map/ppermute | solution.py:280
  20.1 1.3 %collective-permute-start.2 = (bf16[16,1024]{1,0:T(8,128)(2,1)S(1)}, bf16[16,1024]{1,0:T(8,128)(2,1)S(1)}, u32[]{:S(2)}, u32[]{:S(2)}) collective-permute-start(bf16[16,1024]{1,0:T(8,128)(2,1)S(1)} %add_convert_fusion.1), channel_id=1, source_target_pairs={{0,24},{1,25},{2,26},{3,27},{4,28},{5,29},{6,30},{7,31},{8,16},{9,... | collective-permute-start | bytes 98312 | tf_op jit(solution)/shard_map/ppermute | solution.py:280
  21.4 2.1 %collective-permute-done.2 = bf16[16,1024]{1,0:T(8,128)(2,1)S(1)} collective-permute-done((bf16[16,1024]{1,0:T(8,128)(2,1)S(1)}, bf16[16,1024]{1,0:T(8,128)(2,1)S(1)}, u32[]{:S(2)}, u32[]{:S(2)}) %collective-permute-start.2) | collective-permute-done | bytes 32800 | tf_op jit(solution)/shard_map/ppermute | solution.py:280
  23.5 0.0 copy-start.4
  23.5 0.7 %collective-permute-start.5 = (bf16[16,1024]{1,0:T(8,128)(2,1)S(1)}, bf16[16,1024]{1,0:T(8,128)(2,1)S(1)}, u32[]{:S(2)}, u32[]{:S(2)}) collective-permute-start(bf16[16,1024]{1,0:T(8,128)(2,1)S(1)} %add_convert_fusion), channel_id=1, source_target_pairs={{0,3},{1,2},{2,1},{3,0},{4,7},{5,6},{6,5},{7,4},{8,11},{9,10},{10,... | collective-permute-start | bytes 98312 | tf_op jit(solution)/shard_map/ppermute | solution.py:280
  24.2 0.5 %collective-permute-start.4 = (bf16[16,1024]{1,0:T(8,128)(2,1)S(1)}, bf16[16,1024]{1,0:T(8,128)(2,1)S(1)}, u32[]{:S(2)}, u32[]{:S(2)}) collective-permute-start(bf16[16,1024]{1,0:T(8,128)(2,1)S(1)} %add_convert_fusion), channel_id=1, source_target_pairs={{0,9},{1,8},{2,11},{3,10},{4,13},{5,12},{6,15},{7,14},{8,1},{9,0},... | collective-permute-start | bytes 98312 | tf_op jit(solution)/shard_map/ppermute | solution.py:280
  24.8 2.0 %collective-permute-start.3 = (bf16[16,1024]{1,0:T(8,128)(2,1)S(1)}, bf16[16,1024]{1,0:T(8,128)(2,1)S(1)}, u32[]{:S(2)}, u32[]{:S(2)}) collective-permute-start(bf16[16,1024]{1,0:T(8,128)(2,1)S(1)} %add_convert_fusion), channel_id=1, source_target_pairs={{0,10},{1,11},{2,8},{3,9},{4,14},{5,15},{6,12},{7,13},{8,2},{9,3},... | collective-permute-start | bytes 98312 | tf_op jit(solution)/shard_map/ppermute | solution.py:280
  26.8 0.0 copy-done.4
  26.8 1.2 %shard_map.115 = bf16[32,16,32]{2,1,0:T(8,128)(2,1)} custom-call(bf16[32,640]{1,0:T(8,128)(2,1)S(1)} %get-tuple-element.35.hidden_ref, bf16[64,640]{1,0:T(8,128)(2,1)S(1)} %get-tuple-element.36.up_ref, bf16[3,3,32,32]{3,2,1,0:T(8,128)(2,1)S(1)} %copy-done, bf16[32,64]{1,0:T(8,128)(2,1)S(1)} %bitcast.17, f32[1,33]{1,0:T(1,128)S(1)} %maximum_bitcast_fusion.row_ref), custom_call_target="tpu_custom_call" | custom-call | flops 1000000 | bytes 200000 | tf_op jit(solution)/shard_map/pallas_call | solution.py:365
  28.0 0.6 %collective-permute-done.5 = bf16[16,1024]{1,0:T(8,128)(2,1)S(1)} collective-permute-done((bf16[16,1024]{1,0:T(8,128)(2,1)S(1)}, bf16[16,1024]{1,0:T(8,128)(2,1)S(1)}, u32[]{:S(2)}, u32[]{:S(2)}) %collective-permute-start.5) | collective-permute-done | bytes 32800 | tf_op jit(solution)/shard_map/ppermute | solution.py:280
  28.6 0.0 collective-permute-done.4
  28.6 0.0 collective-permute-done.3
  28.7 0.2 collective-permute-start.6
  28.8 1.1 %collective-permute-done.6.other_ref = f32[16,1024]{1,0:T(8,128)S(1)} collective-permute-done((f32[16,1024]{1,0:T(8,128)S(1)}, f32[16,1024]{1,0:T(8,128)S(1)}, u32[]{:S(2)}, u32[]{:S(2)}) %collective-permute-start.6) | collective-permute-done | bytes 65568 | tf_op jit(solution)/shard_map/ppermute | solution.py:280
  30.0 0.8 %shard_map.116 = (f32[3,3,32,64]{3,2,1,0:T(8,128)}, f32[1,32]{1,0:T(1,128)}, f32[3,3,32,32]{3,2,1,0:T(8,128)}, f32[32,64]{1,0:T(8,128)}) custom-call(f32[16,1024]{1,0:T(8,128)S(1)} %add_add_fusion.mine_ref, f32[16,1024]{1,0:T(8,128)S(1)} %collective-permute-done.6.other_ref), custom_call_target="tpu_custom_call" | custom-call | flops 1000000 | bytes 200000 | tf_op jit(solution)/shard_map/pallas_call | solution.py:376
  (3 shorter events, 0.0 us)
Async XLA Ops:
  0.6 8.9 %copy-start.1 = (bf16[1,32,32,16]{2,3,1,0:T(8,128)(2,1)S(1)}, bf16[1,32,32,16]{2,3,1,0:T(8,128)(2,1)}, u32[]{:S(2)}) copy-start(bf16[1,32,32,16]{2,3,1,0:T(8,128)(2,1)} %param.13) | copy-start | bytes 98308
  0.6 0.8 %copy-start.3 = (bf16[1,64,1,128]{3,1,2,0:T(8,128)(2,1)S(1)}, bf16[1,64,1,128]{3,1,2,0:T(8,128)(2,1)}, u32[]{:S(2)}) copy-start(bf16[1,64,1,128]{3,1,2,0:T(8,128)(2,1)} %param.7) | copy-start | bytes 49156
  2.3 14.2 %all-to-all-start = ((bf16[8,32,128]{2,1,0:T(8,128)(2,1)}), bf16[8,32,128]{2,1,0:T(8,128)(2,1)S(1)}, u32[]{:S(2)}, u32[]{:S(2)}) async-start(bf16[8,32,128]{2,1,0:T(8,128)(2,1)} %shard_map.110), calls=%async_computation | async-start | bytes 131072 | tf_op jit(solution)/shard_map/all_to_all | solution.py:320
  9.5 3.8 %copy-start.5 = (f32[32]{0:T(128)S(1)}, f32[32]{0:T(128)}, u32[]{:S(2)}) copy-start(f32[32]{0:T(128)} %param.9) | copy-start | bytes 388
  9.6 3.9 %copy-start = (bf16[3,3,32,32]{3,2,1,0:T(8,128)(2,1)S(1)}, bf16[3,3,32,32]{3,2,1,0:T(8,128)(2,1)}, u32[]{:S(2)}) copy-start(bf16[3,3,32,32]{3,2,1,0:T(8,128)(2,1)} %ws_ref.5) | copy-start | bytes 55300
  9.8 6.7 %copy-start.2 = (bf16[3,3,64,32]{2,3,1,0:T(8,128)(2,1)S(1)}, bf16[3,3,64,32]{2,3,1,0:T(8,128)(2,1)}, u32[]{:S(2)}) copy-start(bf16[3,3,64,32]{2,3,1,0:T(8,128)(2,1)} %param.8) | copy-start | bytes 110596
  9.8 8.2 %collective-permute-start = (bf16[32,640]{1,0:T(8,128)(2,1)S(1)}, bf16[32,640]{1,0:T(8,128)(2,1)S(1)}, u32[]{:S(2)}, u32[]{:S(2)}) collective-permute-start(bf16[32,640]{1,0:T(8,128)(2,1)S(1)} %shard_map.111.flat_ref), channel_id=1, source_target_pairs={{0,4},{1,5},{2,6},{3,7},{4,0},{5,1},{6,2},{7,3},{8,12},{9,13},{10,... | collective-permute-start | bytes 122888 | tf_op jit(solution)/shard_map/ppermute | solution.py:280
  18.8 1.3 %collective-permute-start.1 = (f32[16,1024]{1,0:T(8,128)S(1)}, f32[16,1024]{1,0:T(8,128)S(1)}, u32[]{:S(2)}, u32[]{:S(2)}) collective-permute-start(f32[16,1024]{1,0:T(8,128)S(1)} %get-tuple-element.34), channel_id=1, source_target_pairs={{0,8},{1,9},{2,10},{3,11},{4,12},{5,13},{6,14},{7,15},{8,0},{9,1},... | collective-permute-start | bytes 196616 | tf_op jit(solution)/shard_map/ppermute | solution.py:280
  20.1 3.4 %collective-permute-start.2 = (bf16[16,1024]{1,0:T(8,128)(2,1)S(1)}, bf16[16,1024]{1,0:T(8,128)(2,1)S(1)}, u32[]{:S(2)}, u32[]{:S(2)}) collective-permute-start(bf16[16,1024]{1,0:T(8,128)(2,1)S(1)} %add_convert_fusion.1), channel_id=1, source_target_pairs={{0,24},{1,25},{2,26},{3,27},{4,28},{5,29},{6,30},{7,31},{8,16},{9,... | collective-permute-start | bytes 98312 | tf_op jit(solution)/shard_map/ppermute | solution.py:280
  23.5 3.3 %copy-start.4 = (bf16[64,32]{0,1:T(8,128)(2,1)S(1)}, bf16[64,32]{0,1:T(8,128)(2,1)}, u32[]{:S(2)}) copy-start(bf16[64,32]{0,1:T(8,128)(2,1)} %param.11) | copy-start | bytes 12292
  23.5 5.1 %collective-permute-start.5 = (bf16[16,1024]{1,0:T(8,128)(2,1)S(1)}, bf16[16,1024]{1,0:T(8,128)(2,1)S(1)}, u32[]{:S(2)}, u32[]{:S(2)}) collective-permute-start(bf16[16,1024]{1,0:T(8,128)(2,1)S(1)} %add_convert_fusion), channel_id=1, source_target_pairs={{0,3},{1,2},{2,1},{3,0},{4,7},{5,6},{6,5},{7,4},{8,11},{9,10},{10,... | collective-permute-start | bytes 98312 | tf_op jit(solution)/shard_map/ppermute | solution.py:280
  24.2 4.4 %collective-permute-start.4 = (bf16[16,1024]{1,0:T(8,128)(2,1)S(1)}, bf16[16,1024]{1,0:T(8,128)(2,1)S(1)}, u32[]{:S(2)}, u32[]{:S(2)}) collective-permute-start(bf16[16,1024]{1,0:T(8,128)(2,1)S(1)} %add_convert_fusion), channel_id=1, source_target_pairs={{0,9},{1,8},{2,11},{3,10},{4,13},{5,12},{6,15},{7,14},{8,1},{9,0},... | collective-permute-start | bytes 98312 | tf_op jit(solution)/shard_map/ppermute | solution.py:280
  24.8 3.9 %collective-permute-start.3 = (bf16[16,1024]{1,0:T(8,128)(2,1)S(1)}, bf16[16,1024]{1,0:T(8,128)(2,1)S(1)}, u32[]{:S(2)}, u32[]{:S(2)}) collective-permute-start(bf16[16,1024]{1,0:T(8,128)(2,1)S(1)} %add_convert_fusion), channel_id=1, source_target_pairs={{0,10},{1,11},{2,8},{3,9},{4,14},{5,15},{6,12},{7,13},{8,2},{9,3},... | collective-permute-start | bytes 98312 | tf_op jit(solution)/shard_map/ppermute | solution.py:280
  28.7 1.3 %collective-permute-start.6 = (f32[16,1024]{1,0:T(8,128)S(1)}, f32[16,1024]{1,0:T(8,128)S(1)}, u32[]{:S(2)}, u32[]{:S(2)}) collective-permute-start(f32[16,1024]{1,0:T(8,128)S(1)} %add_add_fusion.mine_ref), channel_id=1, source_target_pairs={{0,8},{1,9},{2,10},{3,11},{4,12},{5,13},{6,14},{7,15},{8,0},{9,1},... | collective-permute-start | bytes 196616 | tf_op jit(solution)/shard_map/ppermute | solution.py:280

commit v6 on v5

--- a/solution.py
+++ b/solution.py
@@ -213,8 +213,8 @@
         grads = jnp.concatenate([grads, jnp.zeros((z.cout, full - used), F32)], axis=1)
     half = z.cout // 2
     top = holds_top(z)
-    keep_ref[...] = jnp.where(top, grads[:half], grads[half:])
-    give_ref[...] = jnp.where(top, grads[half:], grads[:half])
+    keep_ref[...] = jnp.where(top, grads[:half], grads[half:]).astype(BF16)
+    give_ref[...] = jnp.where(top, grads[half:], grads[:half]).astype(BF16)
 
 
 def blend_kernel(z, hidden_ref, up_ref, ws_ref, wk_ref, row_ref, out_ref, tall_ref):
@@ -280,9 +280,17 @@
     return lax.ppermute(values, ("img", "tile"), pairs)
 
 
-def total_over_chips(mine, images, tiles):
+def total_over_devices(keep, give, images, tiles):
+    own = keep.astype(F32)
+    if images >= 4:
+        core = swap(give, images, tiles, (1, 0))
+        cross = swap(keep, images, tiles, (3, 0))
+        straight = swap(give, images, tiles, (2, 0))
+        mine = (own + cross.astype(F32)) + (core.astype(F32) + straight.astype(F32))
+    else:
+        mine = own + swap(give, images, tiles, (1, 0)).astype(F32)
     bits = []
-    k = 2
+    k = 4
     while k < images:
         bits.append((k, 0))
         k *= 2
@@ -354,7 +362,7 @@
         [pltpu.VMEM((9 * z.cin, z.lanes), BF16)],
     )(got, d_hidden, spread, dskip, jnp.transpose(w_first, (0, 1, 3, 2)), bias, interp)
 
-    half = f32(z.cout // 2, up128(used))
+    half = bf(z.cout // 2, up128(used))
     keep, give = call(
         functools.partial(other_kernel, z, scale),
         (half, half),
@@ -369,8 +377,7 @@
         [pltpu.VMEM((z.cout * z.height, 128), F32)],
     )(hidden, up, w_second, jnp.transpose(w_skip), row)
 
-    mine = keep + swap(give, images, tiles, (1, 0))
-    mine = total_over_chips(mine, images, tiles)
+    mine = total_over_devices(keep, give, images, tiles)
     mine, blended = lax.optimization_barrier((mine, blended))
     other = swap(mine, images, tiles, (1, 0))
     first, bias, second, skip = call(

time: 31.1 us -> 30.4 us (0.977)
  waiting for transfers between devices: 7.56 us -> 6.09 us
  starting transfers between devices: 15.1 us -> 15.8 us
    ppermute x7 -> x8, waiting for transfers between devices: 5.04 us -> 3.57 us  [swap(): return lax.ppermute(values, ('img', 'tile'), pairs)]
    ppermute x7 -> x8, starting transfers between devices: 7.84 us -> 8.51 us  [swap(): return lax.ppermute(values, ('img', 'tile'), pairs)]
  transfers between devices with their start and end apart: 8 -> 9, of which waited for: 5 -> 5; matrix products, arithmetic and copies ran while one was open for 0% -> 0% of each run, Pallas kernels for 11% -> 11%
where the time goes in v6:
time: 30.4 us; the launch traced here: 30 us
  starting transfers between devices  15.8 us (52%)
  waiting for transfers between devices  6.09 us (20%)
  Pallas kernels  5.86 us (19%)
  between operations  1.39 us (5%)
  local copies, waits for them, and re-layouts  0.77 us (3%)
    ppermute x8, starting transfers between devices, swap(): return lax.ppermute(values, ('img', 'tile'), pairs)  8.51 us
    all_to_all x1, starting transfers between devices, local(): lax.all_to_all(packed, 'tile', split_axis=0, concat_axis=0, tiled=True)  7.25 us
    ppermute x8, waiting for transfers between devices, swap(): return lax.ppermute(values, ('img', 'tile'), pairs)  3.57 us
    all_to_all x1, waiting for transfers between devices, local(): lax.all_to_all(packed, 'tile', split_axis=0, concat_axis=0, tiled=True)  2.51 us
    pallas_call x1, Pallas kernels, local(): call(functools.partial(forward_kernel, z), (f32(z.cout, used), bf(z.cin,...  1.47 us
    pallas_call x1, Pallas kernels, local(): call(functools.partial(blend_kernel, z), bf(z.cout, z.height, z.width), [...  1.24 us
    pallas_call x1, Pallas kernels, local(): call(functools.partial(pack_kernel, z), bf(tiles, 2 * ROWS, 2 * z.cin), [...  0.9 us
    pallas_call x1, Pallas kernels, local(): call(functools.partial(finish_kernel, z), (f32(3, 3, z.cout, z.cin), f32(...  0.81 us
  transfers between devices with their start and end apart: 9, of which 5 were waited for; matrix products, arithmetic and copies ran while one was open for 0% of the time, Pallas kernels for 11%

profile of v6, /device:TPU:0, one launch (start us, length us, event | category | flops | bytes accessed | tf_op | source)
XLA Modules:
  0.0 30.0 jit_solution(12622719647252841174)
XLA Ops:
  0.6 0.0 copy-start.1
  0.6 0.0 copy-start.3
  0.7 0.7 %copy-done.3 = bf16[1,64,1,128]{3,1,2,0:T(8,128)(2,1)S(1)} copy-done((bf16[1,64,1,128]{3,1,2,0:T(8,128)(2,1)S(1)}, bf16[1,64,1,128]{3,1,2,0:T(8,128)(2,1)}, u32[]{:S(2)}) %copy-start.3) | copy-done | bytes 16408
  1.4 0.9 %shard_map.110 = bf16[8,32,128]{2,1,0:T(8,128)(2,1)} custom-call(bf16[64,128]{1,0:T(8,128)(2,1)S(1)} %bitcast.16), custom_call_target="tpu_custom_call" | custom-call | flops 1000000 | bytes 200000 | tf_op jit(solution)/shard_map/pallas_call | solution.py:325
  2.3 7.3 %all-to-all-start = ((bf16[8,32,128]{2,1,0:T(8,128)(2,1)}), bf16[8,32,128]{2,1,0:T(8,128)(2,1)S(1)}, u32[]{:S(2)}, u32[]{:S(2)}) async-start(bf16[8,32,128]{2,1,0:T(8,128)(2,1)} %shard_map.110), calls=%async_computation | async-start | bytes 131072 | tf_op jit(solution)/shard_map/all_to_all | solution.py:328
  9.5 0.0 copy-done.1
  9.5 0.0 copy-start.5
  9.6 0.0 copy-start
  9.6 0.2 shard_map.111.flat_ref
  9.8 0.0 copy-start.2
  9.8 3.0 %collective-permute-start = (bf16[32,640]{1,0:T(8,128)(2,1)S(1)}, bf16[32,640]{1,0:T(8,128)(2,1)S(1)}, u32[]{:S(2)}, u32[]{:S(2)}) collective-permute-start(bf16[32,640]{1,0:T(8,128)(2,1)S(1)} %shard_map.111.flat_ref), channel_id=1, source_target_pairs={{0,4},{1,5},{2,6},{3,7},{4,0},{5,1},{6,2},{7,3},{8,12},{9,13},{10,... | collective-permute-start | bytes 122888 | tf_op jit(solution)/shard_map/ppermute | solution.py:280
  13.4 0.0 copy-done.5
  13.4 0.1 maximum_bitcast_fusion.row_ref
  13.5 0.0 copy-done
  13.5 0.5 %shard_map.112 = (f32[32,640]{1,0:T(8,128)S(1)}, bf16[288,640]{1,0:T(8,128)(2,1)S(1)}, bf16[32,640]{1,0:T(8,128)(2,1)S(1)}, bf16[256,768]{1,0:T(8,128)(2,1)S(1)}, f32[32,1]{1,0:T(8,128)S(1)}) custom-call(bf16[32,640]{1,0:T(8,128)(2,1)S(1)} %shard_map.111.flat_ref, bf16[3,3,32,32]{3,2,1,0:T(8,128)(2,1)S(1)} %copy-done, f32[1,33]{1,0:T(1,128)S(1)} %maximum_bitcast_fusion.row_ref), custom_call_target="tpu_custom_call" | custom-call | flops 1000000 | bytes 200000 | tf_op jit(solution)/shard_map/pallas_call | solution.py:338
  13.9 2.5 %all-to-all-done.got_ref = bf16[8,32,128]{2,1,0:T(8,128)(2,1)S(1)} async-done(((bf16[8,32,128]{2,1,0:T(8,128)(2,1)}), bf16[8,32,128]{2,1,0:T(8,128)(2,1)S(1)}, u32[]{:S(2)}, u32[]{:S(2)}) %all-to-all-start) | async-done | bytes 65568 | tf_op jit(solution)/shard_map/all_to_all | solution.py:328
  16.4 0.0 copy-done.2
  16.5 1.5 %shard_map.113 = (f32[32,960]{1,0:T(8,128)S(1)}, bf16[64,640]{1,0:T(8,128)(2,1)S(1)}, bf16[32,640]{1,0:T(8,128)(2,1)S(1)}, bf16[576,640]{1,0:T(8,128)(2,1)S(1)},...) custom-call(bf16[8,32,128]{2,1,0:T(8,128)(2,1)S(1)} %all-to-all-done.got_ref, ...), custom_call_target="tpu_custom_call" | custom-call | flops 1000000 | bytes 200000 | tf_op jit(solution)/shard_map/pallas_call | solution.py:351
  17.9 0.0 collective-permute-done.flat_ref
  17.9 0.8 %shard_map.114 = (bf16[16,1024]{1,0:T(8,128)(2,1)S(1)}, bf16[16,1024]{1,0:T(8,128)(2,1)S(1)}) custom-call(f32[32,960]{1,0:T(8,128)S(1)} %get-tuple-element.29.sums_ref, bf16[576,640]{1,0:T(8,128)(2,1)S(1)} %get-tuple-element.30.taps_ref, bf16[32,640]{1,0:T(8,128)(2,1)S(1)} %get-tuple-element.31.hidden_ref, f32[32,640]{1,0:T(8,128)S(1)} %get-tuple-element.32.slope_ref, ...), custom_call_target="tpu_custom_call" | custom-call | flops 1000000 | bytes 200000 | tf_op jit(solution)/shard_map/pallas_call | solution.py:366
  18.8 0.1 collective-permute-start.1
  18.8 1.6 %collective-permute-start.3 = (bf16[16,1024]{1,0:T(8,128)(2,1)S(1)}, bf16[16,1024]{1,0:T(8,128)(2,1)S(1)}, u32[]{:S(2)}, u32[]{:S(2)}) collective-permute-start(bf16[16,1024]{1,0:T(8,128)(2,1)S(1)} %get-tuple-element.34), channel_id=1, source_target_pairs={{0,16},{1,17},{2,18},{3,19},{4,20},{5,21},{6,22},{7,23},{8,24},{9,... | collective-permute-start | bytes 98312 | tf_op jit(solution)/shard_map/ppermute | solution.py:280
  20.4 0.3 collective-permute-start.2
  20.7 1.8 %collective-permute-done.1 = bf16[16,1024]{1,0:T(8,128)(2,1)S(1)} collective-permute-done((bf16[16,1024]{1,0:T(8,128)(2,1)S(1)}, bf16[16,1024]{1,0:T(8,128)(2,1)S(1)}, u32[]{:S(2)}, u32[]{:S(2)}) %collective-permute-start.1) | collective-permute-done | bytes 32800 | tf_op jit(solution)/shard_map/ppermute | solution.py:280
  22.4 0.4 %collective-permute-done.3 = bf16[16,1024]{1,0:T(8,128)(2,1)S(1)} collective-permute-done((bf16[16,1024]{1,0:T(8,128)(2,1)S(1)}, bf16[16,1024]{1,0:T(8,128)(2,1)S(1)}, u32[]{:S(2)}, u32[]{:S(2)}) %collective-permute-start.3) | collective-permute-done | bytes 32800 | tf_op jit(solution)/shard_map/ppermute | solution.py:280
  22.9 0.0 collective-permute-done.2
  22.9 0.0 copy-start.4
  22.9 0.7 %collective-permute-start.6 = (bf16[16,1024]{1,0:T(8,128)(2,1)S(1)}, bf16[16,1024]{1,0:T(8,128)(2,1)S(1)}, u32[]{:S(2)}, u32[]{:S(2)}) collective-permute-start(bf16[16,1024]{1,0:T(8,128)(2,1)S(1)} %add_convert_fusion), channel_id=1, source_target_pairs={{0,3},{1,2},{2,1},{3,0},{4,7},{5,6},{6,5},{7,4},{8,11},{9,10},{10,... | collective-permute-start | bytes 98312 | tf_op jit(solution)/shard_map/ppermute | solution.py:280
  23.6 0.7 %collective-permute-start.5 = (bf16[16,1024]{1,0:T(8,128)(2,1)S(1)}, bf16[16,1024]{1,0:T(8,128)(2,1)S(1)}, u32[]{:S(2)}, u32[]{:S(2)}) collective-permute-start(bf16[16,1024]{1,0:T(8,128)(2,1)S(1)} %add_convert_fusion), channel_id=1, source_target_pairs={{0,9},{1,8},{2,11},{3,10},{4,13},{5,12},{6,15},{7,14},{8,1},{9,0},... | collective-permute-start | bytes 98312 | tf_op jit(solution)/shard_map/ppermute | solution.py:280
  24.3 1.9 %collective-permute-start.4 = (bf16[16,1024]{1,0:T(8,128)(2,1)S(1)}, bf16[16,1024]{1,0:T(8,128)(2,1)S(1)}, u32[]{:S(2)}, u32[]{:S(2)}) collective-permute-start(bf16[16,1024]{1,0:T(8,128)(2,1)S(1)} %add_convert_fusion), channel_id=1, source_target_pairs={{0,10},{1,11},{2,8},{3,9},{4,14},{5,15},{6,12},{7,13},{8,2},{9,3},... | collective-permute-start | bytes 98312 | tf_op jit(solution)/shard_map/ppermute | solution.py:280
  26.2 0.0 copy-done.4
  26.2 1.2 %shard_map.115 = bf16[32,16,32]{2,1,0:T(8,128)(2,1)} custom-call(bf16[32,640]{1,0:T(8,128)(2,1)S(1)} %get-tuple-element.35.hidden_ref, bf16[64,640]{1,0:T(8,128)(2,1)S(1)} %get-tuple-element.36.up_ref, bf16[3,3,32,32]{3,2,1,0:T(8,128)(2,1)S(1)} %copy-done, bf16[32,64]{1,0:T(8,128)(2,1)S(1)} %bitcast.17, f32[1,33]{1,0:T(1,128)S(1)} %maximum_bitcast_fusion.row_ref), custom_call_target="tpu_custom_call" | custom-call | flops 1000000 | bytes 200000 | tf_op jit(solution)/shard_map/pallas_call | solution.py:373
  27.4 0.4 %collective-permute-done.6 = bf16[16,1024]{1,0:T(8,128)(2,1)S(1)} collective-permute-done((bf16[16,1024]{1,0:T(8,128)(2,1)S(1)}, bf16[16,1024]{1,0:T(8,128)(2,1)S(1)}, u32[]{:S(2)}, u32[]{:S(2)}) %collective-permute-start.6) | collective-permute-done | bytes 32800 | tf_op jit(solution)/shard_map/ppermute | solution.py:280
  27.8 0.0 collective-permute-done.5
  27.8 0.0 collective-permute-done.4
  27.9 0.3 %collective-permute-start.7 = (f32[16,1024]{1,0:T(8,128)S(1)}, f32[16,1024]{1,0:T(8,128)S(1)}, u32[]{:S(2)}, u32[]{:S(2)}) collective-permute-start(f32[16,1024]{1,0:T(8,128)S(1)} %add_add_fusion.mine_ref), channel_id=1, source_target_pairs={{0,8},{1,9},{2,10},{3,11},{4,12},{5,13},{6,14},{7,15},{8,0},{9,1},... | collective-permute-start | bytes 196616 | tf_op jit(solution)/shard_map/ppermute | solution.py:280
  28.2 1.0 %collective-permute-done.7.other_ref = f32[16,1024]{1,0:T(8,128)S(1)} collective-permute-done((f32[16,1024]{1,0:T(8,128)S(1)}, f32[16,1024]{1,0:T(8,128)S(1)}, u32[]{:S(2)}, u32[]{:S(2)}) %collective-permute-start.7) | collective-permute-done | bytes 65568 | tf_op jit(solution)/shard_map/ppermute | solution.py:280
  29.2 0.8 %shard_map.116 = (f32[3,3,32,64]{3,2,1,0:T(8,128)}, f32[1,32]{1,0:T(1,128)}, f32[3,3,32,32]{3,2,1,0:T(8,128)}, f32[32,64]{1,0:T(8,128)}) custom-call(f32[16,1024]{1,0:T(8,128)S(1)} %add_add_fusion.mine_ref, f32[16,1024]{1,0:T(8,128)S(1)} %collective-permute-done.7.other_ref), custom_call_target="tpu_custom_call" | custom-call | flops 1000000 | bytes 200000 | tf_op jit(solution)/shard_map/pallas_call | solution.py:383
  (2 shorter events, 0.0 us)
Async XLA Ops:
  0.6 8.9 %copy-start.1 = (bf16[1,32,32,16]{2,3,1,0:T(8,128)(2,1)S(1)}, bf16[1,32,32,16]{2,3,1,0:T(8,128)(2,1)}, u32[]{:S(2)}) copy-start(bf16[1,32,32,16]{2,3,1,0:T(8,128)(2,1)} %param.13) | copy-start | bytes 98308
  0.6 0.8 %copy-start.3 = (bf16[1,64,1,128]{3,1,2,0:T(8,128)(2,1)S(1)}, bf16[1,64,1,128]{3,1,2,0:T(8,128)(2,1)}, u32[]{:S(2)}) copy-start(bf16[1,64,1,128]{3,1,2,0:T(8,128)(2,1)} %param.7) | copy-start | bytes 49156
  2.3 14.2 %all-to-all-start = ((bf16[8,32,128]{2,1,0:T(8,128)(2,1)}), bf16[8,32,128]{2,1,0:T(8,128)(2,1)S(1)}, u32[]{:S(2)}, u32[]{:S(2)}) async-start(bf16[8,32,128]{2,1,0:T(8,128)(2,1)} %shard_map.110), calls=%async_computation | async-start | bytes 131072 | tf_op jit(solution)/shard_map/all_to_all | solution.py:328
  9.5 3.8 %copy-start.5 = (f32[32]{0:T(128)S(1)}, f32[32]{0:T(128)}, u32[]{:S(2)}) copy-start(f32[32]{0:T(128)} %param.9) | copy-start | bytes 388
  9.6 3.9 %copy-start = (bf16[3,3,32,32]{3,2,1,0:T(8,128)(2,1)S(1)}, bf16[3,3,32,32]{3,2,1,0:T(8,128)(2,1)}, u32[]{:S(2)}) copy-start(bf16[3,3,32,32]{3,2,1,0:T(8,128)(2,1)} %ws_ref.5) | copy-start | bytes 55300
  9.8 6.7 %copy-start.2 = (bf16[3,3,64,32]{2,3,1,0:T(8,128)(2,1)S(1)}, bf16[3,3,64,32]{2,3,1,0:T(8,128)(2,1)}, u32[]{:S(2)}) copy-start(bf16[3,3,64,32]{2,3,1,0:T(8,128)(2,1)} %param.8) | copy-start | bytes 110596
  9.8 8.2 %collective-permute-start = (bf16[32,640]{1,0:T(8,128)(2,1)S(1)}, bf16[32,640]{1,0:T(8,128)(2,1)S(1)}, u32[]{:S(2)}, u32[]{:S(2)}) collective-permute-start(bf16[32,640]{1,0:T(8,128)(2,1)S(1)} %shard_map.111.flat_ref), channel_id=1, source_target_pairs={{0,4},{1,5},{2,6},{3,7},{4,0},{5,1},{6,2},{7,3},{8,12},{9,13},{10,... | collective-permute-start | bytes 122888 | tf_op jit(solution)/shard_map/ppermute | solution.py:280
  18.8 3.7 %collective-permute-start.1 = (bf16[16,1024]{1,0:T(8,128)(2,1)S(1)}, bf16[16,1024]{1,0:T(8,128)(2,1)S(1)}, u32[]{:S(2)}, u32[]{:S(2)}) collective-permute-start(bf16[16,1024]{1,0:T(8,128)(2,1)S(1)} %get-tuple-element.33), channel_id=1, source_target_pairs={{0,24},{1,25},{2,26},{3,27},{4,28},{5,29},{6,30},{7,31},{8,16},{9,... | collective-permute-start | bytes 98312 | tf_op jit(solution)/shard_map/ppermute | solution.py:280
  18.8 4.0 %collective-permute-start.3 = (bf16[16,1024]{1,0:T(8,128)(2,1)S(1)}, bf16[16,1024]{1,0:T(8,128)(2,1)S(1)}, u32[]{:S(2)}, u32[]{:S(2)}) collective-permute-start(bf16[16,1024]{1,0:T(8,128)(2,1)S(1)} %get-tuple-element.34), channel_id=1, source_target_pairs={{0,16},{1,17},{2,18},{3,19},{4,20},{5,21},{6,22},{7,23},{8,24},{9,... | collective-permute-start | bytes 98312 | tf_op jit(solution)/shard_map/ppermute | solution.py:280
  20.4 2.4 %collective-permute-start.2 = (bf16[16,1024]{1,0:T(8,128)(2,1)S(1)}, bf16[16,1024]{1,0:T(8,128)(2,1)S(1)}, u32[]{:S(2)}, u32[]{:S(2)}) collective-permute-start(bf16[16,1024]{1,0:T(8,128)(2,1)S(1)} %get-tuple-element.34), channel_id=1, source_target_pairs={{0,8},{1,9},{2,10},{3,11},{4,12},{5,13},{6,14},{7,15},{8,0},{9,1},... | collective-permute-start | bytes 98312 | tf_op jit(solution)/shard_map/ppermute | solution.py:280
  22.9 3.3 %copy-start.4 = (bf16[64,32]{0,1:T(8,128)(2,1)S(1)}, bf16[64,32]{0,1:T(8,128)(2,1)}, u32[]{:S(2)}) copy-start(bf16[64,32]{0,1:T(8,128)(2,1)} %param.11) | copy-start | bytes 12292
  22.9 4.9 %collective-permute-start.6 = (bf16[16,1024]{1,0:T(8,128)(2,1)S(1)}, bf16[16,1024]{1,0:T(8,128)(2,1)S(1)}, u32[]{:S(2)}, u32[]{:S(2)}) collective-permute-start(bf16[16,1024]{1,0:T(8,128)(2,1)S(1)} %add_convert_fusion), channel_id=1, source_target_pairs={{0,3},{1,2},{2,1},{3,0},{4,7},{5,6},{6,5},{7,4},{8,11},{9,10},{10,... | collective-permute-start | bytes 98312 | tf_op jit(solution)/shard_map/ppermute | solution.py:280
  23.6 4.2 %collective-permute-start.5 = (bf16[16,1024]{1,0:T(8,128)(2,1)S(1)}, bf16[16,1024]{1,0:T(8,128)(2,1)S(1)}, u32[]{:S(2)}, u32[]{:S(2)}) collective-permute-start(bf16[16,1024]{1,0:T(8,128)(2,1)S(1)} %add_convert_fusion), channel_id=1, source_target_pairs={{0,9},{1,8},{2,11},{3,10},{4,13},{5,12},{6,15},{7,14},{8,1},{9,0},... | collective-permute-start | bytes 98312 | tf_op jit(solution)/shard_map/ppermute | solution.py:280
  24.3 3.5 %collective-permute-start.4 = (bf16[16,1024]{1,0:T(8,128)(2,1)S(1)}, bf16[16,1024]{1,0:T(8,128)(2,1)S(1)}, u32[]{:S(2)}, u32[]{:S(2)}) collective-permute-start(bf16[16,1024]{1,0:T(8,128)(2,1)S(1)} %add_convert_fusion), channel_id=1, source_target_pairs={{0,10},{1,11},{2,8},{3,9},{4,14},{5,15},{6,12},{7,13},{8,2},{9,3},... | collective-permute-start | bytes 98312 | tf_op jit(solution)/shard_map/ppermute | solution.py:280
  27.9 1.3 %collective-permute-start.7 = (f32[16,1024]{1,0:T(8,128)S(1)}, f32[16,1024]{1,0:T(8,128)S(1)}, u32[]{:S(2)}, u32[]{:S(2)}) collective-permute-start(f32[16,1024]{1,0:T(8,128)S(1)} %add_add_fusion.mine_ref), channel_id=1, source_target_pairs={{0,8},{1,9},{2,10},{3,11},{4,12},{5,13},{6,14},{7,15},{8,0},{9,1},... | collective-permute-start | bytes 196616 | tf_op jit(solution)/shard_map/ppermute | solution.py:280

commit v7 on v6

--- a/solution.py
+++ b/solution.py
@@ -44,23 +44,26 @@
         self.wide = up128(self.lanes + 2 * self.pitch + 2)
 
 
-def pack_kernel(z, coarse_ref, out_ref):
-    row = coarse_ref[...]
-    count = z.tiles * 2 * ROWS
+def pick_kernel(z, pick_ref):
+    count = z.tiles * ROWS
     at = ints((count, z.coarse_cols), 0)
     col = ints((count, z.coarse_cols), 1)
-    dest = lax.shift_right_logical(at, 5)
-    strip = lax.bitwise_and(lax.shift_right_logical(at, 4), 1)
-    tile = dest ^ (strip * z.pair)
     slot = lax.bitwise_and(at, ROWS - 1)
-    parts = []
+    want = lax.shift_right_logical(at, 4) * z.own_coarse - 2 + slot
     for half in range(2):
-        want = tile * z.own_coarse - 2 + half * z.half + slot
-        want = jnp.clip(want, 0, z.coarse_cols - 1)
-        pick = jnp.where((want == col) & (slot < z.half), 1.0, 0.0).astype(BF16)
-        parts.append(lax.dot_general(pick, row, NT, preferred_element_type=F32))
-    packed = jnp.concatenate(parts, axis=1).astype(BF16)
-    out_ref[...] = packed.reshape(out_ref.shape)
+        here = jnp.clip(want + half * z.half, 0, z.coarse_cols - 1)
+        pick_ref[half] = jnp.where((here == col) & (slot < z.half), 1.0, 0.0).astype(BF16)
+
+
+def pack_kernel(z, coarse_ref, pick_ref, out_ref):
+    row = coarse_ref[...]
+    parts = [
+        lax.dot_general(pick_ref[half], row, NT, preferred_element_type=F32) for half in range(2)
+    ]
+    packed = jnp.concatenate(parts, axis=1).astype(BF16).reshape(z.tiles, ROWS, 2 * z.cin)
+    out_ref[:, :ROWS, :] = packed
+    out_ref[: z.pair, ROWS:, :] = packed[z.pair :]
+    out_ref[z.pair :, ROWS:, :] = packed[: z.pair]
 
 
 def interpolation(z, interp_ref):
@@ -104,15 +107,15 @@
     blend = row_ref[:, z.cout :]
     flat = flat_ref[...].astype(F32)
     d_skip = (flat * ((1.0 - blend) * scale)).astype(BF16)
-    d_second = (flat * (blend * scale)).astype(BF16).astype(F32)
-    d_second = jnp.concatenate([d_second, jnp.zeros((z.cout, z.wide - z.lanes), F32)], axis=1)
+    d_second = (flat * (blend * scale)).astype(BF16)
+    d_second = jnp.concatenate([d_second, jnp.zeros((z.cout, z.wide - z.lanes), BF16)], axis=1)
     back = []
     for p in range(3):
         for q in range(3):
             shift = (q - 1) * z.pitch + p - 1
             moved = d_second if shift == 0 else pltpu.roll(d_second, shift % z.wide, 1)
             k = (p * 3 + q) * z.cout
-            spread_ref[k : k + z.cout, :] = moved[:, : z.lanes].astype(BF16)
+            spread_ref[k : k + z.cout, :] = moved[:, : z.lanes]
             back.append(ws_ref[p, q])
     d_hidden = jnp.dot(
         jnp.concatenate(back, axis=1), spread_ref[...], preferred_element_type=F32
@@ -144,9 +147,11 @@
 
 def gradients(z, d_hidden, d_skip, spread, slope, hidden, taps, centre):
     d_pre = (d_hidden * slope).astype(BF16)
-    first = lax.dot_general(d_pre, taps, NT, preferred_element_type=F32)
+    stacked = jnp.concatenate([d_pre, d_skip], axis=0)
+    products = lax.dot_general(stacked, taps, NT, preferred_element_type=F32)
+    first = products[: z.cout]
+    skip = products[z.cout :, 4 * z.cin : 5 * z.cin]
     second = lax.dot_general(hidden, spread, NT, preferred_element_type=F32)
-    skip = lax.dot_general(d_skip, centre, NT, preferred_element_type=F32)
     ones = jnp.ones((z.cout, z.lanes), BF16)
     biases = lax.dot_general(ones, d_pre, NT, preferred_element_type=F32)
     return jnp.concatenate([first, second, skip, biases], axis=1)
@@ -171,20 +176,20 @@
         up = jnp.dot(windows, interp_ref[...], preferred_element_type=F32)
         column = tile * z.width + w
         inside = jnp.where((column >= 0) & (column < z.width * z.tiles), 1.0, 0.0)
-        up = (up * inside).astype(BF16).astype(F32)
+        up = (up * inside).astype(BF16)
         for p in range(3):
             for q in range(3):
                 start = q * z.pitch + p
                 moved = up if start == 0 else pltpu.roll(up, z.wide - start, 1)
                 k = (p * 3 + q) * z.cin
-                here_ref[k : k + z.cin, :] = moved[:, : z.lanes].astype(BF16)
+                here_ref[k : k + z.cin, :] = moved[:, : z.lanes]
         column = tile * z.width + mw
         inside = (mw >= -1) & (mw <= z.width) & (mh < z.height)
         inside = inside & (column >= 0) & (column < z.width * z.tiles)
         inside = jnp.where(inside, 1.0, 0.0)
         taps = here_ref[...]
         pre = jnp.dot(kernel, taps, preferred_element_type=F32) + bias_ref[...]
-        sigma = 1.0 / (1.0 + jnp.exp(-pre))
+        sigma = 0.5 * jnp.tanh(0.5 * pre) + 0.5
         hidden = (pre * sigma * inside).astype(BF16)
         slope = sigma * (1.0 + pre * (1.0 - sigma)) * inside
         if s == 0:
@@ -322,9 +327,10 @@
     total_count = coarse.shape[0] * images * z.width * tiles * z.height
     scale = float(total_count) ** (-0.5)
 
+    picks = call(functools.partial(pick_kernel, z), bf(2, tiles * ROWS, z.coarse_cols), [])()
     packed = call(
-        functools.partial(pack_kernel, z), bf(tiles, 2 * ROWS, 2 * z.cin), [vmem]
-    )(coarse.reshape(z.cin, z.coarse_cols))
+        functools.partial(pack_kernel, z), bf(tiles, 2 * ROWS, 2 * z.cin), [vmem] * 2
+    )(coarse.reshape(z.cin, z.coarse_cols), picks)
     got = lax.all_to_all(packed, "tile", split_axis=0, concat_axis=0, tiled=True)
 
     flat = call(

time: 30.4 us -> 30.2 us (level)
  no operation moved by 1% of the time
where the time goes in v7:
time: 30.2 us; the launch traced here: 29.8 us
  starting transfers between devices  15.8 us (52%)
  waiting for transfers between devices  6.15 us (20%)
  Pallas kernels  5.72 us (19%)
  between operations  1.39 us (5%)
  local copies, waits for them, and re-layouts  0.68 us (2%)
    ppermute x8, starting transfers between devices, swap(): return lax.ppermute(values, ('img', 'tile'), pairs)  8.5 us
    all_to_all x1, starting transfers between devices, local(): lax.all_to_all(packed, 'tile', split_axis=0, concat_axis=0, tiled=True)  7.25 us
    ppermute x8, waiting for transfers between devices, swap(): return lax.ppermute(values, ('img', 'tile'), pairs)  3.59 us
    all_to_all x1, waiting for transfers between devices, local(): lax.all_to_all(packed, 'tile', split_axis=0, concat_axis=0, tiled=True)  2.56 us
    pallas_call x1, Pallas kernels, local(): call(functools.partial(forward_kernel, z), (f32(z.cout, used), bf(z.cin,...  1.39 us
    pallas_call x1, Pallas kernels, local(): call(functools.partial(blend_kernel, z), bf(z.cout, z.height, z.width), [...  1.24 us
    pallas_call x1, Pallas kernels, local(): call(functools.partial(pack_kernel, z), bf(tiles, 2 * ROWS, 2 * z.cin), [...  0.85 us
    pallas_call x1, Pallas kernels, local(): call(functools.partial(finish_kernel, z), (f32(3, 3, z.cout, z.cin), f32(...  0.81 us
  transfers between devices with their start and end apart: 9, of which 5 were waited for; matrix products, arithmetic and copies ran while one was open for 0% of the time, Pallas kernels for 11%

profile of v7, /device:TPU:0, one launch (start us, length us, event | category | flops | bytes accessed | tf_op | source)
XLA Modules:
  0.0 29.8 jit_solution(163631558314736835)
XLA Ops:
  0.6 0.0 copy-start.3
  0.7 0.7 %copy-done.3 = bf16[1,64,1,128]{3,1,2,0:T(8,128)(2,1)S(1)} copy-done((bf16[1,64,1,128]{3,1,2,0:T(8,128)(2,1)S(1)}, bf16[1,64,1,128]{3,1,2,0:T(8,128)(2,1)}, u32[]{:S(2)}) %copy-start.3) | copy-done | bytes 16408
  1.3 0.0 copy-start.1
  1.4 0.8 %shard_map.111 = bf16[8,32,128]{2,1,0:T(8,128)(2,1)} custom-call(bf16[64,128]{1,0:T(8,128)(2,1)S(1)} %bitcast.16, bf16[2,128,128]{2,1,0:T(8,128)(2,1)S(1)} %shard_map.110.pick_ref), custom_call_target="tpu_custom_call" | custom-call | flops 1000000 | bytes 200000 | tf_op jit(solution)/shard_map/pallas_call | solution.py:331
  2.2 7.3 %all-to-all-start = ((bf16[8,32,128]{2,1,0:T(8,128)(2,1)}), bf16[8,32,128]{2,1,0:T(8,128)(2,1)S(1)}, u32[]{:S(2)}, u32[]{:S(2)}) async-start(bf16[8,32,128]{2,1,0:T(8,128)(2,1)} %shard_map.111), calls=%async_computation | async-start | bytes 131072 | tf_op jit(solution)/shard_map/all_to_all | solution.py:334
  9.5 0.0 copy-done.1
  9.5 0.0 copy-start.5
  9.5 0.0 copy-start
  9.5 0.2 shard_map.112.flat_ref
  9.7 0.0 copy-start.2
  9.7 3.0 %collective-permute-start = (bf16[32,640]{1,0:T(8,128)(2,1)S(1)}, bf16[32,640]{1,0:T(8,128)(2,1)S(1)}, u32[]{:S(2)}, u32[]{:S(2)}) collective-permute-start(bf16[32,640]{1,0:T(8,128)(2,1)S(1)} %shard_map.112.flat_ref), channel_id=1, source_target_pairs={{0,4},{1,5},{2,6},{3,7},{4,0},{5,1},{6,2},{7,3},{8,12},{9,13},{10,... | collective-permute-start | bytes 122888 | tf_op jit(solution)/shard_map/ppermute | solution.py:285
  13.3 0.0 copy-done.5
  13.3 0.1 maximum_bitcast_fusion.row_ref
  13.4 0.0 copy-done
  13.4 0.4 %shard_map.113 = (f32[32,640]{1,0:T(8,128)S(1)}, bf16[288,640]{1,0:T(8,128)(2,1)S(1)}, bf16[32,640]{1,0:T(8,128)(2,1)S(1)}, bf16[256,768]{1,0:T(8,128)(2,1)S(1)}, f32[32,1]{1,0:T(8,128)S(1)}) custom-call(bf16[32,640]{1,0:T(8,128)(2,1)S(1)} %shard_map.112.flat_ref, bf16[3,3,32,32]{3,2,1,0:T(8,128)(2,1)S(1)} %copy-done, f32[1,33]{1,0:T(1,128)S(1)} %maximum_bitcast_fusion.row_ref), custom_call_target="tpu_custom_call" | custom-call | flops 1000000 | bytes 200000 | tf_op jit(solution)/shard_map/pallas_call | solution.py:344
  13.8 2.6 %all-to-all-done.got_ref = bf16[8,32,128]{2,1,0:T(8,128)(2,1)S(1)} async-done(((bf16[8,32,128]{2,1,0:T(8,128)(2,1)}), bf16[8,32,128]{2,1,0:T(8,128)(2,1)S(1)}, u32[]{:S(2)}, u32[]{:S(2)}) %all-to-all-start) | async-done | bytes 65568 | tf_op jit(solution)/shard_map/all_to_all | solution.py:334
  16.4 0.0 copy-done.2
  16.4 1.4 %shard_map.114 = (f32[32,960]{1,0:T(8,128)S(1)}, bf16[64,640]{1,0:T(8,128)(2,1)S(1)}, bf16[32,640]{1,0:T(8,128)(2,1)S(1)}, bf16[576,640]{1,0:T(8,128)(2,1)S(1)},...) custom-call(bf16[8,32,128]{2,1,0:T(8,128)(2,1)S(1)} %all-to-all-done.got_ref, ...), custom_call_target="tpu_custom_call" | custom-call | flops 1000000 | bytes 200000 | tf_op jit(solution)/shard_map/pallas_call | solution.py:357
  17.8 0.0 collective-permute-done.flat_ref
  17.8 0.8 %shard_map.115 = (bf16[16,1024]{1,0:T(8,128)(2,1)S(1)}, bf16[16,1024]{1,0:T(8,128)(2,1)S(1)}) custom-call(f32[32,960]{1,0:T(8,128)S(1)} %get-tuple-element.29.sums_ref, bf16[576,640]{1,0:T(8,128)(2,1)S(1)} %get-tuple-element.30.taps_ref, bf16[32,640]{1,0:T(8,128)(2,1)S(1)} %get-tuple-element.31.hidden_ref, f32[32,640]{1,0:T(8,128)S(1)} %get-tuple-element.32.slope_ref, ...), custom_call_target="tpu_custom_call" | custom-call | flops 1000000 | bytes 200000 | tf_op jit(solution)/shard_map/pallas_call | solution.py:372
  18.6 0.1 collective-permute-start.1
  18.7 1.6 %collective-permute-start.3 = (bf16[16,1024]{1,0:T(8,128)(2,1)S(1)}, bf16[16,1024]{1,0:T(8,128)(2,1)S(1)}, u32[]{:S(2)}, u32[]{:S(2)}) collective-permute-start(bf16[16,1024]{1,0:T(8,128)(2,1)S(1)} %get-tuple-element.34), channel_id=1, source_target_pairs={{0,16},{1,17},{2,18},{3,19},{4,20},{5,21},{6,22},{7,23},{8,24},{9,... | collective-permute-start | bytes 98312 | tf_op jit(solution)/shard_map/ppermute | solution.py:285
  20.2 0.3 collective-permute-start.2
  20.5 1.8 %collective-permute-done.1 = bf16[16,1024]{1,0:T(8,128)(2,1)S(1)} collective-permute-done((bf16[16,1024]{1,0:T(8,128)(2,1)S(1)}, bf16[16,1024]{1,0:T(8,128)(2,1)S(1)}, u32[]{:S(2)}, u32[]{:S(2)}) %collective-permute-start.1) | collective-permute-done | bytes 32800 | tf_op jit(solution)/shard_map/ppermute | solution.py:285
  22.3 0.4 %collective-permute-done.3 = bf16[16,1024]{1,0:T(8,128)(2,1)S(1)} collective-permute-done((bf16[16,1024]{1,0:T(8,128)(2,1)S(1)}, bf16[16,1024]{1,0:T(8,128)(2,1)S(1)}, u32[]{:S(2)}, u32[]{:S(2)}) %collective-permute-start.3) | collective-permute-done | bytes 32800 | tf_op jit(solution)/shard_map/ppermute | solution.py:285
  22.7 0.0 collective-permute-done.2
  22.7 0.0 copy-start.4
  22.7 0.7 %collective-permute-start.6 = (bf16[16,1024]{1,0:T(8,128)(2,1)S(1)}, bf16[16,1024]{1,0:T(8,128)(2,1)S(1)}, u32[]{:S(2)}, u32[]{:S(2)}) collective-permute-start(bf16[16,1024]{1,0:T(8,128)(2,1)S(1)} %add_convert_fusion), channel_id=1, source_target_pairs={{0,3},{1,2},{2,1},{3,0},{4,7},{5,6},{6,5},{7,4},{8,11},{9,10},{10,... | collective-permute-start | bytes 98312 | tf_op jit(solution)/shard_map/ppermute | solution.py:285
  23.4 0.7 %collective-permute-start.5 = (bf16[16,1024]{1,0:T(8,128)(2,1)S(1)}, bf16[16,1024]{1,0:T(8,128)(2,1)S(1)}, u32[]{:S(2)}, u32[]{:S(2)}) collective-permute-start(bf16[16,1024]{1,0:T(8,128)(2,1)S(1)} %add_convert_fusion), channel_id=1, source_target_pairs={{0,9},{1,8},{2,11},{3,10},{4,13},{5,12},{6,15},{7,14},{8,1},{9,0},... | collective-permute-start | bytes 98312 | tf_op jit(solution)/shard_map/ppermute | solution.py:285
  24.1 1.9 %collective-permute-start.4 = (bf16[16,1024]{1,0:T(8,128)(2,1)S(1)}, bf16[16,1024]{1,0:T(8,128)(2,1)S(1)}, u32[]{:S(2)}, u32[]{:S(2)}) collective-permute-start(bf16[16,1024]{1,0:T(8,128)(2,1)S(1)} %add_convert_fusion), channel_id=1, source_target_pairs={{0,10},{1,11},{2,8},{3,9},{4,14},{5,15},{6,12},{7,13},{8,2},{9,3},... | collective-permute-start | bytes 98312 | tf_op jit(solution)/shard_map/ppermute | solution.py:285
  26.0 0.0 copy-done.4
  26.0 1.2 %shard_map.116 = bf16[32,16,32]{2,1,0:T(8,128)(2,1)} custom-call(bf16[32,640]{1,0:T(8,128)(2,1)S(1)} %get-tuple-element.35.hidden_ref, bf16[64,640]{1,0:T(8,128)(2,1)S(1)} %get-tuple-element.36.up_ref, bf16[3,3,32,32]{3,2,1,0:T(8,128)(2,1)S(1)} %copy-done, bf16[32,64]{1,0:T(8,128)(2,1)S(1)} %bitcast.17, f32[1,33]{1,0:T(1,128)S(1)} %maximum_bitcast_fusion.row_ref), custom_call_target="tpu_custom_call" | custom-call | flops 1000000 | bytes 200000 | tf_op jit(solution)/shard_map/pallas_call | solution.py:379
  27.2 0.4 %collective-permute-done.6 = bf16[16,1024]{1,0:T(8,128)(2,1)S(1)} collective-permute-done((bf16[16,1024]{1,0:T(8,128)(2,1)S(1)}, bf16[16,1024]{1,0:T(8,128)(2,1)S(1)}, u32[]{:S(2)}, u32[]{:S(2)}) %collective-permute-start.6) | collective-permute-done | bytes 32800 | tf_op jit(solution)/shard_map/ppermute | solution.py:285
  27.7 0.0 collective-permute-done.5
  27.7 0.0 collective-permute-done.4
  27.7 0.3 %collective-permute-start.7 = (f32[16,1024]{1,0:T(8,128)S(1)}, f32[16,1024]{1,0:T(8,128)S(1)}, u32[]{:S(2)}, u32[]{:S(2)}) collective-permute-start(f32[16,1024]{1,0:T(8,128)S(1)} %add_add_fusion.mine_ref), channel_id=1, source_target_pairs={{0,8},{1,9},{2,10},{3,11},{4,12},{5,13},{6,14},{7,15},{8,0},{9,1},... | collective-permute-start | bytes 196616 | tf_op jit(solution)/shard_map/ppermute | solution.py:285
  28.0 1.0 %collective-permute-done.7.other_ref = f32[16,1024]{1,0:T(8,128)S(1)} collective-permute-done((f32[16,1024]{1,0:T(8,128)S(1)}, f32[16,1024]{1,0:T(8,128)S(1)}, u32[]{:S(2)}, u32[]{:S(2)}) %collective-permute-start.7) | collective-permute-done | bytes 65568 | tf_op jit(solution)/shard_map/ppermute | solution.py:285
  29.0 0.8 %shard_map.117 = (f32[3,3,32,64]{3,2,1,0:T(8,128)}, f32[1,32]{1,0:T(1,128)}, f32[3,3,32,32]{3,2,1,0:T(8,128)}, f32[32,64]{1,0:T(8,128)}) custom-call(f32[16,1024]{1,0:T(8,128)S(1)} %add_add_fusion.mine_ref, f32[16,1024]{1,0:T(8,128)S(1)} %collective-permute-done.7.other_ref), custom_call_target="tpu_custom_call" | custom-call | flops 1000000 | bytes 200000 | tf_op jit(solution)/shard_map/pallas_call | solution.py:389
  (3 shorter events, 0.1 us)
Async XLA Ops:
  0.6 0.7 %copy-start.3 = (bf16[1,64,1,128]{3,1,2,0:T(8,128)(2,1)S(1)}, bf16[1,64,1,128]{3,1,2,0:T(8,128)(2,1)}, u32[]{:S(2)}) copy-start(bf16[1,64,1,128]{3,1,2,0:T(8,128)(2,1)} %param.7) | copy-start | bytes 49156
  1.3 8.1 %copy-start.1 = (bf16[1,32,32,16]{2,3,1,0:T(8,128)(2,1)S(1)}, bf16[1,32,32,16]{2,3,1,0:T(8,128)(2,1)}, u32[]{:S(2)}) copy-start(bf16[1,32,32,16]{2,3,1,0:T(8,128)(2,1)} %param.13) | copy-start | bytes 98308
  2.2 14.2 %all-to-all-start = ((bf16[8,32,128]{2,1,0:T(8,128)(2,1)}), bf16[8,32,128]{2,1,0:T(8,128)(2,1)S(1)}, u32[]{:S(2)}, u32[]{:S(2)}) async-start(bf16[8,32,128]{2,1,0:T(8,128)(2,1)} %shard_map.111), calls=%async_computation | async-start | bytes 131072 | tf_op jit(solution)/shard_map/all_to_all | solution.py:334
  9.5 3.8 %copy-start.5 = (f32[32]{0:T(128)S(1)}, f32[32]{0:T(128)}, u32[]{:S(2)}) copy-start(f32[32]{0:T(128)} %param.9) | copy-start | bytes 388
  9.5 3.9 %copy-start = (bf16[3,3,32,32]{3,2,1,0:T(8,128)(2,1)S(1)}, bf16[3,3,32,32]{3,2,1,0:T(8,128)(2,1)}, u32[]{:S(2)}) copy-start(bf16[3,3,32,32]{3,2,1,0:T(8,128)(2,1)} %ws_ref.5) | copy-start | bytes 55300
  9.7 6.7 %copy-start.2 = (bf16[3,3,64,32]{2,3,1,0:T(8,128)(2,1)S(1)}, bf16[3,3,64,32]{2,3,1,0:T(8,128)(2,1)}, u32[]{:S(2)}) copy-start(bf16[3,3,64,32]{2,3,1,0:T(8,128)(2,1)} %param.8) | copy-start | bytes 110596
  9.7 8.1 %collective-permute-start = (bf16[32,640]{1,0:T(8,128)(2,1)S(1)}, bf16[32,640]{1,0:T(8,128)(2,1)S(1)}, u32[]{:S(2)}, u32[]{:S(2)}) collective-permute-start(bf16[32,640]{1,0:T(8,128)(2,1)S(1)} %shard_map.112.flat_ref), channel_id=1, source_target_pairs={{0,4},{1,5},{2,6},{3,7},{4,0},{5,1},{6,2},{7,3},{8,12},{9,13},{10,... | collective-permute-start | bytes 122888 | tf_op jit(solution)/shard_map/ppermute | solution.py:285
  18.6 3.7 %collective-permute-start.1 = (bf16[16,1024]{1,0:T(8,128)(2,1)S(1)}, bf16[16,1024]{1,0:T(8,128)(2,1)S(1)}, u32[]{:S(2)}, u32[]{:S(2)}) collective-permute-start(bf16[16,1024]{1,0:T(8,128)(2,1)S(1)} %get-tuple-element.33), channel_id=1, source_target_pairs={{0,24},{1,25},{2,26},{3,27},{4,28},{5,29},{6,30},{7,31},{8,16},{9,... | collective-permute-start | bytes 98312 | tf_op jit(solution)/shard_map/ppermute | solution.py:285
  18.7 4.0 %collective-permute-start.3 = (bf16[16,1024]{1,0:T(8,128)(2,1)S(1)}, bf16[16,1024]{1,0:T(8,128)(2,1)S(1)}, u32[]{:S(2)}, u32[]{:S(2)}) collective-permute-start(bf16[16,1024]{1,0:T(8,128)(2,1)S(1)} %get-tuple-element.34), channel_id=1, source_target_pairs={{0,16},{1,17},{2,18},{3,19},{4,20},{5,21},{6,22},{7,23},{8,24},{9,... | collective-permute-start | bytes 98312 | tf_op jit(solution)/shard_map/ppermute | solution.py:285
  20.2 2.4 %collective-permute-start.2 = (bf16[16,1024]{1,0:T(8,128)(2,1)S(1)}, bf16[16,1024]{1,0:T(8,128)(2,1)S(1)}, u32[]{:S(2)}, u32[]{:S(2)}) collective-permute-start(bf16[16,1024]{1,0:T(8,128)(2,1)S(1)} %get-tuple-element.34), channel_id=1, source_target_pairs={{0,8},{1,9},{2,10},{3,11},{4,12},{5,13},{6,14},{7,15},{8,0},{9,1},... | collective-permute-start | bytes 98312 | tf_op jit(solution)/shard_map/ppermute | solution.py:285
  22.7 3.3 %copy-start.4 = (bf16[64,32]{0,1:T(8,128)(2,1)S(1)}, bf16[64,32]{0,1:T(8,128)(2,1)}, u32[]{:S(2)}) copy-start(bf16[64,32]{0,1:T(8,128)(2,1)} %param.11) | copy-start | bytes 12292
  22.7 4.9 %collective-permute-start.6 = (bf16[16,1024]{1,0:T(8,128)(2,1)S(1)}, bf16[16,1024]{1,0:T(8,128)(2,1)S(1)}, u32[]{:S(2)}, u32[]{:S(2)}) collective-permute-start(bf16[16,1024]{1,0:T(8,128)(2,1)S(1)} %add_convert_fusion), channel_id=1, source_target_pairs={{0,3},{1,2},{2,1},{3,0},{4,7},{5,6},{6,5},{7,4},{8,11},{9,10},{10,... | collective-permute-start | bytes 98312 | tf_op jit(solution)/shard_map/ppermute | solution.py:285
  23.4 4.2 %collective-permute-start.5 = (bf16[16,1024]{1,0:T(8,128)(2,1)S(1)}, bf16[16,1024]{1,0:T(8,128)(2,1)S(1)}, u32[]{:S(2)}, u32[]{:S(2)}) collective-permute-start(bf16[16,1024]{1,0:T(8,128)(2,1)S(1)} %add_convert_fusion), channel_id=1, source_target_pairs={{0,9},{1,8},{2,11},{3,10},{4,13},{5,12},{6,15},{7,14},{8,1},{9,0},... | collective-permute-start | bytes 98312 | tf_op jit(solution)/shard_map/ppermute | solution.py:285
  24.1 3.5 %collective-permute-start.4 = (bf16[16,1024]{1,0:T(8,128)(2,1)S(1)}, bf16[16,1024]{1,0:T(8,128)(2,1)S(1)}, u32[]{:S(2)}, u32[]{:S(2)}) collective-permute-start(bf16[16,1024]{1,0:T(8,128)(2,1)S(1)} %add_convert_fusion), channel_id=1, source_target_pairs={{0,10},{1,11},{2,8},{3,9},{4,14},{5,15},{6,12},{7,13},{8,2},{9,3},... | collective-permute-start | bytes 98312 | tf_op jit(solution)/shard_map/ppermute | solution.py:285
  27.7 1.3 %collective-permute-start.7 = (f32[16,1024]{1,0:T(8,128)S(1)}, f32[16,1024]{1,0:T(8,128)S(1)}, u32[]{:S(2)}, u32[]{:S(2)}) collective-permute-start(f32[16,1024]{1,0:T(8,128)S(1)} %add_add_fusion.mine_ref), channel_id=1, source_target_pairs={{0,8},{1,9},{2,10},{3,11},{4,12},{5,13},{6,14},{7,15},{8,0},{9,1},... | collective-permute-start | bytes 196616 | tf_op jit(solution)/shard_map/ppermute | solution.py:285

commit v8 on v7

--- a/solution.py
+++ b/solution.py
@@ -247,7 +247,7 @@
 
 def finish_kernel(z, mine_ref, other_ref, first_ref, bias_ref, second_ref, skip_ref):
     top = holds_top(z)
-    mine, other = mine_ref[...], other_ref[...]
+    mine, other = mine_ref[...].astype(F32), other_ref[...].astype(F32)
     total = jnp.concatenate(
         [jnp.where(top, mine, other), jnp.where(top, other, mine)], axis=0
     )
@@ -385,6 +385,7 @@
 
     mine = total_over_devices(keep, give, images, tiles)
     mine, blended = lax.optimization_barrier((mine, blended))
+    mine = mine.astype(BF16)
     other = swap(mine, images, tiles, (1, 0))
     first, bias, second, skip = call(
         functools.partial(finish_kernel, z),

time: 30.2 us -> 30.1 us (level)
  no operation moved by 1% of the time
where the time goes in v8:
time: 30.1 us; the launch traced here: 29.8 us
  starting transfers between devices  15.8 us (52%)
  waiting for transfers between devices  6.1 us (20%)
  Pallas kernels  5.71 us (19%)
  between operations  1.39 us (5%)
  local copies, waits for them, and re-layouts  0.68 us (2%)
    ppermute x8, starting transfers between devices, swap(): return lax.ppermute(values, ('img', 'tile'), pairs)  8.5 us
    all_to_all x1, starting transfers between devices, local(): lax.all_to_all(packed, 'tile', split_axis=0, concat_axis=0, tiled=True)  7.25 us
    ppermute x8, waiting for transfers between devices, swap(): return lax.ppermute(values, ('img', 'tile'), pairs)  3.54 us
    all_to_all x1, waiting for transfers between devices, local(): lax.all_to_all(packed, 'tile', split_axis=0, concat_axis=0, tiled=True)  2.56 us
    pallas_call x1, Pallas kernels, local(): call(functools.partial(forward_kernel, z), (f32(z.cout, used), bf(z.cin,...  1.39 us
    pallas_call x1, Pallas kernels, local(): call(functools.partial(blend_kernel, z), bf(z.cout, z.height, z.width), [...  1.24 us
    pallas_call x1, Pallas kernels, local(): call(functools.partial(pack_kernel, z), bf(tiles, 2 * ROWS, 2 * z.cin), [...  0.85 us
    pallas_call x1, Pallas kernels, local(): call(functools.partial(finish_kernel, z), (f32(3, 3, z.cout, z.cin), f32(...  0.8 us
  transfers between devices with their start and end apart: 9, of which 5 were waited for; matrix products, arithmetic and copies ran while one was open for 0% of the time, Pallas kernels for 11%

profile of v8, /device:TPU:0, one launch (start us, length us, event | category | flops | bytes accessed | tf_op | source)
XLA Modules:
  0.0 29.8 jit_solution(16097890923850823452)
XLA Ops:
  0.6 0.0 copy-start.3
  0.7 0.7 %copy-done.3 = bf16[1,64,1,128]{3,1,2,0:T(8,128)(2,1)S(1)} copy-done((bf16[1,64,1,128]{3,1,2,0:T(8,128)(2,1)S(1)}, bf16[1,64,1,128]{3,1,2,0:T(8,128)(2,1)}, u32[]{:S(2)}) %copy-start.3) | copy-done | bytes 16408
  1.3 0.0 copy-start.1
  1.4 0.8 %shard_map.111 = bf16[8,32,128]{2,1,0:T(8,128)(2,1)} custom-call(bf16[64,128]{1,0:T(8,128)(2,1)S(1)} %bitcast.16, bf16[2,128,128]{2,1,0:T(8,128)(2,1)S(1)} %shard_map.110.pick_ref), custom_call_target="tpu_custom_call" | custom-call | flops 1000000 | bytes 200000 | tf_op jit(solution)/shard_map/pallas_call | solution.py:331
  2.2 7.3 %all-to-all-start = ((bf16[8,32,128]{2,1,0:T(8,128)(2,1)}), bf16[8,32,128]{2,1,0:T(8,128)(2,1)S(1)}, u32[]{:S(2)}, u32[]{:S(2)}) async-start(bf16[8,32,128]{2,1,0:T(8,128)(2,1)} %shard_map.111), calls=%async_computation | async-start | bytes 131072 | tf_op jit(solution)/shard_map/all_to_all | solution.py:334
  9.5 0.0 copy-done.1
  9.5 0.0 copy-start.5
  9.5 0.0 copy-start
  9.5 0.2 shard_map.112.flat_ref
  9.7 0.0 copy-start.2
  9.7 3.0 %collective-permute-start = (bf16[32,640]{1,0:T(8,128)(2,1)S(1)}, bf16[32,640]{1,0:T(8,128)(2,1)S(1)}, u32[]{:S(2)}, u32[]{:S(2)}) collective-permute-start(bf16[32,640]{1,0:T(8,128)(2,1)S(1)} %shard_map.112.flat_ref), channel_id=1, source_target_pairs={{0,4},{1,5},{2,6},{3,7},{4,0},{5,1},{6,2},{7,3},{8,12},{9,13},{10,... | collective-permute-start | bytes 122888 | tf_op jit(solution)/shard_map/ppermute | solution.py:285
  13.3 0.0 copy-done.5
  13.3 0.1 maximum_bitcast_fusion.row_ref
  13.4 0.0 copy-done
  13.4 0.4 %shard_map.113 = (f32[32,640]{1,0:T(8,128)S(1)}, bf16[288,640]{1,0:T(8,128)(2,1)S(1)}, bf16[32,640]{1,0:T(8,128)(2,1)S(1)}, bf16[256,768]{1,0:T(8,128)(2,1)S(1)}, f32[32,1]{1,0:T(8,128)S(1)}) custom-call(bf16[32,640]{1,0:T(8,128)(2,1)S(1)} %shard_map.112.flat_ref, bf16[3,3,32,32]{3,2,1,0:T(8,128)(2,1)S(1)} %copy-done, f32[1,33]{1,0:T(1,128)S(1)} %maximum_bitcast_fusion.row_ref), custom_call_target="tpu_custom_call" | custom-call | flops 1000000 | bytes 200000 | tf_op jit(solution)/shard_map/pallas_call | solution.py:344
  13.8 2.6 %all-to-all-done.got_ref = bf16[8,32,128]{2,1,0:T(8,128)(2,1)S(1)} async-done(((bf16[8,32,128]{2,1,0:T(8,128)(2,1)}), bf16[8,32,128]{2,1,0:T(8,128)(2,1)S(1)}, u32[]{:S(2)}, u32[]{:S(2)}) %all-to-all-start) | async-done | bytes 65568 | tf_op jit(solution)/shard_map/all_to_all | solution.py:334
  16.4 0.0 copy-done.2
  16.4 1.4 %shard_map.114 = (f32[32,960]{1,0:T(8,128)S(1)}, bf16[64,640]{1,0:T(8,128)(2,1)S(1)}, bf16[32,640]{1,0:T(8,128)(2,1)S(1)}, bf16[576,640]{1,0:T(8,128)(2,1)S(1)},...) custom-call(bf16[8,32,128]{2,1,0:T(8,128)(2,1)S(1)} %all-to-all-done.got_ref, ...), custom_call_target="tpu_custom_call" | custom-call | flops 1000000 | bytes 200000 | tf_op jit(solution)/shard_map/pallas_call | solution.py:357
  17.8 0.0 collective-permute-done.flat_ref
  17.8 0.8 %shard_map.115 = (bf16[16,1024]{1,0:T(8,128)(2,1)S(1)}, bf16[16,1024]{1,0:T(8,128)(2,1)S(1)}) custom-call(f32[32,960]{1,0:T(8,128)S(1)} %get-tuple-element.29.sums_ref, bf16[576,640]{1,0:T(8,128)(2,1)S(1)} %get-tuple-element.30.taps_ref, bf16[32,640]{1,0:T(8,128)(2,1)S(1)} %get-tuple-element.31.hidden_ref, f32[32,640]{1,0:T(8,128)S(1)} %get-tuple-element.32.slope_ref, ...), custom_call_target="tpu_custom_call" | custom-call | flops 1000000 | bytes 200000 | tf_op jit(solution)/shard_map/pallas_call | solution.py:372
  18.6 0.1 collective-permute-start.1
  18.7 1.6 %collective-permute-start.3 = (bf16[16,1024]{1,0:T(8,128)(2,1)S(1)}, bf16[16,1024]{1,0:T(8,128)(2,1)S(1)}, u32[]{:S(2)}, u32[]{:S(2)}) collective-permute-start(bf16[16,1024]{1,0:T(8,128)(2,1)S(1)} %get-tuple-element.34), channel_id=1, source_target_pairs={{0,16},{1,17},{2,18},{3,19},{4,20},{5,21},{6,22},{7,23},{8,24},{9,... | collective-permute-start | bytes 98312 | tf_op jit(solution)/shard_map/ppermute | solution.py:285
  20.2 0.3 collective-permute-start.2
  20.5 1.8 %collective-permute-done.1 = bf16[16,1024]{1,0:T(8,128)(2,1)S(1)} collective-permute-done((bf16[16,1024]{1,0:T(8,128)(2,1)S(1)}, bf16[16,1024]{1,0:T(8,128)(2,1)S(1)}, u32[]{:S(2)}, u32[]{:S(2)}) %collective-permute-start.1) | collective-permute-done | bytes 32800 | tf_op jit(solution)/shard_map/ppermute | solution.py:285
  22.3 0.4 %collective-permute-done.3 = bf16[16,1024]{1,0:T(8,128)(2,1)S(1)} collective-permute-done((bf16[16,1024]{1,0:T(8,128)(2,1)S(1)}, bf16[16,1024]{1,0:T(8,128)(2,1)S(1)}, u32[]{:S(2)}, u32[]{:S(2)}) %collective-permute-start.3) | collective-permute-done | bytes 32800 | tf_op jit(solution)/shard_map/ppermute | solution.py:285
  22.7 0.0 collective-permute-done.2
  22.7 0.0 copy-start.4
  22.7 0.7 %collective-permute-start.6 = (bf16[16,1024]{1,0:T(8,128)(2,1)S(1)}, bf16[16,1024]{1,0:T(8,128)(2,1)S(1)}, u32[]{:S(2)}, u32[]{:S(2)}) collective-permute-start(bf16[16,1024]{1,0:T(8,128)(2,1)S(1)} %add_convert_fusion), channel_id=1, source_target_pairs={{0,3},{1,2},{2,1},{3,0},{4,7},{5,6},{6,5},{7,4},{8,11},{9,10},{10,... | collective-permute-start | bytes 98312 | tf_op jit(solution)/shard_map/ppermute | solution.py:285
  23.4 0.7 %collective-permute-start.5 = (bf16[16,1024]{1,0:T(8,128)(2,1)S(1)}, bf16[16,1024]{1,0:T(8,128)(2,1)S(1)}, u32[]{:S(2)}, u32[]{:S(2)}) collective-permute-start(bf16[16,1024]{1,0:T(8,128)(2,1)S(1)} %add_convert_fusion), channel_id=1, source_target_pairs={{0,9},{1,8},{2,11},{3,10},{4,13},{5,12},{6,15},{7,14},{8,1},{9,0},... | collective-permute-start | bytes 98312 | tf_op jit(solution)/shard_map/ppermute | solution.py:285
  24.1 1.9 %collective-permute-start.4 = (bf16[16,1024]{1,0:T(8,128)(2,1)S(1)}, bf16[16,1024]{1,0:T(8,128)(2,1)S(1)}, u32[]{:S(2)}, u32[]{:S(2)}) collective-permute-start(bf16[16,1024]{1,0:T(8,128)(2,1)S(1)} %add_convert_fusion), channel_id=1, source_target_pairs={{0,10},{1,11},{2,8},{3,9},{4,14},{5,15},{6,12},{7,13},{8,2},{9,3},... | collective-permute-start | bytes 98312 | tf_op jit(solution)/shard_map/ppermute | solution.py:285
  26.0 0.0 copy-done.4
  26.0 1.2 %shard_map.116 = bf16[32,16,32]{2,1,0:T(8,128)(2,1)} custom-call(bf16[32,640]{1,0:T(8,128)(2,1)S(1)} %get-tuple-element.35.hidden_ref, bf16[64,640]{1,0:T(8,128)(2,1)S(1)} %get-tuple-element.36.up_ref, bf16[3,3,32,32]{3,2,1,0:T(8,128)(2,1)S(1)} %copy-done, bf16[32,64]{1,0:T(8,128)(2,1)S(1)} %bitcast.17, f32[1,33]{1,0:T(1,128)S(1)} %maximum_bitcast_fusion.row_ref), custom_call_target="tpu_custom_call" | custom-call | flops 1000000 | bytes 200000 | tf_op jit(solution)/shard_map/pallas_call | solution.py:379
  27.2 0.4 %collective-permute-done.6 = bf16[16,1024]{1,0:T(8,128)(2,1)S(1)} collective-permute-done((bf16[16,1024]{1,0:T(8,128)(2,1)S(1)}, bf16[16,1024]{1,0:T(8,128)(2,1)S(1)}, u32[]{:S(2)}, u32[]{:S(2)}) %collective-permute-start.6) | collective-permute-done | bytes 32800 | tf_op jit(solution)/shard_map/ppermute | solution.py:285
  27.7 0.0 collective-permute-done.5
  27.7 0.0 collective-permute-done.4
  27.7 0.3 %collective-permute-start.7 = (bf16[16,1024]{1,0:T(8,128)(2,1)S(1)}, bf16[16,1024]{1,0:T(8,128)(2,1)S(1)}, u32[]{:S(2)}, u32[]{:S(2)}) collective-permute-start(bf16[16,1024]{1,0:T(8,128)(2,1)S(1)} %add_add_fusion.mine_ref), channel_id=1, source_target_pairs={{0,8},{1,9},{2,10},{3,11},{4,12},{5,13},{6,14},{7,15},{8,0},{9,1},... | collective-permute-start | bytes 98312 | tf_op jit(solution)/shard_map/ppermute | solution.py:285
  28.0 0.9 %collective-permute-done.7.other_ref = bf16[16,1024]{1,0:T(8,128)(2,1)S(1)} collective-permute-done((bf16[16,1024]{1,0:T(8,128)(2,1)S(1)}, bf16[16,1024]{1,0:T(8,128)(2,1)S(1)}, u32[]{:S(2)}, u32[]{:S(2)}) %collective-permute-start.7) | collective-permute-done | bytes 32800 | tf_op jit(solution)/shard_map/ppermute | solution.py:285
  29.0 0.8 %shard_map.117 = (f32[3,3,32,64]{3,2,1,0:T(8,128)}, f32[1,32]{1,0:T(1,128)}, f32[3,3,32,32]{3,2,1,0:T(8,128)}, f32[32,64]{1,0:T(8,128)}) custom-call(bf16[16,1024]{1,0:T(8,128)(2,1)S(1)} %add_add_fusion.mine_ref, bf16[16,1024]{1,0:T(8,128)(2,1)S(1)} %collective-permute-done.7.other_ref), custom_call_target="tpu_custom_call" | custom-call | flops 1000000 | bytes 200000 | tf_op jit(solution)/shard_map/pallas_call | solution.py:390
  (3 shorter events, 0.1 us)
Async XLA Ops:
  0.6 0.7 %copy-start.3 = (bf16[1,64,1,128]{3,1,2,0:T(8,128)(2,1)S(1)}, bf16[1,64,1,128]{3,1,2,0:T(8,128)(2,1)}, u32[]{:S(2)}) copy-start(bf16[1,64,1,128]{3,1,2,0:T(8,128)(2,1)} %param.7) | copy-start | bytes 49156
  1.3 8.1 %copy-start.1 = (bf16[1,32,32,16]{2,3,1,0:T(8,128)(2,1)S(1)}, bf16[1,32,32,16]{2,3,1,0:T(8,128)(2,1)}, u32[]{:S(2)}) copy-start(bf16[1,32,32,16]{2,3,1,0:T(8,128)(2,1)} %param.13) | copy-start | bytes 98308
  2.2 14.2 %all-to-all-start = ((bf16[8,32,128]{2,1,0:T(8,128)(2,1)}), bf16[8,32,128]{2,1,0:T(8,128)(2,1)S(1)}, u32[]{:S(2)}, u32[]{:S(2)}) async-start(bf16[8,32,128]{2,1,0:T(8,128)(2,1)} %shard_map.111), calls=%async_computation | async-start | bytes 131072 | tf_op jit(solution)/shard_map/all_to_all | solution.py:334
  9.5 3.8 %copy-start.5 = (f32[32]{0:T(128)S(1)}, f32[32]{0:T(128)}, u32[]{:S(2)}) copy-start(f32[32]{0:T(128)} %param.9) | copy-start | bytes 388
  9.5 3.9 %copy-start = (bf16[3,3,32,32]{3,2,1,0:T(8,128)(2,1)S(1)}, bf16[3,3,32,32]{3,2,1,0:T(8,128)(2,1)}, u32[]{:S(2)}) copy-start(bf16[3,3,32,32]{3,2,1,0:T(8,128)(2,1)} %ws_ref.5) | copy-start | bytes 55300
  9.7 6.7 %copy-start.2 = (bf16[3,3,64,32]{2,3,1,0:T(8,128)(2,1)S(1)}, bf16[3,3,64,32]{2,3,1,0:T(8,128)(2,1)}, u32[]{:S(2)}) copy-start(bf16[3,3,64,32]{2,3,1,0:T(8,128)(2,1)} %param.8) | copy-start | bytes 110596
  9.7 8.1 %collective-permute-start = (bf16[32,640]{1,0:T(8,128)(2,1)S(1)}, bf16[32,640]{1,0:T(8,128)(2,1)S(1)}, u32[]{:S(2)}, u32[]{:S(2)}) collective-permute-start(bf16[32,640]{1,0:T(8,128)(2,1)S(1)} %shard_map.112.flat_ref), channel_id=1, source_target_pairs={{0,4},{1,5},{2,6},{3,7},{4,0},{5,1},{6,2},{7,3},{8,12},{9,13},{10,... | collective-permute-start | bytes 122888 | tf_op jit(solution)/shard_map/ppermute | solution.py:285
  18.6 3.7 %collective-permute-start.1 = (bf16[16,1024]{1,0:T(8,128)(2,1)S(1)}, bf16[16,1024]{1,0:T(8,128)(2,1)S(1)}, u32[]{:S(2)}, u32[]{:S(2)}) collective-permute-start(bf16[16,1024]{1,0:T(8,128)(2,1)S(1)} %get-tuple-element.33), channel_id=1, source_target_pairs={{0,24},{1,25},{2,26},{3,27},{4,28},{5,29},{6,30},{7,31},{8,16},{9,... | collective-permute-start | bytes 98312 | tf_op jit(solution)/shard_map/ppermute | solution.py:285
  18.7 4.0 %collective-permute-start.3 = (bf16[16,1024]{1,0:T(8,128)(2,1)S(1)}, bf16[16,1024]{1,0:T(8,128)(2,1)S(1)}, u32[]{:S(2)}, u32[]{:S(2)}) collective-permute-start(bf16[16,1024]{1,0:T(8,128)(2,1)S(1)} %get-tuple-element.34), channel_id=1, source_target_pairs={{0,16},{1,17},{2,18},{3,19},{4,20},{5,21},{6,22},{7,23},{8,24},{9,... | collective-permute-start | bytes 98312 | tf_op jit(solution)/shard_map/ppermute | solution.py:285
  20.2 2.4 %collective-permute-start.2 = (bf16[16,1024]{1,0:T(8,128)(2,1)S(1)}, bf16[16,1024]{1,0:T(8,128)(2,1)S(1)}, u32[]{:S(2)}, u32[]{:S(2)}) collective-permute-start(bf16[16,1024]{1,0:T(8,128)(2,1)S(1)} %get-tuple-element.34), channel_id=1, source_target_pairs={{0,8},{1,9},{2,10},{3,11},{4,12},{5,13},{6,14},{7,15},{8,0},{9,1},... | collective-permute-start | bytes 98312 | tf_op jit(solution)/shard_map/ppermute | solution.py:285
  22.7 3.3 %copy-start.4 = (bf16[64,32]{0,1:T(8,128)(2,1)S(1)}, bf16[64,32]{0,1:T(8,128)(2,1)}, u32[]{:S(2)}) copy-start(bf16[64,32]{0,1:T(8,128)(2,1)} %param.11) | copy-start | bytes 12292
  22.7 4.9 %collective-permute-start.6 = (bf16[16,1024]{1,0:T(8,128)(2,1)S(1)}, bf16[16,1024]{1,0:T(8,128)(2,1)S(1)}, u32[]{:S(2)}, u32[]{:S(2)}) collective-permute-start(bf16[16,1024]{1,0:T(8,128)(2,1)S(1)} %add_convert_fusion), channel_id=1, source_target_pairs={{0,3},{1,2},{2,1},{3,0},{4,7},{5,6},{6,5},{7,4},{8,11},{9,10},{10,... | collective-permute-start | bytes 98312 | tf_op jit(solution)/shard_map/ppermute | solution.py:285
  23.4 4.2 %collective-permute-start.5 = (bf16[16,1024]{1,0:T(8,128)(2,1)S(1)}, bf16[16,1024]{1,0:T(8,128)(2,1)S(1)}, u32[]{:S(2)}, u32[]{:S(2)}) collective-permute-start(bf16[16,1024]{1,0:T(8,128)(2,1)S(1)} %add_convert_fusion), channel_id=1, source_target_pairs={{0,9},{1,8},{2,11},{3,10},{4,13},{5,12},{6,15},{7,14},{8,1},{9,0},... | collective-permute-start | bytes 98312 | tf_op jit(solution)/shard_map/ppermute | solution.py:285
  24.1 3.5 %collective-permute-start.4 = (bf16[16,1024]{1,0:T(8,128)(2,1)S(1)}, bf16[16,1024]{1,0:T(8,128)(2,1)S(1)}, u32[]{:S(2)}, u32[]{:S(2)}) collective-permute-start(bf16[16,1024]{1,0:T(8,128)(2,1)S(1)} %add_convert_fusion), channel_id=1, source_target_pairs={{0,10},{1,11},{2,8},{3,9},{4,14},{5,15},{6,12},{7,13},{8,2},{9,3},... | collective-permute-start | bytes 98312 | tf_op jit(solution)/shard_map/ppermute | solution.py:285
  27.7 1.3 %collective-permute-start.7 = (bf16[16,1024]{1,0:T(8,128)(2,1)S(1)}, bf16[16,1024]{1,0:T(8,128)(2,1)S(1)}, u32[]{:S(2)}, u32[]{:S(2)}) collective-permute-start(bf16[16,1024]{1,0:T(8,128)(2,1)S(1)} %add_add_fusion.mine_ref), channel_id=1, source_target_pairs={{0,8},{1,9},{2,10},{3,11},{4,12},{5,13},{6,14},{7,15},{8,0},{9,1},... | collective-permute-start | bytes 98312 | tf_op jit(solution)/shard_map/ppermute | solution.py:285
